TPU v7x, 32 devices: a whole 2x2x4 slice. The times are simulated.
32 devices in a mesh: chan: 4 (over z), blk: 8 (over y, x, core).
Axes of the slice: x: 2, y: 2, z: 4, core: 2. Of those that a mesh axis runs over, the one named last changes fastest.
Arguments:
- sky_maps: bfloat16 [256, 128, 2048], P('chan', 'blk'), may hold values from -6 to 6
- filters: bfloat16 [1024, 256, 256], P(('chan', 'blk')), may hold values from -0.375 to 0.375
- band_order_values: int32 [128], replicated, may hold values from 0 to 1023, as said below
- slot_degree_values: int32 [1024], replicated, may hold values from 0 to 1023, as said below
Outputs:
- cleaned_maps: bfloat16 [256, 128, 2048], P('chan', 'blk')
Inputs may be any that keep to these rules, and one draw needn't show every extreme that they name: `band_order_values`: distinct orders; 0 and 1023 both occur. `slot_degree_values`: a permutation of the degrees; slots 2 i and 2 i + 1 hold degrees that sum to 1023.
All inputs are finite; a program needn't handle non-finite values.
Results may differ from a plain program's by a relative error of at most 0.015.
Values may be sent and summed in bfloat16 or wider, within the bound.
No kernel may reach another device: no remote copies, remote signals or barrier semaphores. Data moves between devices by JAX's collectives and lax.ppermute only.
A program may use at most 128 MiB of HBM per device.

v0:
```python
import math

import jax
import jax.numpy as jnp
from jax import lax
from jax.sharding import PartitionSpec as P

BAND = 0.38


def polar_angle_values(cycle_total):
    position = (jnp.arange(cycle_total, dtype=jnp.float32) + 0.5) / cycle_total
    return 0.5 * math.pi + BAND * (2.0 * position - 1.0)


def phase_table(mode_ids, pixel_count):
    pixels = jnp.arange(pixel_count, dtype=jnp.int32)
    rotations = pixels[:, None] * mode_ids[None, :] % pixel_count
    angles = 2.0 * math.pi / pixel_count * rotations.astype(jnp.float32)
    return jnp.stack([jnp.cos(angles), -jnp.sin(angles)], axis=-1)


def associated_legendre_rows(colatitude, mode_ids, levels):
    cosine = jnp.cos(colatitude)[None, :]
    sine_col = jnp.sin(colatitude)[None, :]
    orders = mode_ids.astype(jnp.float32)[:, None]
    log_seed = 0.5 * (
        jnp.log(orders + 0.5)
        + lax.lgamma(orders + 0.5)
        - lax.lgamma(orders + 1.0)
        - 0.5 * math.log(math.pi)
    )
    seeded = jnp.exp(log_seed + orders * jnp.log(sine_col))

    def advance(carry, degree):
        latest, earlier = carry
        level = degree.astype(jnp.float32)
        growth = jnp.sqrt(
            jnp.maximum(4.0 * level * level - 1.0, 1.0)
            / jnp.maximum(level * level - orders * orders, 1.0)
        )
        previous = level - 1.0
        shrink = jnp.sqrt(
            jnp.maximum(4.0 * previous * previous - 1.0, 1.0)
            / jnp.maximum(previous * previous - orders * orders, 1.0)
        )
        upward = growth * (cosine * latest - earlier / shrink)
        current = jnp.where(level < orders, 0.0, jnp.where(level == orders, seeded, upward))
        return ((current, latest), current.astype(jnp.bfloat16))

    zeroed = jnp.zeros(seeded.shape, jnp.float32)
    degrees = jnp.arange(levels, dtype=jnp.int32)
    return lax.scan(advance, (zeroed, zeroed), degrees, unroll=8)[1]


def body(sky_maps, filters, band_order_values, slot_degree_values):
    channels_per_unit, cycle_dev, pixel_count = sky_maps.shape
    chan_groups = lax.axis_size("chan")
    blk_groups = lax.axis_size("blk")
    slot_dev = filters.shape[0]
    degree_count = slot_degree_values.shape[0]
    mode_count = band_order_values.shape[0]
    mode_dev = mode_count // blk_groups
    cycle_total = cycle_dev * blk_groups
    colatitude = polar_angle_values(cycle_total)
    cycle_factor = (
        2.0
        * math.sqrt(2.0 * BAND / cycle_total)
        * jnp.sin(colatitude)
        * (1.0 / math.sqrt(pixel_count))
    )
    local_factor = lax.dynamic_slice_in_dim(
        cycle_factor, lax.axis_index("blk") * cycle_dev, cycle_dev
    )
    phases = phase_table(band_order_values, pixel_count).astype(jnp.bfloat16)
    product = jnp.dot(
        sky_maps.reshape(channels_per_unit * cycle_dev, pixel_count),
        phases.reshape(pixel_count, 2 * mode_count),
        preferred_element_type=jnp.float32,
    )
    spectra = (
        product.reshape(channels_per_unit, cycle_dev, mode_count, 2)
        * local_factor[None, :, None, None]
    ).astype(jnp.bfloat16)
    grouped_per_order = lax.all_to_all(spectra, "blk", split_axis=2, concat_axis=1, tiled=True)
    local_modes = lax.dynamic_slice_in_dim(
        band_order_values, lax.axis_index("blk") * mode_dev, mode_dev
    )
    lat_table = associated_legendre_rows(colatitude, local_modes, degree_count)
    coeffs = jnp.einsum(
        "dgu,fugs->dgsf", lat_table, grouped_per_order, preferred_element_type=jnp.float32
    ).astype(jnp.bfloat16)
    slotted = coeffs[slot_degree_values].reshape(degree_count, mode_dev * 2 * channels_per_unit)
    wide_filter = filters.reshape(
        slot_dev, chan_groups, channels_per_unit, chan_groups, channels_per_unit
    )
    received = lax.all_to_all(slotted, ("chan", "blk"), split_axis=0, concat_axis=1, tiled=True)
    inputs = received.reshape(slot_dev, chan_groups, blk_groups, mode_dev, 2, channels_per_unit)
    filtered = jnp.einsum(
        "sabcd,scjmkd->ajsmkb", wide_filter, inputs, preferred_element_type=jnp.float32
    ).astype(jnp.bfloat16)
    outgoing = filtered.reshape(
        chan_groups * blk_groups, slot_dev, mode_dev * 2 * channels_per_unit
    )
    returned = lax.all_to_all(outgoing, ("chan", "blk"), split_axis=0, concat_axis=1, tiled=True)
    back_slots = returned.reshape(degree_count, mode_dev, 2, channels_per_unit)
    inverse = (
        jnp.zeros((degree_count,), jnp.int32)
        .at[slot_degree_values]
        .set(jnp.arange(degree_count, dtype=jnp.int32))
    )
    back_degrees = back_slots[inverse]
    cycle_part = (
        2.0
        / math.sqrt(degree_count)
        * jnp.einsum("utz,utih->ztih", lat_table, back_degrees, preferred_element_type=jnp.float32)
    )
    by_cycle = lax.all_to_all(
        cycle_part.astype(jnp.bfloat16), "blk", split_axis=0, concat_axis=1, tiled=True
    )
    cleaned = jnp.einsum("rmkc,pmk->crp", by_cycle, phases, preferred_element_type=jnp.float32)
    return (cleaned * (1.0 / math.sqrt(mode_count))).astype(jnp.bfloat16)


def solution(mesh):
    in_specs = (P("chan", "blk", None), P(("chan", "blk"), None, None), P(), P())
    out_specs = P("chan", "blk", None)
    return jax.shard_map(body, mesh=mesh, in_specs=in_specs, out_specs=out_specs, check_vma=False)
```

profile of v0, /device:TPU:0, one launch (start us, length us, event | category | flops | bytes accessed | tf_op | source)
XLA Modules:
  0.0 1374.0 jit_solution(1366517708497838825)
XLA Ops:
  0.1 5.1 cosine_convert_fusion
  5.3 1.0 copy.47
  6.7 3.5 convolution_bitcast_fusion
  10.2 4.9 reshape.770
  15.0 6.6 copy.48
  21.9 1.7 copy.49
  23.6 1.5 reshape.819
  25.1 5.4 all-to-all-start
  30.8 945.0 %while.19 = (s32[]{:T(128)}, f32[16,128]{1,0:T(8,128)S(1)}, f32[16,128]{1,0:T(8,128)S(1)}, bf16[128,8,16,128]{3,2,1,0:T(8,128)(2,1)}, s32[128,8]{0,1:T(8,128)S(1...) while((s32[]{:T(128)}, f32[16,128]{1,0:T(8,128)S(1)}, ...), condition=%wide.region_1.2_spmd.clone.clone, body=%wide.region_0.1_spmd.clone.clone.sunk | while | flops 155362 | bytes 328456 | solution.py:53
  37.5 0.6 bitcast_dynamic-update-slice_fusion.2
  44.9 0.6 bitcast_dynamic-update-slice_fusion.2
  52.3 0.6 bitcast_dynamic-update-slice_fusion.2
  59.7 0.6 bitcast_dynamic-update-slice_fusion.2
  74.5 0.6 bitcast_dynamic-update-slice_fusion.2
  81.8 0.6 bitcast_dynamic-update-slice_fusion.2
  89.2 0.6 bitcast_dynamic-update-slice_fusion.2
  96.6 0.6 bitcast_dynamic-update-slice_fusion.2
  104.0 0.6 bitcast_dynamic-update-slice_fusion.2
  111.4 0.6 bitcast_dynamic-update-slice_fusion.2
  118.8 0.6 bitcast_dynamic-update-slice_fusion.2
  126.1 0.6 bitcast_dynamic-update-slice_fusion.2
  133.5 0.6 bitcast_dynamic-update-slice_fusion.2
  140.9 0.6 bitcast_dynamic-update-slice_fusion.2
  148.3 0.6 bitcast_dynamic-update-slice_fusion.2
  163.0 0.6 bitcast_dynamic-update-slice_fusion.2
  170.4 0.6 bitcast_dynamic-update-slice_fusion.2
  177.8 0.6 bitcast_dynamic-update-slice_fusion.2
  185.2 0.6 bitcast_dynamic-update-slice_fusion.2
  192.6 0.6 bitcast_dynamic-update-slice_fusion.2
  200.0 0.6 bitcast_dynamic-update-slice_fusion.2
  214.7 0.6 bitcast_dynamic-update-slice_fusion.2
  222.1 0.6 bitcast_dynamic-update-slice_fusion.2
  229.5 0.6 bitcast_dynamic-update-slice_fusion.2
  236.9 0.6 bitcast_dynamic-update-slice_fusion.2
  244.3 0.6 bitcast_dynamic-update-slice_fusion.2
  251.6 0.6 bitcast_dynamic-update-slice_fusion.2
  259.0 0.6 bitcast_dynamic-update-slice_fusion.2
  266.4 0.6 bitcast_dynamic-update-slice_fusion.2
  975.8 0.7 reshape.820
  976.9 7.3 convert_bitcast_fusion
  984.1 13.0 copy.53
  997.1 13.3 gather_fusion
  1010.4 13.1 copy.54
  1023.4 18.6 %all_to_all.49 = bf16[32,32,2048]{2,1,0:T(8,128)(2,1)} reshape(bf16[1024,16,2,64]{3,2,1,0:T(2,128)(2,1)} %copy.54) | data formatting | bytes 8388608 | tf_op jit(solution)/shard_map/all_to_all | solution.py:97
  1042.0 6.7 all-to-all-start.1
  1048.7 12.9 reshape.776
  1061.6 81.0 %all-to-all-done.1 = bf16[32,32,2048]{2,1,0:T(8,128)(2,1)} async-done(((bf16[32,32,2048]{2,1,0:T(8,128)(2,1)}), bf16[32,32,2048]{2,1,0:T(8,128)(2,1)}, u32[]{:S(2)}, u32[]{:S(2)}) %all-to-all-start.1) | async-done | bytes 4194336 | tf_op jit(solution)/shard_map/all_to_all | solution.py:97
  1142.6 15.8 %reshape.813 = bf16[32,4,8,16,2,64]{5,4,3,0,2,1:T(2,128)(2,1)} reshape(bf16[32,32,2048]{2,0,1:T(8,128)(2,1)} %bitcast.10) | data formatting | bytes 8388608 | tf_op jit(solution)/shard_map/reshape | solution.py:98
  1158.4 14.9 %fusion.27 = bf16[4,8,32,16,2,64]{5,3,0,4,1,2:T(8,128)(2,1)} fusion(bf16[32,4,64,4,64,1,1]{4,3,2,1,0,6,5:T(4,128)(2,1)} %bitcast.191, bf16[32,4,8,16,2,64,1]{5,4,3,0,2,1,6:T(2,128)(2,1)} %bitcast.192), kind=kOutput, calls=%fused_computation.75 | convolution fusion | flops 1075838976 | bytes 12582912 | tf_op jit(solution)/shard_map/sabcd,scjmkd->ajsmkb/dot_general | solution.py:99
  1173.3 13.3 copy.58
  1186.6 18.6 %reshape.777 = bf16[32,32,2048]{2,1,0:T(8,128)(2,1)} reshape(bf16[4,8,32,16,2,64]{5,4,3,2,1,0:T(2,128)(2,1)} %copy.58) | data formatting | bytes 8388608 | tf_op jit(solution)/shard_map/reshape | solution.py:102
  1205.2 4.0 all-to-all-start.2
  1209.2 4.7 scatter_custom_fusion
  1214.0 89.1 %all-to-all-done.2 = bf16[32,32,2048]{2,1,0:T(8,128)(2,1)} async-done(((bf16[32,32,2048]{2,1,0:T(8,128)(2,1)}), bf16[32,32,2048]{2,1,0:T(8,128)(2,1)}, u32[]{:S(2)}, u32[]{:S(2)}) %all-to-all-start.2) | async-done | bytes 4194336 | tf_op jit(solution)/shard_map/all_to_all | solution.py:105
  1303.1 15.9 %reshape.778 = bf16[1024,16,2,64]{3,2,1,0:T(2,128)(2,1)} reshape(bf16[32,32,2048]{2,1,0:T(8,128)(2,1)} %all-to-all-done.2) | data formatting | bytes 8388608 | tf_op jit(solution)/shard_map/reshape | solution.py:106
  1319.0 7.7 copy.59
  1326.7 13.2 gather_fusion.1
  1339.9 12.1 fusion.48
  1352.0 0.9 copy.62
  1353.0 0.7 reshape.821
  1353.7 13.4 all_to_all.61
  1367.1 0.7 reshape.822
  1368.2 1.3 fusion.35
  1369.5 4.3 copy.66
  (1914 shorter events, 260.2 us)
Async XLA Ops:
  15.0 15.5 %copy-start.1 = (s32[128]{0:T(128)S(1)}, s32[128]{0:T(128)}, u32[]{:S(2)}) copy-start(s32[128]{0:T(128)} %param.8) | copy-start | bytes 1540
  15.0 960.7 %copy-start = (s32[1024]{0:T(1024)S(1)}, s32[1024]{0:T(1024)}, u32[]{:S(2)}) copy-start(s32[1024]{0:T(1024)} %param.9) | copy-start | bytes 12292
  25.1 950.6 %all-to-all-start = ((bf16[8,2,16384]{2,1,0:T(2,128)(2,1)}), bf16[8,2,16384]{2,1,0:T(2,128)(2,1)S(1)}, u32[]{:S(2)}, u32[]{:S(2)}) async-start(bf16[8,2,16384]{2,1,0:T(2,128)(2,1)} %reshape.819), calls=%async_computation | async-start | bytes 1048576 | tf_op jit(solution)/shard_map/all_to_all | solution.py:85
  1042.0 100.6 %all-to-all-start.1 = ((bf16[32,32,2048]{2,1,0:T(8,128)(2,1)}), bf16[32,32,2048]{2,1,0:T(8,128)(2,1)}, u32[]{:S(2)}, u32[]{:S(2)}) async-start(bf16[32,32,2048]{2,1,0:T(8,128)(2,1)} %all_to_all.49), calls=%async_computation.1 | async-start | bytes 8388608 | tf_op jit(solution)/shard_map/all_to_all | solution.py:97
  1205.2 97.9 %all-to-all-start.2 = ((bf16[32,32,2048]{2,1,0:T(8,128)(2,1)}), bf16[32,32,2048]{2,1,0:T(8,128)(2,1)}, u32[]{:S(2)}, u32[]{:S(2)}) async-start(bf16[32,32,2048]{2,1,0:T(8,128)(2,1)} %reshape.777), calls=%async_computation.2 | async-start | bytes 8388608 | tf_op jit(solution)/shard_map/all_to_all | solution.py:105
where the time goes:
time: 1400 us; the launch traced here: 1370 us
  loops' own time  669 us (48%)
  local copies, waits for them, and re-layouts  353 us (25%)
  waiting for transfers between devices  170 us (12%)
  other arithmetic  114 us (8%)
  matrix products  39 us (3%)
  starting transfers between devices  16.1 us (1%)
    another operation x1, loops' own time, associated_legendre_rows(): return lax.scan(advance, (zeroed, zeroed), degrees, unroll=8)[1]  669 us
    all_to_all x1, waiting for transfers between devices, body(): lax.all_to_all(outgoing, ('chan', 'blk'), split_axis=0, concat_axis=1, ti...  89.1 us
    all_to_all x1, waiting for transfers between devices, body(): lax.all_to_all(slotted, ('chan', 'blk'), split_axis=0, concat_axis=1, til...  81 us
    dynamic_update_slice x128, local copies, waits for them, and re-layouts, associated_legendre_rows(): return lax.scan(advance, (zeroed, zeroed), degrees, unroll=8)[1]  79.8 us
    while x896, other arithmetic  79.5 us
    slice x128, local copies, waits for them, and re-layouts, associated_legendre_rows(): return lax.scan(advance, (zeroed, zeroed), degrees, unroll=8)[1]  78.8 us
  transfers between devices with their start and end apart: 3, of which 2 were waited for; matrix products, arithmetic and copies ran while one was open for 21% of the time, Pallas kernels for 0%

commit v1 on v0

v1 whole, which is shorter than its diff:
```python
import functools
import math

import jax
import jax.numpy as jnp
from jax import lax
from jax.experimental import pallas as pl
from jax.experimental.pallas import tpu as pltpu
from jax.sharding import PartitionSpec as P

BAND = 0.38
VMEM_LIMIT = 56 * 1024 * 1024
F32 = jnp.float32
BF16 = jnp.bfloat16


def params(**kw):
    return pltpu.CompilerParams(vmem_limit_bytes=VMEM_LIMIT, **kw)


def polar_angle_values(cycle_total):
    position = (jnp.arange(cycle_total, dtype=F32) + 0.5) / cycle_total
    return 0.5 * math.pi + BAND * (2.0 * position - 1.0)


def divisor(n, most):
    return max(d for d in range(1, most + 1) if n % d == 0)


def lane_blocks(width):
    return -(-width // 128)


def put(ref, rows, value):
    width = value.shape[1]
    for h in range(ref.shape[0]):
        piece = value[:, h * 128 : min((h + 1) * 128, width)]
        if piece.shape[1] < 128:
            piece = jnp.concatenate([piece, jnp.zeros((piece.shape[0], 128 - piece.shape[1]), piece.dtype)], axis=1)
        ref[h, rows, :] = piece


def get(ref, rows, width):
    value = jnp.concatenate([ref[h, rows, :] for h in range(ref.shape[0])], axis=1)
    return value if width == value.shape[1] else value[:, :width]


def analysis_kernel(steps, factor_ref, modes_ref, sky_ref, out_ref, phase_ref, prod_ref, turn_ref):
    step = pl.program_id(0)
    chans, cycles, pixels = sky_ref.shape
    modes = modes_ref.shape[1]
    low = 64
    high = pixels // low

    @pl.when(step == 0)
    def _():
        ids = modes_ref[...]
        unit = 2.0 * math.pi / pixels

        def table(rows, stride):
            index = lax.broadcasted_iota(jnp.int32, (rows, modes), 0) * stride
            angle = unit * ((index * ids) & (pixels - 1)).astype(F32)
            return jnp.cos(angle), jnp.sin(angle)

        cos_low, sin_low = table(low, 1)
        cos_high, sin_high = table(high, low)
        for h in range(high):
            ca, sa = cos_high[h : h + 1], sin_high[h : h + 1]
            rows = slice(h * low, (h + 1) * low)
            phase_ref[rows, :modes] = (ca * cos_low - sa * sin_low).astype(BF16)
            phase_ref[rows, modes:] = (-(sa * cos_low + ca * sin_low)).astype(BF16)

    rows = chans * cycles
    product = jnp.dot(sky_ref[...].reshape(rows, pixels), phase_ref[...], preferred_element_type=F32)
    put(prod_ref, pl.ds(pl.multiple_of(step * rows, rows), rows), product)

    @pl.when(step == steps - 1)
    def _():
        total = chans * steps
        for r in range(cycles):
            part = get(prod_ref, pl.ds(r, total, stride=cycles), 2 * modes) * factor_ref[r]
            both = [part[:, k * modes : (k + 1) * modes].T for k in range(2)]
            put(turn_ref, pl.ds(r, modes, stride=cycles), jnp.concatenate(both, axis=1))
        out_ref[...] = get(turn_ref, slice(None), 2 * total).astype(BF16).reshape(out_ref.shape)


def analysis(sky, factor, modes):
    chans, cycles, pixels = sky.shape
    count = modes.shape[0]
    steps = 4
    return pl.pallas_call(
        functools.partial(analysis_kernel, steps),
        grid=(steps,),
        in_specs=[
            pl.BlockSpec(memory_space=pltpu.SMEM),
            pl.BlockSpec((1, count), lambda i: (0, 0)),
            pl.BlockSpec((chans // steps, cycles, pixels), lambda i: (i, 0, 0)),
        ],
        out_specs=pl.BlockSpec((count, cycles, 2 * chans), lambda i: (0, 0, 0)),
        out_shape=jax.ShapeDtypeStruct((count, cycles, 2 * chans), BF16),
        scratch_shapes=[
            pltpu.VMEM((pixels, 2 * count), BF16),
            pltpu.VMEM((lane_blocks(2 * count), chans * cycles, 128), F32),
            pltpu.VMEM((lane_blocks(2 * chans), count * cycles, 128), F32),
        ],
        compiler_params=params(),
        name="analysis",
    )(factor, modes.reshape(1, count), sky)


def legendre_kernel(levels, degree_ref, order_ref, cosine_ref, seed_ref, lat_ref, turned_ref, gain_ref, all_ref, pick_ref):
    modes, cycles = seed_ref.shape
    slots = lat_ref.shape[1]
    block = 128
    level = lax.broadcasted_iota(jnp.int32, (modes, levels), 1).astype(F32)
    squared = order_ref[...] * order_ref[...]

    def growth(n):
        return jnp.sqrt(jnp.maximum(4.0 * n * n - 1.0, 1.0) / jnp.maximum(n * n - squared, 1.0))

    here = growth(level)
    gain_ref[0] = here
    gain_ref[1] = here / growth(level - 1.0)
    cosine = jnp.broadcast_to(cosine_ref[...], (modes, cycles))
    orders = jnp.broadcast_to(order_ref[...], (modes, cycles))
    seed = seed_ref[...]

    def advance(i, carry):
        latest, earlier = carry
        start = pl.multiple_of(i * block, block)
        first = gain_ref[0, :, pl.ds(start, block)]
        second = gain_ref[1, :, pl.ds(start, block)]
        base = (i * block).astype(F32)
        for n in range(block):
            up = jnp.broadcast_to(first[:, n : n + 1], (modes, cycles)) * cosine
            down = jnp.broadcast_to(second[:, n : n + 1], (modes, cycles))
            begin = jnp.where(orders == base + n, seed, 0.0)
            current = up * latest + (begin - down * earlier)
            put(all_ref, pl.ds(pl.multiple_of((start + n) * modes, modes), modes), current)
            latest, earlier = current, latest
        return latest, earlier

    zero = jnp.zeros((modes, cycles), F32)
    lax.fori_loop(0, levels // block, advance, (zero, zero))

    def pick(s, _):
        source = pl.multiple_of(degree_ref[s] * modes, modes)
        for h in range(all_ref.shape[0]):
            pick_ref[h, pl.ds(pl.multiple_of(s * modes, modes), modes), :] = all_ref[h, pl.ds(source, modes), :]
        return 0

    lax.fori_loop(0, slots, pick, 0, unroll=8)
    for j in range(modes):
        rows = get(pick_ref, pl.ds(j, slots, stride=modes), cycles)
        lat_ref[j] = rows.astype(BF16)
        turned_ref[j] = rows.T.astype(BF16)


def legendre(degrees, orders, colatitude, levels):
    slots, modes, cycles = degrees.shape[0], orders.shape[0], colatitude.shape[0]
    m = orders.astype(F32)[:, None]
    log_seed = 0.5 * (
        jnp.log(m + 0.5) + lax.lgamma(m + 0.5) - lax.lgamma(m + 1.0) - 0.5 * math.log(math.pi)
    )
    seed = jnp.exp(log_seed + m * jnp.log(jnp.sin(colatitude))[None, :])
    vmem = pl.BlockSpec(memory_space=pltpu.VMEM)
    return pl.pallas_call(
        functools.partial(legendre_kernel, levels),
        in_specs=[pl.BlockSpec(memory_space=pltpu.SMEM), vmem, vmem, vmem],
        out_specs=[vmem, vmem],
        out_shape=[
            jax.ShapeDtypeStruct((modes, slots, cycles), BF16),
            jax.ShapeDtypeStruct((modes, cycles, slots), BF16),
        ],
        scratch_shapes=[
            pltpu.VMEM((2, modes, levels), F32),
            pltpu.VMEM((lane_blocks(cycles), levels * modes, 128), F32),
            pltpu.VMEM((lane_blocks(cycles), slots * modes, 128), F32),
        ],
        compiler_params=params(),
        cost_estimate=pl.CostEstimate(flops=40_000_000, bytes_accessed=4_000_000, transcendentals=0),
        name="legendre",
    )(degrees, m, jnp.cos(colatitude)[None, :], seed)


def harmonic_kernel(place_ref, lat_ref, *refs):
    parts = len(refs) - 4
    spectra, out_ref, all_ref, wide_ref, turn_ref = refs[:parts], *refs[parts:]
    groups, modes, cycles, pair = spectra[0].shape
    chans = pair // 2
    total = chans * parts
    dests, slot_dev = out_ref.shape[:2]
    slots = dests * slot_dev
    rows = 2 * modes
    step = pl.program_id(0)

    @pl.when(step == 0)
    def _():
        for t in range(parts):
            all_ref[place_ref[t]] = spectra[t][...]
        for j in range(modes):
            pieces = [all_ref[z, :, j].reshape(groups * cycles, pair) for z in range(parts)]
            for k in range(2):
                wide_ref[j, :, k * total : (k + 1) * total] = jnp.concatenate(
                    [p[:, k * chans : (k + 1) * chans] for p in pieces], axis=1
                )

    lanes = turn_ref.shape[2]
    for j in range(modes):
        result = jnp.dot(lat_ref[j], wide_ref[j], preferred_element_type=F32)
        for k in range(2):
            for h in range(total // lanes):
                turn_ref[h, pl.ds(2 * j + k, slots, stride=rows), :] = result[
                    :, k * total + h * lanes : k * total + (h + 1) * lanes
                ]
    for h in range(total // lanes):
        out_ref[:, :, :, h * lanes : (h + 1) * lanes] = (
            turn_ref[h].astype(BF16).reshape(dests, slot_dev, rows, lanes)
        )


def harmonic(place, lat, spectra, slot_dev):
    modes, slots, cycle_total = lat.shape
    groups, _, cycles, pair = spectra[0].shape
    total = pair // 2 * len(spectra)
    dests = slots // slot_dev
    steps = divisor(dests, 2)
    lanes = min(128, total)
    whole = pl.BlockSpec((groups, modes, cycles, pair), lambda i: (0, 0, 0, 0))
    return pl.pallas_call(
        harmonic_kernel,
        grid=(steps,),
        in_specs=[
            pl.BlockSpec(memory_space=pltpu.SMEM),
            pl.BlockSpec((modes, slots // steps, cycle_total), lambda i: (0, i, 0)),
        ]
        + [whole] * len(spectra),
        out_specs=pl.BlockSpec((dests // steps, slot_dev, 2 * modes, total), lambda i: (i, 0, 0, 0)),
        out_shape=jax.ShapeDtypeStruct((dests, slot_dev, 2 * modes, total), BF16),
        scratch_shapes=[
            pltpu.VMEM((len(spectra), groups, modes, cycles, pair), BF16),
            pltpu.VMEM((modes, cycle_total, 2 * total), BF16),
            pltpu.VMEM((total // lanes, slots // steps * 2 * modes, lanes), F32),
        ],
        compiler_params=params(),
        name="harmonic",
    )(place, lat, *spectra)


def filter_kernel(filters_ref, coeffs_ref, out_ref, turn_ref):
    groups, slots, rows, total = coeffs_ref.shape
    lanes = turn_ref.shape[2]
    for s in range(slots):
        result = lax.dot_general(
            coeffs_ref[:, s].reshape(groups * rows, total),
            filters_ref[s],
            (((1,), (1,)), ((), ())),
            preferred_element_type=F32,
        )
        for h in range(total // lanes):
            turn_ref[h, pl.ds(s, groups * rows, stride=slots), :] = result[:, h * lanes : (h + 1) * lanes]
    for h in range(total // lanes):
        out_ref[:, :, :, h * lanes : (h + 1) * lanes] = (
            turn_ref[h].astype(BF16).reshape(groups, rows, slots, lanes)
        )


def apply_filters(filters, coeffs):
    groups, slots, rows, total = coeffs.shape
    step = min(slots, 16)
    lanes = min(128, total)
    return pl.pallas_call(
        filter_kernel,
        grid=(slots // step,),
        in_specs=[
            pl.BlockSpec((step, total, total), lambda i: (i, 0, 0)),
            pl.BlockSpec((groups, step, rows, total), lambda i: (0, i, 0, 0)),
        ],
        out_specs=pl.BlockSpec((groups, rows, step, total), lambda i: (0, 0, i, 0)),
        out_shape=jax.ShapeDtypeStruct((groups, rows, slots, total), BF16),
        scratch_shapes=[pltpu.VMEM((total // lanes, groups * rows * step, lanes), F32)],
        compiler_params=params(),
        name="filters",
    )(filters, coeffs)


def cycles_kernel(scale, place_ref, turned_ref, filtered_ref, out_ref):
    groups, rows, slot_dev, total = filtered_ref.shape
    parts, blocks, modes, cycles, pair = out_ref.shape
    chans = pair // 2
    for j in range(modes):
        result = [
            jnp.dot(
                turned_ref[j],
                filtered_ref[:, 2 * j + k].reshape(groups * slot_dev, total),
                preferred_element_type=F32,
            )
            for k in range(2)
        ]
        for z in range(parts):
            piece = jnp.concatenate([r[:, z * chans : (z + 1) * chans] for r in result], axis=1) * scale
            out_ref[place_ref[z], :, j] = piece.astype(BF16).reshape(blocks, cycles, pair)


def to_cycles(place, turned, filtered, scale, blocks, parts):
    modes, cycle_total, slots = turned.shape
    groups, rows, slot_dev, total = filtered.shape
    vmem = pl.BlockSpec(memory_space=pltpu.VMEM)
    return pl.pallas_call(
        functools.partial(cycles_kernel, scale),
        in_specs=[pl.BlockSpec(memory_space=pltpu.SMEM), vmem, vmem],
        out_specs=vmem,
        out_shape=jax.ShapeDtypeStruct(
            (parts, blocks, modes, cycle_total // blocks, 2 * total // parts), BF16
        ),
        compiler_params=params(),
        name="cycles",
    )(place, turned, filtered)


def synthesis_kernel(modes_ref, parts_ref, out_ref, phase_ref, wide_ref, turn_ref, left_ref):
    step = pl.program_id(0)
    chans, cycles, pixels = out_ref.shape
    modes, _, pair = parts_ref.shape
    low = 128
    total = pair // 2

    @pl.when(step == 0)
    def _():
        ids = modes_ref[...]
        unit = 2.0 * math.pi / pixels

        def table(columns, stride):
            index = lax.broadcasted_iota(jnp.int32, (modes, columns), 1) * stride
            angle = unit * ((index * ids) & (pixels - 1)).astype(F32)
            return jnp.cos(angle), jnp.sin(angle)

        cos_low, sin_low = table(low, 1)
        cos_high, sin_high = table(pixels // low, low)
        for h in range(pixels // low):
            ca, sa = cos_high[:, h : h + 1], sin_high[:, h : h + 1]
            columns = slice(h * low, (h + 1) * low)
            phase_ref[:modes, columns] = (ca * cos_low - sa * sin_low).astype(BF16)
            phase_ref[modes:, columns] = (-(sa * cos_low + ca * sin_low)).astype(BF16)
        put(wide_ref, slice(None), parts_ref[...].astype(F32).reshape(modes * cycles, pair))
        for r in range(cycles):
            part = get(wide_ref, pl.ds(r, modes, stride=cycles), pair)
            both = [part[:, k * total : (k + 1) * total].T for k in range(2)]
            put(turn_ref, pl.ds(r, total, stride=cycles), jnp.concatenate(both, axis=1))
        left_ref[...] = get(turn_ref, slice(None), 2 * modes).astype(BF16)

    rows = chans * cycles
    result = jnp.dot(
        left_ref[pl.ds(pl.multiple_of(step * rows, rows), rows), :], phase_ref[...], preferred_element_type=F32
    )
    out_ref[...] = (result * (1.0 / math.sqrt(modes))).astype(BF16).reshape(chans, cycles, pixels)


def synthesis(parts, modes, pixels):
    count, cycles, pair = parts.shape
    chans = pair // 2
    steps = 4
    return pl.pallas_call(
        synthesis_kernel,
        grid=(steps,),
        in_specs=[
            pl.BlockSpec((count, 1), lambda i: (0, 0)),
            pl.BlockSpec((count, cycles, pair), lambda i: (0, 0, 0)),
        ],
        out_specs=pl.BlockSpec((chans // steps, cycles, pixels), lambda i: (i, 0, 0)),
        out_shape=jax.ShapeDtypeStruct((chans, cycles, pixels), BF16),
        scratch_shapes=[
            pltpu.VMEM((2 * count, pixels), BF16),
            pltpu.VMEM((lane_blocks(pair), count * cycles, 128), F32),
            pltpu.VMEM((lane_blocks(2 * count), chans * cycles, 128), F32),
            pltpu.VMEM((chans * cycles, 2 * count), BF16),
        ],
        compiler_params=params(),
        name="synthesis",
    )(modes.reshape(count, 1), parts)


def body(sky_maps, filters, band_order_values, slot_degree_values):
    chans, cycle_dev, pixels = sky_maps.shape
    chan_groups = lax.axis_size("chan")
    blk_groups = lax.axis_size("blk")
    chan, blk = lax.axis_index("chan"), lax.axis_index("blk")
    slot_dev = filters.shape[0]
    degree_count = slot_degree_values.shape[0]
    mode_dev = band_order_values.shape[0] // blk_groups
    cycle_total = cycle_dev * blk_groups
    group_slots = slot_dev * blk_groups
    colatitude = polar_angle_values(cycle_total)
    cycle_factor = (
        2.0 * math.sqrt(2.0 * BAND / cycle_total) * jnp.sin(colatitude) * (1.0 / math.sqrt(pixels))
    )
    local_factor = lax.dynamic_slice_in_dim(cycle_factor, blk * cycle_dev, cycle_dev)
    local_modes = lax.dynamic_slice_in_dim(band_order_values, blk * mode_dev, mode_dev)
    degrees = lax.dynamic_slice_in_dim(slot_degree_values, chan * group_slots, group_slots)

    spectra = analysis(sky_maps, local_factor, band_order_values)
    spectra = spectra.reshape(blk_groups, mode_dev, cycle_dev, 2 * chans)
    spectra = lax.all_to_all(spectra, "blk", split_axis=0, concat_axis=0, tiled=True)
    shift = [[(i, (i + t) % chan_groups) for i in range(chan_groups)] for t in range(chan_groups)]
    gathered = [spectra] + [lax.ppermute(spectra, "chan", shift[t]) for t in range(1, chan_groups)]
    lat, turned = legendre(degrees, local_modes, colatitude, degree_count)
    hops = jnp.arange(chan_groups, dtype=jnp.int32)
    coeffs = harmonic((chan - hops) % chan_groups, lat, gathered, slot_dev)
    coeffs = lax.all_to_all(coeffs, "blk", split_axis=0, concat_axis=0, tiled=True)
    filtered = apply_filters(filters, coeffs)
    filtered = lax.all_to_all(filtered, "blk", split_axis=0, concat_axis=0, tiled=True)
    scale = 2.0 / math.sqrt(degree_count)
    partial = to_cycles((hops - chan) % chan_groups, turned, filtered, scale, blk_groups, chan_groups)
    arrived = [partial[0]] + [lax.ppermute(partial[t], "chan", shift[t]) for t in range(1, chan_groups)]
    cycle_part = functools.reduce(jnp.add, [a.astype(F32) for a in arrived]).astype(BF16)
    by_cycle = lax.all_to_all(cycle_part, "blk", split_axis=0, concat_axis=0, tiled=True)
    by_cycle = by_cycle.reshape(blk_groups * mode_dev, cycle_dev, 2 * chans)
    return synthesis(by_cycle, band_order_values, pixels)


def solution(mesh):
    in_specs = (P("chan", "blk", None), P(("chan", "blk"), None, None), P(), P())
    out_specs = P("chan", "blk", None)
    return jax.shard_map(body, mesh=mesh, in_specs=in_specs, out_specs=out_specs, check_vma=False)
```

time: 1400 us -> 270 us (0.19)
  the two profiles are of different devices: /device:TPU:0 before, /device:TPU:8 now
where the time goes in v1:
time: 270 us; the launch traced here: 269 us
  waiting for transfers between devices  135 us (50%)
  blocking collectives  53.6 us (20%)
  Pallas kernels  46.9 us (17%)
  starting transfers between devices  21.9 us (8%)
  local copies, waits for them, and re-layouts  6.56 us (2%)
  other arithmetic  4.8 us (2%)
    all_to_all x1, blocking collectives, body(): lax.all_to_all(coeffs, 'blk', split_axis=0, concat_axis=0, tiled=True)  53.6 us
    all_to_all x1, waiting for transfers between devices, body(): lax.all_to_all(filtered, 'blk', split_axis=0, concat_axis=0, tiled=True)  48.6 us
    ppermute x3, waiting for transfers between devices, body(): lax.ppermute(partial[t], 'chan', shift[t])  40.7 us
    ppermute x3, waiting for transfers between devices, body(): lax.ppermute(spectra, 'chan', shift[t])  29.5 us
    pallas_call x1, Pallas kernels, harmonic(): pl.pallas_call(harmonic_kernel, grid=(steps,), in_specs=[pl.BlockSpec(mem...  11.2 us
    pallas_call x1, Pallas kernels, legendre(): pl.pallas_call(functools.partial(legendre_kernel, levels), in_specs=[pl.B...  9.79 us
    all_to_all x1, waiting for transfers between devices, body(): lax.all_to_all(cycle_part, 'blk', split_axis=0, concat_axis=0, tiled=True)  9.01 us
    all_to_all x1, waiting for transfers between devices, body(): lax.all_to_all(spectra, 'blk', split_axis=0, concat_axis=0, tiled=True)  7.58 us
  transfers between devices with their start and end apart: 9, of which 9 were waited for; matrix products, arithmetic and copies ran while one was open for 2% of the time, Pallas kernels for 4%

profile of v1, /device:TPU:8, one launch (start us, length us, event | category | flops | bytes accessed | tf_op | source)
XLA Modules:
  0.0 269.2 jit_solution(13406090804260005959)
XLA Ops:
  0.0 0.0 copy-start.5
  0.0 0.1 broadcast_multiply_fusion
  0.1 0.6 dynamic_slice.11.factor_ref
  0.6 6.6 %analysis.1 = bf16[128,16,128]{2,1,0:T(8,128)(2,1)} custom-call(f32[16]{0:T(128)} %dynamic_slice.11.factor_ref, s32[1,128]{1,0:T(1,128)} %bitcast.18, bf16[64,16,2048]{2,1,0:T(8,128)(2,1)} %sky_ref.1), custom_call_target="tpu_custom_call" | custom-call | tf_op jit(solution)/shard_map/analysis/pallas_call | solution.py:91
  7.2 3.7 %all-to-all-start = ((bf16[8,16,16,128]{3,2,1,0:T(8,128)(2,1)}), bf16[8,16,16,128]{3,2,1,0:T(8,128)(2,1)S(1)}, u32[]{:S(2)}, u32[]{:S(2)}) async-start(bf16[8,16,16,128]{3,2,1,0:T(8,128)(2,1)} %bitcast.16), calls=%async_computation | async-start | bytes 1048576 | tf_op jit(solution)/shard_map/all_to_all | solution.py:403
  10.9 0.0 copy-done.5
  11.0 0.2 add_multiply_fusion
  11.1 0.7 copy.5.order_ref
  11.8 1.3 dynamic_slice.9.degree_ref
  13.1 7.6 %all-to-all-done.refs_0_ = bf16[8,16,16,128]{3,2,1,0:T(8,128)(2,1)S(1)} async-done(((bf16[8,16,16,128]{3,2,1,0:T(8,128)(2,1)}), bf16[8,16,16,128]{3,2,1,0:T(8,128)(2,1)S(1)}, u32[]{:S(2)}, u32[]{:S(2)}) %all-to-all-start) | async-done | bytes 524320 | tf_op jit(solution)/shard_map/all_to_all | solution.py:403
  20.7 0.0 copy-start.1
  20.7 1.6 collective-permute-start
  22.3 1.2 collective-permute-start.1
  23.5 1.8 collective-permute-start.2
  25.3 0.1 fusion.11
  25.4 0.6 add_cosine_fusion.cosine_ref
  26.0 0.7 add_exponential_fusion.seed_ref
  26.7 9.8 %legendre.1 = (bf16[16,256,128]{2,1,0:T(8,128)(2,1)}, bf16[16,128,256]{2,1,0:T(8,128)(2,1)}) custom-call(s32[256]{0:T(256)} %dynamic_slice.9.degree_ref, f32[16,1]{1,0:T(8,128)} %copy.5.order_ref, f32[1,128]{1,0:T(1,128)} %add_cosine_fusion.cosine_ref, f32[16,128]{1,0:T(8,128)} %add_exponential_fusion.seed_ref), custom_call_target="tpu_custom_call" | custom-call | flops 40000000 | bytes 4000000 | tf_op jit(solution)/shard_map/legendre/pallas_call | solution.py:167
  36.5 0.6 and_select_fusion.place_ref
  37.1 20.1 %collective-permute-done.refs_1_ = bf16[8,16,16,128]{3,2,1,0:T(8,128)(2,1)S(1)} collective-permute-done((bf16[8,16,16,128]{3,2,1,0:T(8,128)(2,1)S(1)}, bf16[8,16,16,128]{3,2,1,0:T(8,128)(2,1)S(1)}, u32[]{:S(2)}, u32[]{:S(2)}) %collective-permute-start) | collective-permute-done | bytes 524320 | tf_op jit(solution)/shard_map/ppermute | solution.py:405
  57.1 0.0 copy-start.2
  57.1 7.7 %collective-permute-done.1.refs_2_ = bf16[8,16,16,128]{3,2,1,0:T(8,128)(2,1)S(1)} collective-permute-done((bf16[8,16,16,128]{3,2,1,0:T(8,128)(2,1)S(1)}, bf16[8,16,16,128]{3,2,1,0:T(8,128)(2,1)S(1)}, u32[]{:S(2)}, u32[]{:S(2)}) %collective-permute-start.1) | collective-permute-done | bytes 524320 | tf_op jit(solution)/shard_map/ppermute | solution.py:405
  64.8 0.0 copy-start.3
  64.8 1.8 collective-permute-done.2.refs_3_
  66.6 0.0 copy-start.4
  66.6 0.0 copy-done.1
  66.6 0.0 copy-done.2
  66.6 0.0 copy-done.3
  66.6 0.8 copy-done.4
  67.4 11.2 %harmonic.1 = bf16[8,32,32,256]{3,2,1,0:T(8,128)(2,1)} custom-call(s32[4]{0:T(128)} %and_select_fusion.place_ref, bf16[16,256,128]{2,1,0:T(8,128)(2,1)} %get-tuple-element.8.lat_ref, bf16[8,16,16,128]{3,2,1,0:T(8,128)(2,1)} %copy-done.1, bf16[8,16,16,128]{3,2,1,0:T(8,128)(2,1)} %copy-done.2, bf16[8,16,16,128]{3,2,1,0:T(8,128)(2,1)} %copy-done.3, ...), custom_call_target="tpu_custom_call" | custom-call | tf_op jit(solution)/shard_map/harmonic/pallas_call | solution.py:230
  78.6 53.6 %all_to_all.20.coeffs_ref = bf16[8,32,32,256]{3,2,1,0:T(8,128)(2,1)} all-to-all(bf16[8,32,32,256]{3,2,1,0:T(8,128)(2,1)} %harmonic.1), channel_id=1, replica_groups=mesh['chan'=4,'blk'=8] {'blk'}, dimensions={0} | all-to-all | bytes 8388608 | tf_op jit(solution)/shard_map/all_to_all | solution.py:409
  132.2 7.4 %filters.1 = bf16[8,32,32,256]{3,2,1,0:T(8,128)(2,1)} custom-call(bf16[32,256,256]{2,1,0:T(8,128)(2,1)} %filters_ref.1, bf16[8,32,32,256]{3,2,1,0:T(8,128)(2,1)} %all_to_all.20.coeffs_ref), custom_call_target="tpu_custom_call" | custom-call | tf_op jit(solution)/shard_map/filters/pallas_call | solution.py:272
  139.6 4.5 %all-to-all-start.2 = ((bf16[8,32,32,256]{3,2,1,0:T(8,128)(2,1)}), bf16[8,32,32,256]{3,2,1,0:T(8,128)(2,1)}, u32[]{:S(2)}, u32[]{:S(2)}) async-start(bf16[8,32,32,256]{3,2,1,0:T(8,128)(2,1)} %filters.1), calls=%async_computation.2 | async-start | bytes 8388608 | tf_op jit(solution)/shard_map/all_to_all | solution.py:411
  144.2 0.5 and_select_fusion.1.place_ref
  144.7 48.6 %all-to-all-done.2.filtered_ref = bf16[8,32,32,256]{3,2,1,0:T(8,128)(2,1)} async-done(((bf16[8,32,32,256]{3,2,1,0:T(8,128)(2,1)}), bf16[8,32,32,256]{3,2,1,0:T(8,128)(2,1)}, u32[]{:S(2)}, u32[]{:S(2)}) %all-to-all-start.2) | async-done | bytes 4194336 | tf_op jit(solution)/shard_map/all_to_all | solution.py:411
  193.3 5.3 %cycles.1 = bf16[4,8,16,16,128]{4,3,2,1,0:T(8,128)(2,1)} custom-call(s32[4]{0:T(128)} %and_select_fusion.1.place_ref, bf16[16,128,256]{2,1,0:T(8,128)(2,1)} %get-tuple-element.7.turned_ref, bf16[8,32,32,256]{3,2,1,0:T(8,128)(2,1)} %all-to-all-done.2.filtered_ref), custom_call_target="tpu_custom_call" | custom-call | tf_op jit(solution)/shard_map/cycles/pallas_call | solution.py:309
  198.6 1.6 slice_bitcast_fusion.2
  200.2 0.2 collective-permute-start.3
  200.5 1.8 collective-permute-start.4
  202.3 1.9 collective-permute-start.5
  204.3 31.1 %collective-permute-done.3 = bf16[8,16,16,128]{3,2,1,0:T(8,128)(2,1)S(1)} collective-permute-done((bf16[8,16,16,128]{3,2,1,0:T(8,128)(2,1)S(1)}, bf16[8,16,16,128]{3,2,1,0:T(8,128)(2,1)S(1)}, u32[]{:S(2)}, u32[]{:S(2)}) %collective-permute-start.3) | collective-permute-done | bytes 524320 | tf_op jit(solution)/shard_map/ppermute | solution.py:414
  235.3 7.4 %collective-permute-done.4 = bf16[8,16,16,128]{3,2,1,0:T(8,128)(2,1)S(1)} collective-permute-done((bf16[8,16,16,128]{3,2,1,0:T(8,128)(2,1)S(1)}, bf16[8,16,16,128]{3,2,1,0:T(8,128)(2,1)S(1)}, u32[]{:S(2)}, u32[]{:S(2)}) %collective-permute-start.4) | collective-permute-done | bytes 524320 | tf_op jit(solution)/shard_map/ppermute | solution.py:414
  242.7 2.3 collective-permute-done.5
  245.0 2.1 fusion.2
  247.1 5.0 %all-to-all-start.3 = ((bf16[8,16,16,128]{3,2,1,0:T(8,128)(2,1)}), bf16[8,16,16,128]{3,2,1,0:T(8,128)(2,1)S(1)}, u32[]{:S(2)}, u32[]{:S(2)}) async-start(bf16[8,16,16,128]{3,2,1,0:T(8,128)(2,1)} %fusion.2), calls=%async_computation.3 | async-start | bytes 1048576 | tf_op jit(solution)/shard_map/all_to_all | solution.py:416
  252.0 0.7 copy.6.modes_ref
  252.8 9.0 %all-to-all-done.3 = bf16[8,16,16,128]{3,2,1,0:T(8,128)(2,1)S(1)} async-done(((bf16[8,16,16,128]{3,2,1,0:T(8,128)(2,1)}), bf16[8,16,16,128]{3,2,1,0:T(8,128)(2,1)S(1)}, u32[]{:S(2)}, u32[]{:S(2)}) %all-to-all-start.3) | async-done | bytes 524320 | tf_op jit(solution)/shard_map/all_to_all | solution.py:416
  261.8 0.0 copy-start
  261.8 0.8 copy-done
  262.6 6.6 %synthesis.1 = bf16[64,16,2048]{2,1,0:T(8,128)(2,1)} custom-call(s32[128,1]{1,0:T(8,128)} %copy.6.modes_ref, bf16[128,16,128]{2,1,0:T(8,128)(2,1)} %bitcast.17), custom_call_target="tpu_custom_call" | custom-call | tf_op jit(solution)/shard_map/synthesis/pallas_call | solution.py:363
Async XLA Ops:
  0.0 10.9 %copy-start.5 = (s32[128]{0:T(128)S(1)}, s32[128]{0:T(128)}, u32[]{:S(2)}) copy-start(s32[128]{0:T(128)} %param.6) | copy-start | bytes 1540
  7.2 13.5 %all-to-all-start = ((bf16[8,16,16,128]{3,2,1,0:T(8,128)(2,1)}), bf16[8,16,16,128]{3,2,1,0:T(8,128)(2,1)S(1)}, u32[]{:S(2)}, u32[]{:S(2)}) async-start(bf16[8,16,16,128]{3,2,1,0:T(8,128)(2,1)} %bitcast.16), calls=%async_computation | async-start | bytes 1048576 | tf_op jit(solution)/shard_map/all_to_all | solution.py:403
  20.7 45.9 %copy-start.1 = (bf16[8,16,16,128]{3,2,1,0:T(8,128)(2,1)}, bf16[8,16,16,128]{3,2,1,0:T(8,128)(2,1)S(1)}, u32[]{:S(2)}) copy-start(bf16[8,16,16,128]{3,2,1,0:T(8,128)(2,1)S(1)} %all-to-all-done.refs_0_) | copy-start | bytes 1572868
  20.7 36.4 %collective-permute-start = (bf16[8,16,16,128]{3,2,1,0:T(8,128)(2,1)S(1)}, bf16[8,16,16,128]{3,2,1,0:T(8,128)(2,1)S(1)}, u32[]{:S(2)}, u32[]{:S(2)}) collective-permute-start(bf16[8,16,16,128]{3,2,1,0:T(8,128)(2,1)S(1)} %all-to-all-done.refs_0_), channel_id=1, source_target_pairs={{0,8},{8,16},{16,24},{24,0},{1,9},{9,17},{17,25},{25,1},{2,10},{10... | collective-permute-start | bytes 1572872 | tf_op jit(solution)/shard_map/ppermute | solution.py:405
  22.3 42.5 %collective-permute-start.1 = (bf16[8,16,16,128]{3,2,1,0:T(8,128)(2,1)S(1)}, bf16[8,16,16,128]{3,2,1,0:T(8,128)(2,1)S(1)}, u32[]{:S(2)}, u32[]{:S(2)}) collective-permute-start(bf16[8,16,16,128]{3,2,1,0:T(8,128)(2,1)S(1)} %all-to-all-done.refs_0_), channel_id=1, source_target_pairs={{0,16},{8,24},{16,0},{24,8},{1,17},{9,25},{17,1},{25,9},{2,18},{10... | collective-permute-start | bytes 1572872 | tf_op jit(solution)/shard_map/ppermute | solution.py:405
  23.5 43.1 %collective-permute-start.2 = (bf16[8,16,16,128]{3,2,1,0:T(8,128)(2,1)S(1)}, bf16[8,16,16,128]{3,2,1,0:T(8,128)(2,1)S(1)}, u32[]{:S(2)}, u32[]{:S(2)}) collective-permute-start(bf16[8,16,16,128]{3,2,1,0:T(8,128)(2,1)S(1)} %all-to-all-done.refs_0_), channel_id=1, source_target_pairs={{0,24},{8,0},{16,8},{24,16},{1,25},{9,1},{17,9},{25,17},{2,26},{10... | collective-permute-start | bytes 1572872 | tf_op jit(solution)/shard_map/ppermute | solution.py:405
  57.1 9.5 %copy-start.2 = (bf16[8,16,16,128]{3,2,1,0:T(8,128)(2,1)}, bf16[8,16,16,128]{3,2,1,0:T(8,128)(2,1)S(1)}, u32[]{:S(2)}) copy-start(bf16[8,16,16,128]{3,2,1,0:T(8,128)(2,1)S(1)} %collective-permute-done.refs_1_) | copy-start | bytes 1572868
  64.8 1.8 copy-start.3
  66.6 0.8 copy-start.4
  139.6 53.7 %all-to-all-start.2 = ((bf16[8,32,32,256]{3,2,1,0:T(8,128)(2,1)}), bf16[8,32,32,256]{3,2,1,0:T(8,128)(2,1)}, u32[]{:S(2)}, u32[]{:S(2)}) async-start(bf16[8,32,32,256]{3,2,1,0:T(8,128)(2,1)} %filters.1), calls=%async_computation.2 | async-start | bytes 8388608 | tf_op jit(solution)/shard_map/all_to_all | solution.py:411
  200.2 35.1 %collective-permute-start.3 = (bf16[8,16,16,128]{3,2,1,0:T(8,128)(2,1)S(1)}, bf16[8,16,16,128]{3,2,1,0:T(8,128)(2,1)S(1)}, u32[]{:S(2)}, u32[]{:S(2)}) collective-permute-start(bf16[8,16,16,128]{3,2,1,0:T(8,128)(2,1)S(1)} %get-tuple-element.11), channel_id=1, source_target_pairs={{0,8},{8,16},{16,24},{24,0},{1,9},{9,17},{17,25},{25,1},{2,10},{10... | collective-permute-start | bytes 1572872 | tf_op jit(solution)/shard_map/ppermute | solution.py:414
  200.5 42.2 %collective-permute-start.4 = (bf16[8,16,16,128]{3,2,1,0:T(8,128)(2,1)S(1)}, bf16[8,16,16,128]{3,2,1,0:T(8,128)(2,1)S(1)}, u32[]{:S(2)}, u32[]{:S(2)}) collective-permute-start(bf16[8,16,16,128]{3,2,1,0:T(8,128)(2,1)S(1)} %get-tuple-element.13), channel_id=1, source_target_pairs={{0,16},{8,24},{16,0},{24,8},{1,17},{9,25},{17,1},{25,9},{2,18},{10... | collective-permute-start | bytes 1572872 | tf_op jit(solution)/shard_map/ppermute | solution.py:414
  202.3 42.6 %collective-permute-start.5 = (bf16[8,16,16,128]{3,2,1,0:T(8,128)(2,1)S(1)}, bf16[8,16,16,128]{3,2,1,0:T(8,128)(2,1)S(1)}, u32[]{:S(2)}, u32[]{:S(2)}) collective-permute-start(bf16[8,16,16,128]{3,2,1,0:T(8,128)(2,1)S(1)} %get-tuple-element.12), channel_id=1, source_target_pairs={{0,24},{8,0},{16,8},{24,16},{1,25},{9,1},{17,9},{25,17},{2,26},{10... | collective-permute-start | bytes 1572872 | tf_op jit(solution)/shard_map/ppermute | solution.py:414
  247.1 14.7 %all-to-all-start.3 = ((bf16[8,16,16,128]{3,2,1,0:T(8,128)(2,1)}), bf16[8,16,16,128]{3,2,1,0:T(8,128)(2,1)S(1)}, u32[]{:S(2)}, u32[]{:S(2)}) async-start(bf16[8,16,16,128]{3,2,1,0:T(8,128)(2,1)} %fusion.2), calls=%async_computation.3 | async-start | bytes 1048576 | tf_op jit(solution)/shard_map/all_to_all | solution.py:416
  261.8 0.8 copy-start

commit v2 on v1

--- a/solution.py
+++ b/solution.py
@@ -12,6 +12,7 @@
 VMEM_LIMIT = 56 * 1024 * 1024
 F32 = jnp.float32
 BF16 = jnp.bfloat16
+COST = pl.CostEstimate(flops=2_000_000_000, bytes_accessed=12_000_000, transcendentals=0)
 
 
 def params(**kw):
@@ -178,144 +179,139 @@
             pltpu.VMEM((lane_blocks(cycles), slots * modes, 128), F32),
         ],
         compiler_params=params(),
-        cost_estimate=pl.CostEstimate(flops=40_000_000, bytes_accessed=4_000_000, transcendentals=0),
+        cost_estimate=pl.CostEstimate(flops=40_000_000, bytes_accessed=30_000_000, transcendentals=0),
         name="legendre",
     )(degrees, m, jnp.cos(colatitude)[None, :], seed)
 
 
-def harmonic_kernel(place_ref, lat_ref, *refs):
-    parts = len(refs) - 4
-    spectra, out_ref, all_ref, wide_ref, turn_ref = refs[:parts], *refs[parts:]
+def harmonic_kernel(lat_ref, *refs):
+    parts = len(refs) - 2
+    spectra, out_ref, turn_ref = refs[:parts], *refs[parts:]
     groups, modes, cycles, pair = spectra[0].shape
-    chans = pair // 2
-    total = chans * parts
-    dests, slot_dev = out_ref.shape[:2]
-    slots = dests * slot_dev
-    rows = 2 * modes
-    step = pl.program_id(0)
-
-    @pl.when(step == 0)
-    def _():
+    slots = out_ref.shape[0] * out_ref.shape[1]
+    for j in range(modes):
         for t in range(parts):
-            all_ref[place_ref[t]] = spectra[t][...]
-        for j in range(modes):
-            pieces = [all_ref[z, :, j].reshape(groups * cycles, pair) for z in range(parts)]
-            for k in range(2):
-                wide_ref[j, :, k * total : (k + 1) * total] = jnp.concatenate(
-                    [p[:, k * chans : (k + 1) * chans] for p in pieces], axis=1
-                )
-
-    lanes = turn_ref.shape[2]
-    for j in range(modes):
-        result = jnp.dot(lat_ref[j], wide_ref[j], preferred_element_type=F32)
-        for k in range(2):
-            for h in range(total // lanes):
-                turn_ref[h, pl.ds(2 * j + k, slots, stride=rows), :] = result[
-                    :, k * total + h * lanes : k * total + (h + 1) * lanes
-                ]
-    for h in range(total // lanes):
-        out_ref[:, :, :, h * lanes : (h + 1) * lanes] = (
-            turn_ref[h].astype(BF16).reshape(dests, slot_dev, rows, lanes)
-        )
-
-
-def harmonic(place, lat, spectra, slot_dev):
+            result = jnp.dot(
+                lat_ref[j], spectra[t][:, j].reshape(groups * cycles, pair), preferred_element_type=F32
+            )
+            put(turn_ref.at[t], pl.ds(j, slots, stride=modes), result)
+    for t in range(parts):
+        value = get(turn_ref.at[t], slice(None), pair).astype(BF16)
+        out_ref[:, :, :, t * pair : (t + 1) * pair] = value.reshape(out_ref.shape[:3] + (pair,))
+
+
+def harmonic(lat, spectra, slot_dev):
     modes, slots, cycle_total = lat.shape
     groups, _, cycles, pair = spectra[0].shape
-    total = pair // 2 * len(spectra)
+    parts = len(spectra)
     dests = slots // slot_dev
     steps = divisor(dests, 2)
-    lanes = min(128, total)
     whole = pl.BlockSpec((groups, modes, cycles, pair), lambda i: (0, 0, 0, 0))
     return pl.pallas_call(
         harmonic_kernel,
         grid=(steps,),
+        in_specs=[pl.BlockSpec((modes, slots // steps, cycle_total), lambda i: (0, i, 0))] + [whole] * parts,
+        out_specs=pl.BlockSpec((dests // steps, slot_dev, modes, parts * pair), lambda i: (i, 0, 0, 0)),
+        out_shape=jax.ShapeDtypeStruct((dests, slot_dev, modes, parts * pair), BF16),
+        scratch_shapes=[pltpu.VMEM((parts, lane_blocks(pair), slots // steps * modes, 128), F32)],
+        compiler_params=params(),
+        cost_estimate=COST,
+        name="harmonic",
+    )(lat, *spectra)
+
+
+def filter_kernel(hops, counts, place_ref, filters_ref, *refs):
+    inputs, outs, all_ref, turn_ref = refs[: len(counts)], refs[len(counts) : -2], *refs[-2:]
+    groups, slots, modes, _ = inputs[0].shape
+    pair = all_ref.shape[4]
+    chans = pair // 2
+    parts = all_ref.shape[0]
+    t = 0
+    for ref, count in zip(inputs, counts):
+        for i in range(count):
+            all_ref[place_ref[t]] = ref[:, :, :, i * pair : (i + 1) * pair]
+            t += 1
+    rows = groups * modes
+    for s in range(slots):
+        pieces = [all_ref[z, :, s].reshape(rows, pair) for z in range(parts)]
+        both = [
+            jnp.concatenate([p[:, k * chans : (k + 1) * chans] for p in pieces], axis=1) for k in range(2)
+        ]
+        left = jnp.concatenate(both, axis=0)
+        for i, hop in enumerate(hops):
+            start = pl.multiple_of(place_ref[hop] * chans, chans)
+            result = lax.dot_general(
+                left, filters_ref[s, pl.ds(start, chans), :], (((1,), (1,)), ((), ())), preferred_element_type=F32
+            )
+            put(
+                turn_ref.at[i],
+                pl.ds(s, rows, stride=slots),
+                jnp.concatenate([result[:rows], result[rows:]], axis=1),
+            )
+    i = 0
+    for ref in outs:
+        for n in range(ref.shape[3] // pair):
+            value = get(turn_ref.at[i], slice(None), pair).astype(BF16)
+            ref[:, :, :, n * pair : (n + 1) * pair] = value.reshape(ref.shape[:3] + (pair,))
+            i += 1
+
+
+def apply_filters(place, filters, coeffs, counts, wanted):
+    groups, slots, modes, _ = coeffs[0].shape
+    total = filters.shape[2]
+    pair = coeffs[0].shape[3] // counts[0]
+    step = min(slots, 16)
+    hops = sum(wanted, [])
+    return pl.pallas_call(
+        functools.partial(filter_kernel, hops, counts),
+        grid=(slots // step,),
         in_specs=[
             pl.BlockSpec(memory_space=pltpu.SMEM),
-            pl.BlockSpec((modes, slots // steps, cycle_total), lambda i: (0, i, 0)),
+            pl.BlockSpec((step, total, total), lambda i: (i, 0, 0)),
         ]
-        + [whole] * len(spectra),
-        out_specs=pl.BlockSpec((dests // steps, slot_dev, 2 * modes, total), lambda i: (i, 0, 0, 0)),
-        out_shape=jax.ShapeDtypeStruct((dests, slot_dev, 2 * modes, total), BF16),
+        + [pl.BlockSpec((groups, step, modes, n * pair), lambda i: (0, i, 0, 0)) for n in counts],
+        out_specs=[
+            pl.BlockSpec((groups, modes, step, len(w) * pair), lambda i: (0, 0, i, 0)) for w in wanted
+        ],
+        out_shape=[jax.ShapeDtypeStruct((groups, modes, slots, len(w) * pair), BF16) for w in wanted],
         scratch_shapes=[
-            pltpu.VMEM((len(spectra), groups, modes, cycles, pair), BF16),
-            pltpu.VMEM((modes, cycle_total, 2 * total), BF16),
-            pltpu.VMEM((total // lanes, slots // steps * 2 * modes, lanes), F32),
-        ],
-        compiler_params=params(),
-        name="harmonic",
-    )(place, lat, *spectra)
-
-
-def filter_kernel(filters_ref, coeffs_ref, out_ref, turn_ref):
-    groups, slots, rows, total = coeffs_ref.shape
-    lanes = turn_ref.shape[2]
-    for s in range(slots):
-        result = lax.dot_general(
-            coeffs_ref[:, s].reshape(groups * rows, total),
-            filters_ref[s],
-            (((1,), (1,)), ((), ())),
+            pltpu.VMEM((sum(counts), groups, step, modes, pair), BF16),
+            pltpu.VMEM((len(hops), lane_blocks(pair), groups * modes * step, 128), F32),
+        ],
+        compiler_params=params(),
+        cost_estimate=COST,
+        name="filters",
+    )(place, filters, *coeffs)
+
+
+def cycles_kernel(scale, turned_ref, filtered_ref, *outs):
+    groups, modes, slot_dev, width = filtered_ref.shape
+    blocks, _, cycles, pair = outs[0].shape
+    for j in range(modes):
+        result = jnp.dot(
+            turned_ref[j],
+            filtered_ref[:, j].reshape(groups * slot_dev, width),
             preferred_element_type=F32,
         )
-        for h in range(total // lanes):
-            turn_ref[h, pl.ds(s, groups * rows, stride=slots), :] = result[:, h * lanes : (h + 1) * lanes]
-    for h in range(total // lanes):
-        out_ref[:, :, :, h * lanes : (h + 1) * lanes] = (
-            turn_ref[h].astype(BF16).reshape(groups, rows, slots, lanes)
-        )
-
-
-def apply_filters(filters, coeffs):
-    groups, slots, rows, total = coeffs.shape
-    step = min(slots, 16)
-    lanes = min(128, total)
-    return pl.pallas_call(
-        filter_kernel,
-        grid=(slots // step,),
-        in_specs=[
-            pl.BlockSpec((step, total, total), lambda i: (i, 0, 0)),
-            pl.BlockSpec((groups, step, rows, total), lambda i: (0, i, 0, 0)),
-        ],
-        out_specs=pl.BlockSpec((groups, rows, step, total), lambda i: (0, 0, i, 0)),
-        out_shape=jax.ShapeDtypeStruct((groups, rows, slots, total), BF16),
-        scratch_shapes=[pltpu.VMEM((total // lanes, groups * rows * step, lanes), F32)],
-        compiler_params=params(),
-        name="filters",
-    )(filters, coeffs)
-
-
-def cycles_kernel(scale, place_ref, turned_ref, filtered_ref, out_ref):
-    groups, rows, slot_dev, total = filtered_ref.shape
-    parts, blocks, modes, cycles, pair = out_ref.shape
-    chans = pair // 2
-    for j in range(modes):
-        result = [
-            jnp.dot(
-                turned_ref[j],
-                filtered_ref[:, 2 * j + k].reshape(groups * slot_dev, total),
-                preferred_element_type=F32,
-            )
-            for k in range(2)
-        ]
-        for z in range(parts):
-            piece = jnp.concatenate([r[:, z * chans : (z + 1) * chans] for r in result], axis=1) * scale
-            out_ref[place_ref[z], :, j] = piece.astype(BF16).reshape(blocks, cycles, pair)
-
-
-def to_cycles(place, turned, filtered, scale, blocks, parts):
+        result = (result * scale).astype(BF16)
+        for t, ref in enumerate(outs):
+            ref[:, j] = result[:, t * pair : (t + 1) * pair].reshape(blocks, cycles, pair)
+
+
+def to_cycles(turned, filtered, scale, blocks, parts):
     modes, cycle_total, slots = turned.shape
-    groups, rows, slot_dev, total = filtered.shape
+    width = filtered.shape[3]
     vmem = pl.BlockSpec(memory_space=pltpu.VMEM)
+    shape = (blocks, modes, cycle_total // blocks, width // parts)
     return pl.pallas_call(
         functools.partial(cycles_kernel, scale),
-        in_specs=[pl.BlockSpec(memory_space=pltpu.SMEM), vmem, vmem],
-        out_specs=vmem,
-        out_shape=jax.ShapeDtypeStruct(
-            (parts, blocks, modes, cycle_total // blocks, 2 * total // parts), BF16
-        ),
-        compiler_params=params(),
+        in_specs=[vmem, vmem],
+        out_specs=[vmem] * parts,
+        out_shape=[jax.ShapeDtypeStruct(shape, BF16)] * parts,
+        compiler_params=params(),
+        cost_estimate=COST,
         name="cycles",
-    )(place, turned, filtered)
+    )(turned, filtered)
 
 
 def synthesis_kernel(modes_ref, parts_ref, out_ref, phase_ref, wide_ref, turn_ref, left_ref):
@@ -401,18 +397,46 @@
     spectra = analysis(sky_maps, local_factor, band_order_values)
     spectra = spectra.reshape(blk_groups, mode_dev, cycle_dev, 2 * chans)
     spectra = lax.all_to_all(spectra, "blk", split_axis=0, concat_axis=0, tiled=True)
-    shift = [[(i, (i + t) % chan_groups) for i in range(chan_groups)] for t in range(chan_groups)]
-    gathered = [spectra] + [lax.ppermute(spectra, "chan", shift[t]) for t in range(1, chan_groups)]
+    def swap(value, t):
+        return lax.ppermute(value, "chan", [(i, i ^ t) for i in range(chan_groups)])
+
+    def exchange(value):
+        return lax.all_to_all(value, "blk", split_axis=0, concat_axis=0, tiled=True)
+
+    near = max(1, chan_groups // 2)
+    hops = [[0], list(range(1, near)), list(range(near, chan_groups))]
+    hops = [h for h in hops if h]
+    counts = [len(h) for h in hops]
+    place = jnp.arange(chan_groups, dtype=jnp.int32) ^ chan
+    gathered = [spectra]
+    for t in range(1, chan_groups):
+        top = 1 << (t.bit_length() - 1)
+        gathered.append(swap(gathered[0], t) if t == top else swap(gathered[top], t ^ top))
     lat, turned = legendre(degrees, local_modes, colatitude, degree_count)
-    hops = jnp.arange(chan_groups, dtype=jnp.int32)
-    coeffs = harmonic((chan - hops) % chan_groups, lat, gathered, slot_dev)
-    coeffs = lax.all_to_all(coeffs, "blk", split_axis=0, concat_axis=0, tiled=True)
-    filtered = apply_filters(filters, coeffs)
-    filtered = lax.all_to_all(filtered, "blk", split_axis=0, concat_axis=0, tiled=True)
+    coeffs = []
+    for part in hops:
+        incoming = [gathered[t] for t in part]
+        result = harmonic(lat, incoming, slot_dev)
+        if coeffs:
+            result, coeffs[-1] = lax.optimization_barrier((result, coeffs[-1]))
+        lat, result = lax.optimization_barrier((lat, result))
+        coeffs.append(exchange(result))
     scale = 2.0 / math.sqrt(degree_count)
-    partial = to_cycles((hops - chan) % chan_groups, turned, filtered, scale, blk_groups, chan_groups)
-    arrived = [partial[0]] + [lax.ppermute(partial[t], "chan", shift[t]) for t in range(1, chan_groups)]
-    cycle_part = functools.reduce(jnp.add, [a.astype(F32) for a in arrived]).astype(BF16)
+    far = apply_filters(place, filters, coeffs, counts, hops[-1:])
+    place, far = lax.optimization_barrier((place, far))
+    rest = apply_filters(place, filters, coeffs, counts, hops[-2::-1])
+    partial = {}
+    for part, filtered in zip(hops[::-1], list(far) + list(rest)):
+        partial.update(zip(part, to_cycles(turned, exchange(filtered), scale, blk_groups, len(part))))
+    total = partial[0].astype(F32)
+    top = chan_groups // 2
+    while top:
+        group = partial[top].astype(F32)
+        for t in range(top + 1, 2 * top):
+            group = group + swap(partial[t], t ^ top).astype(F32)
+        total = total + swap(group.astype(BF16), top).astype(F32)
+        top //= 2
+    cycle_part = total.astype(BF16)
     by_cycle = lax.all_to_all(cycle_part, "blk", split_axis=0, concat_axis=0, tiled=True)
     by_cycle = by_cycle.reshape(blk_groups * mode_dev, cycle_dev, 2 * chans)
     return synthesis(by_cycle, band_order_values, pixels)

time: 270 us -> 235 us (0.87)
  the two profiles are of different devices: /device:TPU:8 before, /device:TPU:0 now
where the time goes in v2:
time: 235 us; the launch traced here: 234 us
  waiting for transfers between devices  120 us (51%)
  Pallas kernels  59.4 us (25%)
  starting transfers between devices  39.7 us (17%)
  local copies, waits for them, and re-layouts  9.81 us (4%)
  other arithmetic  4.13 us (2%)
    all_to_all x6, waiting for transfers between devices, exchange(): return lax.all_to_all(value, 'blk', split_axis=0, concat_axis=0, tiled=True)  65.4 us
    ppermute x6, waiting for transfers between devices, swap(): return lax.ppermute(value, 'chan', [(i, i ^ t) for i in range(chan_groups)])  46.1 us
    all_to_all x6, starting transfers between devices, exchange(): return lax.all_to_all(value, 'blk', split_axis=0, concat_axis=0, tiled=True)  22.9 us
    pallas_call x2, Pallas kernels, apply_filters(): pl.pallas_call(functools.partial(filter_kernel, hops, counts), grid=(slot...  16.2 us
    pallas_call x3, Pallas kernels, harmonic(): pl.pallas_call(harmonic_kernel, grid=(steps,), in_specs=[pl.BlockSpec((mo...  11.4 us
    pallas_call x1, Pallas kernels, legendre(): pl.pallas_call(functools.partial(legendre_kernel, levels), in_specs=[pl.B...  9.81 us
    all_to_all x1, waiting for transfers between devices, body(): lax.all_to_all(cycle_part, 'blk', split_axis=0, concat_axis=0, tiled=True)  9.01 us
    pallas_call x3, Pallas kernels, to_cycles(): pl.pallas_call(functools.partial(cycles_kernel, scale), in_specs=[vmem, v...  8.92 us
  transfers between devices with their start and end apart: 14, of which 9 were waited for; matrix products, arithmetic and copies ran while one was open for 2% of the time, Pallas kernels for 15%

profile of v2, /device:TPU:0, one launch (start us, length us, event | category | flops | bytes accessed | tf_op | source)
XLA Modules:
  0.0 233.7 jit_solution(14357632689882383975)
XLA Ops:
  0.0 0.1 broadcast_multiply_fusion
  0.1 0.6 dynamic_slice.11.factor_ref
  0.7 6.5 %analysis.1 = bf16[128,16,128]{2,1,0:T(8,128)(2,1)} custom-call(f32[16]{0:T(128)} %dynamic_slice.11.factor_ref, s32[1,128]{1,0:T(1,128)} %bitcast.7, bf16[64,16,2048]{2,1,0:T(8,128)(2,1)} %sky_ref.1), custom_call_target="tpu_custom_call" | custom-call | tf_op jit(solution)/shard_map/analysis/pallas_call | solution.py:92
  7.1 5.2 %all-to-all-start = ((bf16[8,16,16,128]{3,2,1,0:T(8,128)(2,1)}), bf16[8,16,16,128]{3,2,1,0:T(8,128)(2,1)S(1)}, u32[]{:S(2)}, u32[]{:S(2)}) async-start(bf16[8,16,16,128]{3,2,1,0:T(8,128)(2,1)} %bitcast.5), calls=%async_computation | async-start | bytes 1048576 | tf_op jit(solution)/shard_map/all_to_all | solution.py:399
  12.3 0.0 copy-done.10
  12.3 0.2 add_multiply_fusion
  12.5 0.7 copy.5.order_ref
  13.2 1.4 dynamic_slice.9.degree_ref
  14.5 0.1 fusion.6
  14.6 0.5 add_cosine_fusion.cosine_ref
  15.1 0.7 add_exponential_fusion.seed_ref
  15.8 9.8 %legendre.1 = (bf16[16,256,128]{2,1,0:T(8,128)(2,1)}, bf16[16,128,256]{2,1,0:T(8,128)(2,1)}) custom-call(s32[256]{0:T(256)} %dynamic_slice.9.degree_ref, f32[16,1]{1,0:T(8,128)} %copy.5.order_ref, f32[1,128]{1,0:T(1,128)} %add_cosine_fusion.cosine_ref, f32[16,128]{1,0:T(8,128)} %add_exponential_fusion.seed_ref), custom_call_target="tpu_custom_call" | custom-call | flops 40000000 | bytes 30000000 | tf_op jit(solution)/shard_map/legendre/pallas_call | solution.py:168
  25.6 0.0 all-to-all-done.refs_0_
  25.6 0.8 copy-done.8
  26.4 3.1 %harmonic.3 = bf16[8,32,16,128]{3,2,1,0:T(8,128)(2,1)} custom-call(bf16[16,256,128]{2,1,0:T(8,128)(2,1)} %get-tuple-element.28.lat_ref, bf16[8,16,16,128]{3,2,1,0:T(8,128)(2,1)} %copy-done.8), custom_call_target="tpu_custom_call" | custom-call | flops 2000000000 | bytes 12000000 | tf_op jit(solution)/shard_map/harmonic/pallas_call | solution.py:210
  29.5 4.3 %all-to-all-start.1 = ((bf16[8,32,16,128]{3,2,1,0:T(8,128)(2,1)}), bf16[8,32,16,128]{3,2,1,0:T(8,128)(2,1)S(1)}, u32[]{:S(2)}, u32[]{:S(2)}) async-start(bf16[8,32,16,128]{3,2,1,0:T(8,128)(2,1)} %harmonic.3), calls=%async_computation.1 | async-start | bytes 2097152 | tf_op jit(solution)/shard_map/all_to_all | solution.py:404
  33.9 0.0 copy-done.9
  33.9 1.6 collective-permute-start
  35.5 2.6 %collective-permute-start.1 = (bf16[8,16,16,128]{3,2,1,0:T(8,128)(2,1)S(1)}, bf16[8,16,16,128]{3,2,1,0:T(8,128)(2,1)S(1)}, u32[]{:S(2)}, u32[]{:S(2)}) collective-permute-start(bf16[8,16,16,128]{3,2,1,0:T(8,128)(2,1)S(1)} %copy-done.9), channel_id=1, source_target_pairs={{0,16},{8,24},{16,0},{24,8},{1,17},{9,25},{17,1},{25,9},{2,18},{10... | collective-permute-start | bytes 1572872 | tf_op jit(solution)/shard_map/ppermute | solution.py:401
  38.1 21.2 %collective-permute-done.refs_0_ = bf16[8,16,16,128]{3,2,1,0:T(8,128)(2,1)S(1)} collective-permute-done((bf16[8,16,16,128]{3,2,1,0:T(8,128)(2,1)S(1)}, bf16[8,16,16,128]{3,2,1,0:T(8,128)(2,1)S(1)}, u32[]{:S(2)}, u32[]{:S(2)}) %collective-permute-start) | collective-permute-done | bytes 524320 | tf_op jit(solution)/shard_map/ppermute | solution.py:401
  59.3 0.8 copy-done.12
  60.1 3.2 %harmonic.4 = bf16[8,32,16,128]{3,2,1,0:T(8,128)(2,1)} custom-call(bf16[16,256,128]{2,1,0:T(8,128)(2,1)} %get-tuple-element.28.lat_ref, bf16[8,16,16,128]{3,2,1,0:T(8,128)(2,1)} %copy-done.12), custom_call_target="tpu_custom_call" | custom-call | flops 2000000000 | bytes 12000000 | tf_op jit(solution)/shard_map/harmonic/pallas_call | solution.py:210
  63.3 0.0 all-to-all-done.1.refs_0_
  63.3 3.8 %all-to-all-start.2 = ((bf16[8,32,16,128]{3,2,1,0:T(8,128)(2,1)}), bf16[8,32,16,128]{3,2,1,0:T(8,128)(2,1)S(1)}, u32[]{:S(2)}, u32[]{:S(2)}) async-start(bf16[8,32,16,128]{3,2,1,0:T(8,128)(2,1)} %harmonic.4), calls=%async_computation.2 | async-start | bytes 2097152 | tf_op jit(solution)/shard_map/all_to_all | solution.py:404
  67.1 0.0 collective-permute-done.1.refs_0_
  67.1 0.0 copy-start.11
  67.1 0.1 collective-permute-start.2
  67.2 14.3 %collective-permute-done.2.refs_1_ = bf16[8,16,16,128]{3,2,1,0:T(8,128)(2,1)S(1)} collective-permute-done((bf16[8,16,16,128]{3,2,1,0:T(8,128)(2,1)S(1)}, bf16[8,16,16,128]{3,2,1,0:T(8,128)(2,1)S(1)}, u32[]{:S(2)}, u32[]{:S(2)}) %collective-permute-start.2) | collective-permute-done | bytes 524320 | tf_op jit(solution)/shard_map/ppermute | solution.py:401
  81.5 0.0 copy-done.11
  81.5 0.8 copy-done.13
  82.3 5.1 %harmonic.5 = bf16[8,32,16,256]{3,2,1,0:T(8,128)(2,1)} custom-call(bf16[16,256,128]{2,1,0:T(8,128)(2,1)} %get-tuple-element.28.lat_ref, bf16[8,16,16,128]{3,2,1,0:T(8,128)(2,1)} %copy-done.11, bf16[8,16,16,128]{3,2,1,0:T(8,128)(2,1)} %copy-done.13), custom_call_target="tpu_custom_call" | custom-call | flops 2000000000 | bytes 12000000 | tf_op jit(solution)/shard_map/harmonic/pallas_call | solution.py:210
  87.4 0.0 all-to-all-done.2.refs_1_
  87.4 1.0 copy-done.2
  88.4 3.8 %all-to-all-start.3 = ((bf16[8,32,16,256]{3,2,1,0:T(8,128)(2,1)}), bf16[8,32,16,256]{3,2,1,0:T(8,128)(2,1)S(1)}, u32[]{:S(2)}, u32[]{:S(2)}) async-start(bf16[8,32,16,256]{3,2,1,0:T(8,128)(2,1)} %harmonic.5), calls=%async_computation.3 | async-start | bytes 4194304 | tf_op jit(solution)/shard_map/all_to_all | solution.py:404
  92.2 0.5 iota_xor_fusion.place_ref
  92.7 26.2 %all-to-all-done.3.refs_2_ = bf16[8,32,16,256]{3,2,1,0:T(8,128)(2,1)S(1)} async-done(((bf16[8,32,16,256]{3,2,1,0:T(8,128)(2,1)}), bf16[8,32,16,256]{3,2,1,0:T(8,128)(2,1)S(1)}, u32[]{:S(2)}, u32[]{:S(2)}) %all-to-all-start.3) | async-done | bytes 2097184 | tf_op jit(solution)/shard_map/all_to_all | solution.py:404
  118.9 1.3 copy-done
  120.2 8.1 %filters.2 = bf16[8,16,32,256]{3,2,1,0:T(8,128)(2,1)} custom-call(s32[4]{0:T(128)} %iota_xor_fusion.place_ref, bf16[32,256,256]{2,1,0:T(8,128)(2,1)} %filters_ref.3, bf16[8,32,16,128]{3,2,1,0:T(8,128)(2,1)} %copy-done.1, bf16[8,32,16,128]{3,2,1,0:T(8,128)(2,1)} %copy-done.2, bf16[8,32,16,256]{3,2,1,0:T(8,128)(2,1)} %copy-done), custom_call_target="tpu_custom_call" | custom-call | flops 2000000000 | bytes 12000000 | tf_op jit(solution)/shard_map/filters/pallas_call | solution.py:265
  128.3 3.6 %all-to-all-start.5 = ((bf16[8,16,32,256]{3,2,1,0:T(8,128)(2,1)}), bf16[8,16,32,256]{3,2,1,0:T(8,128)(2,1)S(1)}, u32[]{:S(2)}, u32[]{:S(2)}) async-start(bf16[8,16,32,256]{3,2,1,0:T(8,128)(2,1)} %filters.2), calls=%async_computation.5 | async-start | bytes 4194304 | tf_op jit(solution)/shard_map/all_to_all | solution.py:404
  132.0 8.1 %filters.3 = (bf16[8,16,32,128]{3,2,1,0:T(8,128)(2,1)}, bf16[8,16,32,128]{3,2,1,0:T(8,128)(2,1)}) custom-call(s32[4]{0:T(128)} %iota_xor_fusion.place_ref, bf16[32,256,256]{2,1,0:T(8,128)(2,1)} %filters_ref.3, bf16[8,32,16,128]{3,2,1,0:T(8,128)(2,1)} %copy-done.1, bf16[8,32,16,128]{3,2,1,0:T(8,128)(2,1)} %copy-done.2, bf16[8,32,16,256]{3,2,1,0:T(8,128)(2,1)} %copy-done), custom_call_target="tpu_custom_call" | custom-call | flops 2000000000 | bytes 12000000 | tf_op jit(solution)/shard_map/filters/pallas_call | solution.py:265
  140.0 18.5 %all-to-all-done.5.filtered_ref = bf16[8,16,32,256]{3,2,1,0:T(8,128)(2,1)S(1)} async-done(((bf16[8,16,32,256]{3,2,1,0:T(8,128)(2,1)}), bf16[8,16,32,256]{3,2,1,0:T(8,128)(2,1)S(1)}, u32[]{:S(2)}, u32[]{:S(2)}) %all-to-all-start.5) | async-done | bytes 2097184 | tf_op jit(solution)/shard_map/all_to_all | solution.py:404
  158.5 3.6 %all-to-all-start.6 = ((bf16[8,16,32,128]{3,2,1,0:T(8,128)(2,1)}), bf16[8,16,32,128]{3,2,1,0:T(8,128)(2,1)S(1)}, u32[]{:S(2)}, u32[]{:S(2)}) async-start(bf16[8,16,32,128]{3,2,1,0:T(8,128)(2,1)} %get-tuple-element.38), calls=%async_computation.6 | async-start | bytes 2097152 | tf_op jit(solution)/shard_map/all_to_all | solution.py:404
  162.1 3.4 %cycles.4 = (bf16[8,16,16,128]{3,2,1,0:T(8,128)(2,1)}, bf16[8,16,16,128]{3,2,1,0:T(8,128)(2,1)}) custom-call(bf16[16,128,256]{2,1,0:T(8,128)(2,1)} %get-tuple-element.22.turned_ref, bf16[8,16,32,256]{3,2,1,0:T(8,128)(2,1)} %copy-done.4), custom_call_target="tpu_custom_call" | custom-call | flops 2000000000 | bytes 12000000 | tf_op jit(solution)/shard_map/cycles/pallas_call | solution.py:306
  165.5 0.3 collective-permute-start.3
  165.8 11.7 %all-to-all-done.6.filtered_ref = bf16[8,16,32,128]{3,2,1,0:T(8,128)(2,1)S(1)} async-done(((bf16[8,16,32,128]{3,2,1,0:T(8,128)(2,1)}), bf16[8,16,32,128]{3,2,1,0:T(8,128)(2,1)S(1)}, u32[]{:S(2)}, u32[]{:S(2)}) %all-to-all-start.6) | async-done | bytes 1048608 | tf_op jit(solution)/shard_map/all_to_all | solution.py:404
  177.4 3.7 %all-to-all-start.4 = ((bf16[8,16,32,128]{3,2,1,0:T(8,128)(2,1)}), bf16[8,16,32,128]{3,2,1,0:T(8,128)(2,1)S(1)}, u32[]{:S(2)}, u32[]{:S(2)}) async-start(bf16[8,16,32,128]{3,2,1,0:T(8,128)(2,1)} %get-tuple-element.34), calls=%async_computation.4 | async-start | bytes 2097152 | tf_op jit(solution)/shard_map/all_to_all | solution.py:404
  181.2 0.0 copy-done.6
  181.2 0.0 copy-start.7
  181.2 2.8 %cycles.5 = bf16[8,16,16,128]{3,2,1,0:T(8,128)(2,1)} custom-call(bf16[16,128,256]{2,1,0:T(8,128)(2,1)} %get-tuple-element.22.turned_ref, bf16[8,16,32,128]{3,2,1,0:T(8,128)(2,1)} %copy-done.6), custom_call_target="tpu_custom_call" | custom-call | flops 2000000000 | bytes 12000000 | tf_op jit(solution)/shard_map/cycles/pallas_call | solution.py:306
  184.0 0.3 collective-permute-start.5
  184.3 0.0 collective-permute-done.3
  184.3 0.1 add_convert_fusion.1
  184.5 2.8 %collective-permute-start.4 = (bf16[8,16,16,128]{3,2,1,0:T(8,128)(2,1)S(1)}, bf16[8,16,16,128]{3,2,1,0:T(8,128)(2,1)S(1)}, u32[]{:S(2)}, u32[]{:S(2)}) collective-permute-start(bf16[8,16,16,128]{3,2,1,0:T(8,128)(2,1)S(1)} %add_convert_fusion.1), channel_id=1, source_target_pairs={{0,16},{8,24},{16,0},{24,8},{1,17},{9,25},{17,1},{25,9},{2,18},{10... | collective-permute-start | bytes 1572872 | tf_op jit(solution)/shard_map/ppermute | solution.py:401
  187.3 9.0 %all-to-all-done.4.filtered_ref = bf16[8,16,32,128]{3,2,1,0:T(8,128)(2,1)S(1)} async-done(((bf16[8,16,32,128]{3,2,1,0:T(8,128)(2,1)}), bf16[8,16,32,128]{3,2,1,0:T(8,128)(2,1)S(1)}, u32[]{:S(2)}, u32[]{:S(2)}) %all-to-all-start.4) | async-done | bytes 1048608 | tf_op jit(solution)/shard_map/all_to_all | solution.py:404
  196.3 1.0 copy-done.5
  197.3 2.8 %cycles.3 = bf16[8,16,16,128]{3,2,1,0:T(8,128)(2,1)} custom-call(bf16[16,128,256]{2,1,0:T(8,128)(2,1)} %get-tuple-element.22.turned_ref, bf16[8,16,32,128]{3,2,1,0:T(8,128)(2,1)} %copy-done.5), custom_call_target="tpu_custom_call" | custom-call | flops 2000000000 | bytes 12000000 | tf_op jit(solution)/shard_map/cycles/pallas_call | solution.py:306
  200.1 9.2 %collective-permute-done.5 = bf16[8,16,16,128]{3,2,1,0:T(8,128)(2,1)S(1)} collective-permute-done((bf16[8,16,16,128]{3,2,1,0:T(8,128)(2,1)}, bf16[8,16,16,128]{3,2,1,0:T(8,128)(2,1)S(1)}, u32[]{:S(2)}, u32[]{:S(2)}) %collective-permute-start.5) | collective-permute-done | bytes 524320 | tf_op jit(solution)/shard_map/ppermute | solution.py:401
  209.3 1.3 collective-permute-done.4
  210.6 2.0 add_convert_fusion
  212.6 3.9 %all-to-all-start.7 = ((bf16[8,16,16,128]{3,2,1,0:T(8,128)(2,1)}), bf16[8,16,16,128]{3,2,1,0:T(8,128)(2,1)S(1)}, u32[]{:S(2)}, u32[]{:S(2)}) async-start(bf16[8,16,16,128]{3,2,1,0:T(8,128)(2,1)} %add_convert_fusion), calls=%async_computation.7 | async-start | bytes 1048576 | tf_op jit(solution)/shard_map/all_to_all | solution.py:440
  216.5 0.7 copy.6.modes_ref
  217.2 9.0 %all-to-all-done.7 = bf16[8,16,16,128]{3,2,1,0:T(8,128)(2,1)S(1)} async-done(((bf16[8,16,16,128]{3,2,1,0:T(8,128)(2,1)}), bf16[8,16,16,128]{3,2,1,0:T(8,128)(2,1)S(1)}, u32[]{:S(2)}, u32[]{:S(2)}) %all-to-all-start.7) | async-done | bytes 524320 | tf_op jit(solution)/shard_map/all_to_all | solution.py:440
  226.3 0.8 copy-done.3
  227.1 6.6 %synthesis.1 = bf16[64,16,2048]{2,1,0:T(8,128)(2,1)} custom-call(s32[128,1]{1,0:T(8,128)} %copy.6.modes_ref, bf16[128,16,128]{2,1,0:T(8,128)(2,1)} %bitcast.6), custom_call_target="tpu_custom_call" | custom-call | tf_op jit(solution)/shard_map/synthesis/pallas_call | solution.py:359
  (15 shorter events, 0.0 us)
Async XLA Ops:
  0.7 11.7 %copy-start.10 = (s32[128]{0:T(128)S(1)}, s32[128]{0:T(128)}, u32[]{:S(2)}) copy-start(s32[128]{0:T(128)} %param.6) | copy-start | bytes 1540
  7.1 18.4 %all-to-all-start = ((bf16[8,16,16,128]{3,2,1,0:T(8,128)(2,1)}), bf16[8,16,16,128]{3,2,1,0:T(8,128)(2,1)S(1)}, u32[]{:S(2)}, u32[]{:S(2)}) async-start(bf16[8,16,16,128]{3,2,1,0:T(8,128)(2,1)} %bitcast.5), calls=%async_computation | async-start | bytes 1048576 | tf_op jit(solution)/shard_map/all_to_all | solution.py:399
  25.6 0.8 copy-start.8
  29.5 4.3 %copy-start.9 = (bf16[8,16,16,128]{3,2,1,0:T(8,128)(2,1)S(1)}, bf16[8,16,16,128]{3,2,1,0:T(8,128)(2,1)}, u32[]{:S(2)}) copy-start(bf16[8,16,16,128]{3,2,1,0:T(8,128)(2,1)} %copy-done.8) | copy-start | bytes 1572868
  29.5 33.7 %all-to-all-start.1 = ((bf16[8,32,16,128]{3,2,1,0:T(8,128)(2,1)}), bf16[8,32,16,128]{3,2,1,0:T(8,128)(2,1)S(1)}, u32[]{:S(2)}, u32[]{:S(2)}) async-start(bf16[8,32,16,128]{3,2,1,0:T(8,128)(2,1)} %harmonic.3), calls=%async_computation.1 | async-start | bytes 2097152 | tf_op jit(solution)/shard_map/all_to_all | solution.py:404
  33.9 25.4 %collective-permute-start = (bf16[8,16,16,128]{3,2,1,0:T(8,128)(2,1)S(1)}, bf16[8,16,16,128]{3,2,1,0:T(8,128)(2,1)S(1)}, u32[]{:S(2)}, u32[]{:S(2)}) collective-permute-start(bf16[8,16,16,128]{3,2,1,0:T(8,128)(2,1)S(1)} %copy-done.9), channel_id=1, source_target_pairs={{0,8},{8,0},{16,24},{24,16},{1,9},{9,1},{17,25},{25,17},{2,10},{10... | collective-permute-start | bytes 1572872 | tf_op jit(solution)/shard_map/ppermute | solution.py:401
  35.5 31.6 %collective-permute-start.1 = (bf16[8,16,16,128]{3,2,1,0:T(8,128)(2,1)S(1)}, bf16[8,16,16,128]{3,2,1,0:T(8,128)(2,1)S(1)}, u32[]{:S(2)}, u32[]{:S(2)}) collective-permute-start(bf16[8,16,16,128]{3,2,1,0:T(8,128)(2,1)S(1)} %copy-done.9), channel_id=1, source_target_pairs={{0,16},{8,24},{16,0},{24,8},{1,17},{9,25},{17,1},{25,9},{2,18},{10... | collective-permute-start | bytes 1572872 | tf_op jit(solution)/shard_map/ppermute | solution.py:401
  59.3 0.8 copy-start.12
  63.3 24.1 %copy-start.1 = (bf16[8,32,16,128]{3,2,1,0:T(8,128)(2,1)}, bf16[8,32,16,128]{3,2,1,0:T(8,128)(2,1)S(1)}, u32[]{:S(2)}) copy-start(bf16[8,32,16,128]{3,2,1,0:T(8,128)(2,1)S(1)} %all-to-all-done.1.refs_0_) | copy-start | bytes 3145732
  63.3 24.1 %all-to-all-start.2 = ((bf16[8,32,16,128]{3,2,1,0:T(8,128)(2,1)}), bf16[8,32,16,128]{3,2,1,0:T(8,128)(2,1)S(1)}, u32[]{:S(2)}, u32[]{:S(2)}) async-start(bf16[8,32,16,128]{3,2,1,0:T(8,128)(2,1)} %harmonic.4), calls=%async_computation.2 | async-start | bytes 2097152 | tf_op jit(solution)/shard_map/all_to_all | solution.py:404
  67.1 14.4 %copy-start.11 = (bf16[8,16,16,128]{3,2,1,0:T(8,128)(2,1)}, bf16[8,16,16,128]{3,2,1,0:T(8,128)(2,1)S(1)}, u32[]{:S(2)}) copy-start(bf16[8,16,16,128]{3,2,1,0:T(8,128)(2,1)S(1)} %collective-permute-done.1.refs_0_) | copy-start | bytes 1572868
  67.1 14.4 %collective-permute-start.2 = (bf16[8,16,16,128]{3,2,1,0:T(8,128)(2,1)S(1)}, bf16[8,16,16,128]{3,2,1,0:T(8,128)(2,1)S(1)}, u32[]{:S(2)}, u32[]{:S(2)}) collective-permute-start(bf16[8,16,16,128]{3,2,1,0:T(8,128)(2,1)S(1)} %collective-permute-done.1.refs_0_), channel_id=1, source_target_pairs={{0,8},{8,0},{16,24},{24,16},{1,9},{9,1},{17,25},{25,17},{2,10},{10... | collective-permute-start | bytes 1572872 | tf_op jit(solution)/shard_map/ppermute | solution.py:401
  81.5 0.8 copy-start.13
  87.4 1.0 copy-start.2
  88.4 30.5 %all-to-all-start.3 = ((bf16[8,32,16,256]{3,2,1,0:T(8,128)(2,1)}), bf16[8,32,16,256]{3,2,1,0:T(8,128)(2,1)S(1)}, u32[]{:S(2)}, u32[]{:S(2)}) async-start(bf16[8,32,16,256]{3,2,1,0:T(8,128)(2,1)} %harmonic.5), calls=%async_computation.3 | async-start | bytes 4194304 | tf_op jit(solution)/shard_map/all_to_all | solution.py:404
  118.9 1.3 copy-start
  128.3 30.2 %all-to-all-start.5 = ((bf16[8,16,32,256]{3,2,1,0:T(8,128)(2,1)}), bf16[8,16,32,256]{3,2,1,0:T(8,128)(2,1)S(1)}, u32[]{:S(2)}, u32[]{:S(2)}) async-start(bf16[8,16,32,256]{3,2,1,0:T(8,128)(2,1)} %filters.2), calls=%async_computation.5 | async-start | bytes 4194304 | tf_op jit(solution)/shard_map/all_to_all | solution.py:404
  158.5 3.6 %copy-start.4 = (bf16[8,16,32,256]{3,2,1,0:T(8,128)(2,1)}, bf16[8,16,32,256]{3,2,1,0:T(8,128)(2,1)S(1)}, u32[]{:S(2)}) copy-start(bf16[8,16,32,256]{3,2,1,0:T(8,128)(2,1)S(1)} %all-to-all-done.5.filtered_ref) | copy-start | bytes 6291460
  158.5 18.9 %all-to-all-start.6 = ((bf16[8,16,32,128]{3,2,1,0:T(8,128)(2,1)}), bf16[8,16,32,128]{3,2,1,0:T(8,128)(2,1)S(1)}, u32[]{:S(2)}, u32[]{:S(2)}) async-start(bf16[8,16,32,128]{3,2,1,0:T(8,128)(2,1)} %get-tuple-element.38), calls=%async_computation.6 | async-start | bytes 2097152 | tf_op jit(solution)/shard_map/all_to_all | solution.py:404
  165.5 18.9 %collective-permute-start.3 = (bf16[8,16,16,128]{3,2,1,0:T(8,128)(2,1)}, bf16[8,16,16,128]{3,2,1,0:T(8,128)(2,1)S(1)}, u32[]{:S(2)}, u32[]{:S(2)}) collective-permute-start(bf16[8,16,16,128]{3,2,1,0:T(8,128)(2,1)} %get-tuple-element.37), channel_id=1, source_target_pairs={{0,8},{8,0},{16,24},{24,16},{1,9},{9,1},{17,25},{25,17},{2,10},{10... | collective-permute-start | bytes 1572872 | tf_op jit(solution)/shard_map/ppermute | solution.py:401
  177.4 3.7 %copy-start.6 = (bf16[8,16,32,128]{3,2,1,0:T(8,128)(2,1)}, bf16[8,16,32,128]{3,2,1,0:T(8,128)(2,1)S(1)}, u32[]{:S(2)}) copy-start(bf16[8,16,32,128]{3,2,1,0:T(8,128)(2,1)S(1)} %all-to-all-done.6.filtered_ref) | copy-start | bytes 3145732
  177.4 18.9 %all-to-all-start.4 = ((bf16[8,16,32,128]{3,2,1,0:T(8,128)(2,1)}), bf16[8,16,32,128]{3,2,1,0:T(8,128)(2,1)S(1)}, u32[]{:S(2)}, u32[]{:S(2)}) async-start(bf16[8,16,32,128]{3,2,1,0:T(8,128)(2,1)} %get-tuple-element.34), calls=%async_computation.4 | async-start | bytes 2097152 | tf_op jit(solution)/shard_map/all_to_all | solution.py:404
  181.2 3.1 %copy-start.7 = (bf16[8,16,16,128]{3,2,1,0:T(8,128)(2,1)S(1)}, bf16[8,16,16,128]{3,2,1,0:T(8,128)(2,1)}, u32[]{:S(2)}) copy-start(bf16[8,16,16,128]{3,2,1,0:T(8,128)(2,1)} %get-tuple-element.36) | copy-start | bytes 1572868
  184.0 25.2 %collective-permute-start.5 = (bf16[8,16,16,128]{3,2,1,0:T(8,128)(2,1)}, bf16[8,16,16,128]{3,2,1,0:T(8,128)(2,1)S(1)}, u32[]{:S(2)}, u32[]{:S(2)}) collective-permute-start(bf16[8,16,16,128]{3,2,1,0:T(8,128)(2,1)} %cycles.5), channel_id=1, source_target_pairs={{0,8},{8,0},{16,24},{24,16},{1,9},{9,1},{17,25},{25,17},{2,10},{10... | collective-permute-start | bytes 1572872 | tf_op jit(solution)/shard_map/ppermute | solution.py:401
  184.5 26.1 %collective-permute-start.4 = (bf16[8,16,16,128]{3,2,1,0:T(8,128)(2,1)S(1)}, bf16[8,16,16,128]{3,2,1,0:T(8,128)(2,1)S(1)}, u32[]{:S(2)}, u32[]{:S(2)}) collective-permute-start(bf16[8,16,16,128]{3,2,1,0:T(8,128)(2,1)S(1)} %add_convert_fusion.1), channel_id=1, source_target_pairs={{0,16},{8,24},{16,0},{24,8},{1,17},{9,25},{17,1},{25,9},{2,18},{10... | collective-permute-start | bytes 1572872 | tf_op jit(solution)/shard_map/ppermute | solution.py:401
  196.3 1.0 copy-start.5
  212.6 13.6 %all-to-all-start.7 = ((bf16[8,16,16,128]{3,2,1,0:T(8,128)(2,1)}), bf16[8,16,16,128]{3,2,1,0:T(8,128)(2,1)S(1)}, u32[]{:S(2)}, u32[]{:S(2)}) async-start(bf16[8,16,16,128]{3,2,1,0:T(8,128)(2,1)} %add_convert_fusion), calls=%async_computation.7 | async-start | bytes 1048576 | tf_op jit(solution)/shard_map/all_to_all | solution.py:440
  226.3 0.8 copy-start.3

commit v3 on v2

v3 whole, which is shorter than its diff:
```python
import functools
import math

import jax
import jax.numpy as jnp
from jax import lax
from jax.experimental import pallas as pl
from jax.experimental.pallas import tpu as pltpu
from jax.sharding import PartitionSpec as P

BAND = 0.38
VMEM_LIMIT = 56 * 1024 * 1024
F32 = jnp.float32
BF16 = jnp.bfloat16
COST = pl.CostEstimate(flops=2_000_000_000, bytes_accessed=12_000_000, transcendentals=0)


def params(**kw):
    return pltpu.CompilerParams(vmem_limit_bytes=VMEM_LIMIT, **kw)


def polar_angle_values(cycle_total):
    position = (jnp.arange(cycle_total, dtype=F32) + 0.5) / cycle_total
    return 0.5 * math.pi + BAND * (2.0 * position - 1.0)


def divisor(n, most):
    return max(d for d in range(1, most + 1) if n % d == 0)


def lane_blocks(width):
    return -(-width // 128)


def put(ref, rows, value):
    width = value.shape[1]
    for h in range(ref.shape[0]):
        piece = value[:, h * 128 : min((h + 1) * 128, width)]
        if piece.shape[1] < 128:
            piece = jnp.concatenate([piece, jnp.zeros((piece.shape[0], 128 - piece.shape[1]), piece.dtype)], axis=1)
        ref[h, rows, :] = piece


def get(ref, rows, width):
    value = jnp.concatenate([ref[h, rows, :] for h in range(ref.shape[0])], axis=1)
    return value if width == value.shape[1] else value[:, :width]


def analysis_kernel(steps, factor_ref, modes_ref, sky_ref, out_ref, phase_ref, prod_ref, turn_ref):
    step = pl.program_id(0)
    chans, cycles, pixels = sky_ref.shape
    modes = modes_ref.shape[1]
    low = 64
    high = pixels // low

    @pl.when(step == 0)
    def _():
        ids = modes_ref[...]
        unit = 2.0 * math.pi / pixels

        def table(rows, stride):
            index = lax.broadcasted_iota(jnp.int32, (rows, modes), 0) * stride
            angle = unit * ((index * ids) & (pixels - 1)).astype(F32)
            return jnp.cos(angle), jnp.sin(angle)

        cos_low, sin_low = table(low, 1)
        cos_high, sin_high = table(high, low)
        for h in range(high):
            ca, sa = cos_high[h : h + 1], sin_high[h : h + 1]
            rows = slice(h * low, (h + 1) * low)
            phase_ref[rows, :modes] = (ca * cos_low - sa * sin_low).astype(BF16)
            phase_ref[rows, modes:] = (-(sa * cos_low + ca * sin_low)).astype(BF16)

    rows = chans * cycles
    product = jnp.dot(sky_ref[...].reshape(rows, pixels), phase_ref[...], preferred_element_type=F32)
    put(prod_ref, pl.ds(pl.multiple_of(step * rows, rows), rows), product)

    @pl.when(step == steps - 1)
    def _():
        total = chans * steps
        for r in range(cycles):
            part = get(prod_ref, pl.ds(r, total, stride=cycles), 2 * modes) * factor_ref[r]
            both = [part[:, k * modes : (k + 1) * modes].T for k in range(2)]
            put(turn_ref, pl.ds(r, modes, stride=cycles), jnp.concatenate(both, axis=1))
        out_ref[...] = get(turn_ref, slice(None), 2 * total).astype(BF16).reshape(out_ref.shape)


def analysis(sky, factor, modes):
    chans, cycles, pixels = sky.shape
    count = modes.shape[0]
    steps = divisor(chans, 2)
    return pl.pallas_call(
        functools.partial(analysis_kernel, steps),
        grid=(steps,),
        in_specs=[
            pl.BlockSpec(memory_space=pltpu.SMEM),
            pl.BlockSpec((1, count), lambda i: (0, 0)),
            pl.BlockSpec((chans // steps, cycles, pixels), lambda i: (i, 0, 0)),
        ],
        out_specs=pl.BlockSpec((count, cycles, 2 * chans), lambda i: (0, 0, 0)),
        out_shape=jax.ShapeDtypeStruct((count, cycles, 2 * chans), BF16),
        scratch_shapes=[
            pltpu.VMEM((pixels, 2 * count), BF16),
            pltpu.VMEM((lane_blocks(2 * count), chans * cycles, 128), F32),
            pltpu.VMEM((lane_blocks(2 * chans), count * cycles, 128), F32),
        ],
        compiler_params=params(),
        name="analysis",
    )(factor, modes.reshape(1, count), sky)


def legendre_kernel(levels, first_ref, degree_ref, band_ref, log_ref, lat_ref, turned_ref, gain_ref, all_ref, pick_ref):
    modes, slots, cycles = lat_ref.shape
    block = 128
    row = lax.broadcasted_iota(jnp.int32, (modes, 1), 0)
    order = jnp.zeros((modes, 1), F32)
    log_seed = jnp.zeros((modes, 1), F32)
    for j in range(modes):
        order = jnp.where(row == j, band_ref[first_ref[0] + j].astype(F32), order)
        log_seed = jnp.where(row == j, log_ref[first_ref[0] + j], log_seed)
    level = lax.broadcasted_iota(jnp.int32, (modes, levels), 1).astype(F32)
    squared = order * order

    def growth(n):
        return jnp.sqrt(jnp.maximum(4.0 * n * n - 1.0, 1.0) / jnp.maximum(n * n - squared, 1.0))

    here = growth(level)
    gain_ref[0] = here
    gain_ref[1] = here / growth(level - 1.0)
    position = (lax.broadcasted_iota(jnp.int32, (1, cycles), 1).astype(F32) + 0.5) / cycles
    colatitude = 0.5 * math.pi + BAND * (2.0 * position - 1.0)
    cosine = jnp.broadcast_to(jnp.cos(colatitude), (modes, cycles))
    orders = jnp.broadcast_to(order, (modes, cycles))
    seed = jnp.exp(log_seed + order * jnp.log(jnp.sin(colatitude)))

    def advance(i, carry):
        latest, earlier = carry
        start = pl.multiple_of(i * block, block)
        first = gain_ref[0, :, pl.ds(start, block)]
        second = gain_ref[1, :, pl.ds(start, block)]
        base = (i * block).astype(F32)
        for n in range(block):
            up = jnp.broadcast_to(first[:, n : n + 1], (modes, cycles)) * cosine
            down = jnp.broadcast_to(second[:, n : n + 1], (modes, cycles))
            begin = jnp.where(orders == base + n, seed, 0.0)
            current = up * latest + (begin - down * earlier)
            put(all_ref, pl.ds(pl.multiple_of((start + n) * modes, modes), modes), current)
            latest, earlier = current, latest
        return latest, earlier

    zero = jnp.zeros((modes, cycles), F32)
    lax.fori_loop(0, levels // block, advance, (zero, zero))

    def pick(s, _):
        source = pl.multiple_of(degree_ref[first_ref[1] + s] * modes, modes)
        for h in range(all_ref.shape[0]):
            pick_ref[h, pl.ds(pl.multiple_of(s * modes, modes), modes), :] = all_ref[h, pl.ds(source, modes), :]
        return 0

    lax.fori_loop(0, slots, pick, 0, unroll=8)
    for j in range(modes):
        rows = get(pick_ref, pl.ds(j, slots, stride=modes), cycles)
        lat_ref[j] = rows.astype(BF16)
        turned_ref[j] = rows.T.astype(BF16)


def legendre(first, degrees, band, modes, slots, cycles):
    levels = degrees.shape[0]
    m = band.astype(F32)
    log_seed = 0.5 * (
        jnp.log(m + 0.5) + lax.lgamma(m + 0.5) - lax.lgamma(m + 1.0) - 0.5 * math.log(math.pi)
    )
    vmem = pl.BlockSpec(memory_space=pltpu.VMEM)
    return pl.pallas_call(
        functools.partial(legendre_kernel, levels),
        in_specs=[pl.BlockSpec(memory_space=pltpu.SMEM)] * 4,
        out_specs=[vmem, vmem],
        out_shape=[
            jax.ShapeDtypeStruct((modes, slots, cycles), BF16),
            jax.ShapeDtypeStruct((modes, cycles, slots), BF16),
        ],
        scratch_shapes=[
            pltpu.VMEM((2, modes, levels), F32),
            pltpu.VMEM((lane_blocks(cycles), levels * modes, 128), F32),
            pltpu.VMEM((lane_blocks(cycles), slots * modes, 128), F32),
        ],
        compiler_params=params(),
        cost_estimate=pl.CostEstimate(flops=40_000_000, bytes_accessed=30_000_000, transcendentals=0),
        name="legendre",
    )(first, degrees, band, log_seed)


def arrange(pieces, low):
    placed = []
    for p in range(len(pieces)):
        value = pieces[p]
        for q in range(1, len(pieces)):
            value = lax.select(low == q, pieces[p ^ q], value)
        placed.append(value)
    return placed


def by_part(placed, chans):
    return [jnp.concatenate([p[:, k * chans : (k + 1) * chans] for p in placed], axis=1) for k in range(2)]


def harmonic_kernel(counts, family, low_ref, lat_ref, *refs):
    spectra, out_ref, turn_ref = refs[: sum(counts)], *refs[sum(counts) :]
    _, modes, cycles, pair = spectra[0].shape
    slots = out_ref.shape[0] * out_ref.shape[1]
    width = out_ref.shape[3]
    for j in range(modes):
        rights = []
        first = 0
        for count in counts:
            pieces = [p[:, j].reshape(p.shape[0] * cycles, pair) for p in spectra[first : first + count]]
            rights.append(pieces[0] if count == 1 else jnp.concatenate(pieces, axis=0))
            first += count
        if family:
            rights = by_part(arrange(rights, low_ref[0]), pair // 2)
        right = rights[0] if len(rights) == 1 else jnp.concatenate(rights, axis=1)
        result = jnp.dot(lat_ref[j], right, preferred_element_type=F32)
        put(turn_ref, pl.ds(j, slots, stride=modes), result)
    out_ref[...] = get(turn_ref, slice(None), width).astype(BF16).reshape(out_ref.shape)


def harmonic(low, lat, spectra, slot_dev, family):
    modes, slots, cycle_total = lat.shape
    _, _, cycles, pair = spectra[0][0].shape
    counts = [len(pieces) for pieces in spectra]
    pieces = sum(spectra, [])
    width = len(spectra) * pair
    dests = slots // slot_dev
    steps = divisor(dests, 2)
    return pl.pallas_call(
        functools.partial(harmonic_kernel, counts, family),
        grid=(steps,),
        in_specs=[
            pl.BlockSpec(memory_space=pltpu.SMEM),
            pl.BlockSpec((modes, slots // steps, cycle_total), lambda i: (0, i, 0)),
        ]
        + [pl.BlockSpec(p.shape, lambda i: (0, 0, 0, 0)) for p in pieces],
        out_specs=pl.BlockSpec((dests // steps, slot_dev, modes, width), lambda i: (i, 0, 0, 0)),
        out_shape=jax.ShapeDtypeStruct((dests, slot_dev, modes, width), BF16),
        scratch_shapes=[pltpu.VMEM((lane_blocks(width), slots // steps * modes, 128), F32)],
        compiler_params=params(),
        cost_estimate=COST,
        name="harmonic",
    )(low, lat, *pieces)


def filter_kernel(counts, wanted, low_ref, filters_ref, *refs):
    inputs, outs, turn_ref = refs[: len(counts)], refs[len(counts) : -1], refs[-1]
    groups, slots, modes, _ = inputs[0].shape
    pair = inputs[0].shape[3] // counts[0]
    chans = pair // 2
    rows = groups * modes
    total = filters_ref.shape[2]
    low, high = low_ref[0], low_ref[1]
    families = total // chans // sum(counts[:2]) if len(counts) > 1 else 1
    width = total // families
    own = pl.multiple_of(high * width, width)
    other = pl.multiple_of((1 - high) * width, width)
    for s in range(slots):
        pieces = []
        for ref, count in zip(inputs[:2], counts):
            pieces += [ref[:, s, :, i * pair : (i + 1) * pair].reshape(rows, pair) for i in range(count)]
        left = jnp.concatenate(by_part(arrange(pieces, low), chans), axis=0)
        if families > 1:
            far = [inputs[2][:, s, :, k * width : (k + 1) * width].reshape(rows, width) for k in range(2)]
            left = jnp.concatenate([left, jnp.concatenate(far, axis=0)], axis=1)
        lane = 0
        for family, hops in wanted:
            if family:
                start, count = other, width
            else:
                start, count = pl.multiple_of(own + (low ^ hops) * chans, chans), chans
            right = filters_ref[s, pl.ds(start, count), pl.ds(own, width)]
            if families > 1:
                right = jnp.concatenate([right, filters_ref[s, pl.ds(start, count), pl.ds(other, width)]], axis=1)
            result = lax.dot_general(left, right, (((1,), (1,)), ((), ())), preferred_element_type=F32)
            result = jnp.concatenate([result[:rows], result[rows:]], axis=1)
            blocks = lane_blocks(2 * count)
            put(turn_ref.at[lane : lane + blocks], pl.ds(s, rows, stride=slots), result)
            lane += blocks
    lane = 0
    for (family, hops), ref in zip(wanted, outs):
        blocks = lane_blocks(ref.shape[3])
        value = get(turn_ref.at[lane : lane + blocks], slice(None), ref.shape[3])
        ref[...] = value.astype(BF16).reshape(ref.shape)
        lane += blocks


def apply_filters(place, filters, coeffs, counts, wanted):
    groups, slots, modes, _ = coeffs[0].shape
    total = filters.shape[2]
    pair = coeffs[0].shape[3] // counts[0]
    step = min(slots, 16)
    widths = [counts[-1] * pair if family else pair for family, _ in wanted]
    return pl.pallas_call(
        functools.partial(filter_kernel, counts, wanted),
        grid=(slots // step,),
        in_specs=[
            pl.BlockSpec(memory_space=pltpu.SMEM),
            pl.BlockSpec((step, total, total), lambda i: (i, 0, 0)),
        ]
        + [pl.BlockSpec((groups, step, modes, c.shape[3]), lambda i: (0, i, 0, 0)) for c in coeffs],
        out_specs=[pl.BlockSpec((groups, modes, step, w), lambda i: (0, 0, i, 0)) for w in widths],
        out_shape=[jax.ShapeDtypeStruct((groups, modes, slots, w), BF16) for w in widths],
        scratch_shapes=[pltpu.VMEM((sum(lane_blocks(w) for w in widths), groups * modes * step, 128), F32)],
        compiler_params=params(),
        cost_estimate=COST,
        name="filters",
    )(place, filters, *coeffs)


def cycles_kernel(scale, low_ref, turned_ref, filtered_ref, *outs):
    groups, modes, slot_dev, width = filtered_ref.shape
    blocks, _, cycles, pair = outs[0].shape
    chans = pair // 2
    parts = len(outs)
    for j in range(modes):
        result = jnp.dot(
            turned_ref[j],
            filtered_ref[:, j].reshape(groups * slot_dev, width),
            preferred_element_type=F32,
        )
        result = result * scale
        if parts == 1:
            pieces = [result]
        else:
            half = width // 2
            pieces = [
                jnp.concatenate([result[:, k * half + p * chans : k * half + (p + 1) * chans] for k in range(2)], axis=1)
                for p in range(parts)
            ]
            pieces = arrange(pieces, low_ref[0])
        for piece, ref in zip(pieces, outs):
            ref[:, j] = piece.astype(BF16).reshape(blocks, cycles, pair)


def to_cycles(low, turned, filtered, scale, blocks, parts):
    modes, cycle_total, slots = turned.shape
    width = filtered.shape[3]
    vmem = pl.BlockSpec(memory_space=pltpu.VMEM)
    shape = (blocks, modes, cycle_total // blocks, width // parts)
    return pl.pallas_call(
        functools.partial(cycles_kernel, scale),
        in_specs=[pl.BlockSpec(memory_space=pltpu.SMEM), vmem, vmem],
        out_specs=[vmem] * parts,
        out_shape=[jax.ShapeDtypeStruct(shape, BF16)] * parts,
        compiler_params=params(),
        cost_estimate=COST,
        name="cycles",
    )(low, turned, filtered)


def synthesis_kernel(modes_ref, parts_ref, out_ref, there_ref, phase_ref, wide_ref, turn_ref, left_ref, sent):
    chans, cycles, pixels = there_ref.shape
    steps = sent.shape[0]
    modes, _, pair = parts_ref.shape
    low = 128
    total = pair // 2
    ids = modes_ref[...]
    unit = 2.0 * math.pi / pixels

    def table(columns, stride):
        index = lax.broadcasted_iota(jnp.int32, (modes, columns), 1) * stride
        angle = unit * ((index * ids) & (pixels - 1)).astype(F32)
        return jnp.cos(angle), jnp.sin(angle)

    cos_low, sin_low = table(low, 1)
    cos_high, sin_high = table(pixels // low, low)
    for h in range(pixels // low):
        ca, sa = cos_high[:, h : h + 1], sin_high[:, h : h + 1]
        columns = slice(h * low, (h + 1) * low)
        phase_ref[:modes, columns] = (ca * cos_low - sa * sin_low).astype(BF16)
        phase_ref[modes:, columns] = (-(sa * cos_low + ca * sin_low)).astype(BF16)
    put(wide_ref, slice(None), parts_ref[...].astype(F32).reshape(modes * cycles, pair))
    for r in range(cycles):
        part = get(wide_ref, pl.ds(r, modes, stride=cycles), pair)
        both = [part[:, k * total : (k + 1) * total].T for k in range(2)]
        put(turn_ref, pl.ds(r, total, stride=cycles), jnp.concatenate(both, axis=1))
    left_ref[...] = get(turn_ref, slice(None), 2 * modes).astype(BF16)

    part = chans // steps
    rows = part * cycles
    copies = []
    for i in range(steps):
        left = left_ref[i * rows : (i + 1) * rows, :]
        result = jnp.dot(left, phase_ref[...], preferred_element_type=F32) * (1.0 / math.sqrt(modes))
        there_ref[i * part : (i + 1) * part] = result.astype(BF16).reshape(part, cycles, pixels)
        window = pl.ds(i * part, part)
        copies.append(pltpu.make_async_copy(there_ref.at[window], out_ref.at[window], sent.at[i]))
        copies[i].start()
    for copy in copies:
        copy.wait()


def synthesis(parts, modes, pixels):
    count, cycles, pair = parts.shape
    chans = pair // 2
    steps = divisor(chans, 8)
    vmem = pl.BlockSpec(memory_space=pltpu.VMEM)
    return pl.pallas_call(
        synthesis_kernel,
        in_specs=[vmem, vmem],
        out_specs=pl.BlockSpec(memory_space=pl.ANY),
        out_shape=jax.ShapeDtypeStruct((chans, cycles, pixels), BF16),
        scratch_shapes=[
            pltpu.VMEM((chans, cycles, pixels), BF16),
            pltpu.VMEM((2 * count, pixels), BF16),
            pltpu.VMEM((lane_blocks(pair), count * cycles, 128), F32),
            pltpu.VMEM((lane_blocks(2 * count), chans * cycles, 128), F32),
            pltpu.VMEM((chans * cycles, 2 * count), BF16),
            pltpu.SemaphoreType.DMA((steps,)),
        ],
        compiler_params=params(),
        name="synthesis",
    )(modes.reshape(count, 1), parts)


def body(sky_maps, filters, band_order_values, slot_degree_values):
    chans, cycle_dev, pixels = sky_maps.shape
    chan_groups = lax.axis_size("chan")
    blk_groups = lax.axis_size("blk")
    chan, blk = lax.axis_index("chan"), lax.axis_index("blk")
    slot_dev = filters.shape[0]
    degree_count = slot_degree_values.shape[0]
    mode_dev = band_order_values.shape[0] // blk_groups
    cycle_total = cycle_dev * blk_groups
    group_slots = slot_dev * blk_groups
    colatitude = polar_angle_values(cycle_total)
    cycle_factor = (
        2.0 * math.sqrt(2.0 * BAND / cycle_total) * jnp.sin(colatitude) * (1.0 / math.sqrt(pixels))
    )
    local_factor = lax.dynamic_slice_in_dim(cycle_factor, blk * cycle_dev, cycle_dev)
    spectra = analysis(sky_maps, local_factor, band_order_values)
    spectra = spectra.reshape(blk_groups, mode_dev, cycle_dev, 2 * chans)
    def swap(value, t):
        return lax.ppermute(value, "chan", [(i, i ^ t) for i in range(chan_groups)])

    def exchange(value):
        return lax.all_to_all(value, "blk", split_axis=0, concat_axis=0, tiled=True)

    near = max(1, chan_groups // 2)
    hops = [[0], list(range(1, near)), list(range(near, chan_groups))]
    hops = [h for h in hops if h]
    counts = [len(h) for h in hops]
    place = jnp.stack([chan % near, chan // near])
    first = jnp.stack([blk * mode_dev, chan * group_slots])
    lat, turned = legendre(first, slot_degree_values, band_order_values, mode_dev, group_slots, cycle_total)
    own = exchange(spectra)
    gathered = [[own]]
    half = max(1, blk_groups * 4 // 8)
    if chan_groups > 1:
        beside = swap(spectra, 1)
        beside, lat, own = lax.optimization_barrier((beside, lat, own))
        beside = exchange(beside)
        gathered = [[own], [beside]]
    for t in range(2, chan_groups):
        top = 1 << (t.bit_length() - 1)
        source = [own[:half], own[half:]] if t == top else gathered[top]
        gathered.append([swap(piece, t if t == top else t ^ top) for piece in source])
    coeffs = []
    for n, part in enumerate(hops):
        result = harmonic(place, lat, [gathered[t] for t in part], slot_dev, n == 2)
        if n == 0 and chan_groups > 1:
            result, gathered[1][0] = lax.optimization_barrier((result, gathered[1][0]))
            if chan_groups > 2:
                result, gathered[2][0] = lax.optimization_barrier((result, gathered[2][0]))
        if n == 1:
            result, coeffs[0] = lax.optimization_barrier((result, coeffs[0]))
            if chan_groups > 2:
                result, gathered[2][1], gathered[3][0] = lax.optimization_barrier((result, gathered[2][1], gathered[3][0]))
        if n == 2:
            result, coeffs[1] = lax.optimization_barrier((result, coeffs[1]))
        lat, result = lax.optimization_barrier((lat, result))
        coeffs.append(exchange(result))
    scale = 2.0 / math.sqrt(degree_count)
    partial = {}
    tasks = [[(False, t)] for part in hops[:2] for t in part][::-1]
    if len(hops) == 3:
        tasks = [[(True, None)]] + [sum(tasks, [])]
    else:
        tasks = [sum(tasks, [])]
    for n, task in enumerate(tasks):
        results = list(apply_filters(place, filters, coeffs, counts, task))
        place, results[0] = lax.optimization_barrier((place, results[0]))
        for (family, t), filtered in zip(task, results):
            names = hops[2] if family else [t]
            outs = to_cycles(place, turned, exchange(filtered), scale, blk_groups, len(names))
            partial.update(zip(names, outs))
    total = partial[0].astype(F32)
    top = chan_groups // 2
    while top:
        group = partial[top].astype(F32)
        for t in range(top + 1, 2 * top):
            group = group + swap(partial[t], t ^ top).astype(F32)
        total = total + swap(group.astype(BF16), top).astype(F32)
        top //= 2
    cycle_part = total.astype(BF16)
    by_cycle = lax.all_to_all(cycle_part, "blk", split_axis=0, concat_axis=0, tiled=True)
    by_cycle = by_cycle.reshape(blk_groups * mode_dev, cycle_dev, 2 * chans)
    return synthesis(by_cycle, band_order_values, pixels)


def solution(mesh):
    in_specs = (P("chan", "blk", None), P(("chan", "blk"), None, None), P(), P())
    out_specs = P("chan", "blk", None)
    return jax.shard_map(body, mesh=mesh, in_specs=in_specs, out_specs=out_specs, check_vma=False)
```

time: 235 us -> 224 us (0.953)
  waiting for transfers between devices: 120 us -> 87.7 us
  blocking collectives: 0 us -> 30.9 us
  local copies, waits for them, and re-layouts: 9.81 us -> 3.91 us
  Pallas kernels: 59.4 us -> 54.3 us
  starting transfers between devices: 39.7 us -> 42.1 us
    all_to_all x0 -> x1, blocking collectives: none -> 30.9 us  [exchange(): return lax.all_to_all(value, 'blk', split_axis=0, concat_axis=0, tiled=True)]
    ppermute x6 -> x8, waiting for transfers between devices: 46.1 us -> 24.6 us  [swap(): return lax.ppermute(value, 'chan', [(i, i ^ t) for i in range(chan_groups)])]
    all_to_all x6 -> x7, waiting for transfers between devices: 65.4 us -> 54.1 us  [exchange(): return lax.all_to_all(value, 'blk', split_axis=0, concat_axis=0, tiled=True)]
    all_to_all x1 -> x0, starting transfers between devices: 5.17 us -> none  [body(): lax.all_to_all(spectra, 'blk', split_axis=0, concat_axis=0, tiled=True)]
    pallas_call x9, Pallas kernels: 43.1 us -> 38.6 us  [the longest x2 12.9 us: apply_filters(): pl.pallas_call(functools.partial(filter_kernel, counts, wanted), grid=(sl...]
    ppermute x6 -> x8, starting transfers between devices: 7.74 us -> 11.7 us  [swap(): return lax.ppermute(value, 'chan', [(i, i ^ t) for i in range(chan_groups)])]
    unnamed x28 -> x30, local copies, waits for them, and re-layouts: 6.45 us -> 2.51 us
    all_to_all x6 -> x7, starting transfers between devices: 22.9 us -> 26.5 us  [exchange(): return lax.all_to_all(value, 'blk', split_axis=0, concat_axis=0, tiled=True)]
  transfers between devices with their start and end apart: 14 -> 16, of which waited for: 9 -> 11; matrix products, arithmetic and copies ran while one was open for 2% -> 1% of each run, Pallas kernels for 15% -> 17%
where the time goes in v3:
time: 224 us; the launch traced here: 223 us
  waiting for transfers between devices  87.7 us (39%)
  Pallas kernels  54.3 us (24%)
  starting transfers between devices  42.1 us (19%)
  blocking collectives  30.9 us (14%)
  other arithmetic  4.18 us (2%)
  local copies, waits for them, and re-layouts  3.91 us (2%)
    all_to_all x7, waiting for transfers between devices, exchange(): return lax.all_to_all(value, 'blk', split_axis=0, concat_axis=0, tiled=True)  54.1 us
    all_to_all x1, blocking collectives, exchange(): return lax.all_to_all(value, 'blk', split_axis=0, concat_axis=0, tiled=True)  30.9 us
    all_to_all x7, starting transfers between devices, exchange(): return lax.all_to_all(value, 'blk', split_axis=0, concat_axis=0, tiled=True)  26.5 us
    ppermute x8, waiting for transfers between devices, swap(): return lax.ppermute(value, 'chan', [(i, i ^ t) for i in range(chan_groups)])  24.6 us
    pallas_call x2, Pallas kernels, apply_filters(): pl.pallas_call(functools.partial(filter_kernel, counts, wanted), grid=(sl...  12.9 us
    ppermute x8, starting transfers between devices, swap(): return lax.ppermute(value, 'chan', [(i, i ^ t) for i in range(chan_groups)])  11.7 us
    pallas_call x3, Pallas kernels, harmonic(): pl.pallas_call(functools.partial(harmonic_kernel, counts, family), grid=(...  10.9 us
    pallas_call x1, Pallas kernels, legendre(): pl.pallas_call(functools.partial(legendre_kernel, levels), in_specs=[pl.B...  9.83 us
  transfers between devices with their start and end apart: 16, of which 11 were waited for; matrix products, arithmetic and copies ran while one was open for 1% of the time, Pallas kernels for 17%

profile of v3, /device:TPU:0, one launch (start us, length us, event | category | flops | bytes accessed | tf_op | source)
XLA Modules:
  0.0 223.3 jit_solution(8482918929402338155)
XLA Ops:
  0.0 0.1 sine_multiply_fusion
  0.1 0.6 dynamic_slice.3.factor_ref
  0.7 5.8 %analysis.1 = bf16[128,16,128]{2,1,0:T(8,128)(2,1)} custom-call(f32[16]{0:T(128)} %dynamic_slice.3.factor_ref, s32[1,128]{1,0:T(1,128)} %bitcast.11, bf16[64,16,2048]{2,1,0:T(8,128)(2,1)} %sky_ref.1), custom_call_target="tpu_custom_call" | custom-call | tf_op jit(solution)/shard_map/analysis/pallas_call | solution.py:92
  6.5 3.0 %collective-permute-start = (bf16[8,16,16,128]{3,2,1,0:T(8,128)(2,1)}, bf16[8,16,16,128]{3,2,1,0:T(8,128)(2,1)}, u32[]{:S(2)}, u32[]{:S(2)}) collective-permute-start(bf16[8,16,16,128]{3,2,1,0:T(8,128)(2,1)} %bitcast.8), channel_id=1, source_target_pairs={{0,8},{8,0},{16,24},{24,16},{1,9},{9,1},{17,25},{25,17},{2,10},{10... | collective-permute-start | bytes 1572872 | tf_op jit(solution)/shard_map/ppermute | solution.py:441
  9.5 3.7 %all-to-all-start = ((bf16[8,16,16,128]{3,2,1,0:T(8,128)(2,1)}), bf16[8,16,16,128]{3,2,1,0:T(8,128)(2,1)S(1)}, u32[]{:S(2)}, u32[]{:S(2)}) async-start(bf16[8,16,16,128]{3,2,1,0:T(8,128)(2,1)} %bitcast.9), calls=%async_computation | async-start | bytes 1048576 | tf_op jit(solution)/shard_map/all_to_all | solution.py:444
  13.3 0.6 pad_add_fusion.1.first_ref
  13.9 0.0 copy-done.9
  13.9 0.7 add_multiply_fusion.log_ref
  14.6 9.8 %legendre.1 = (bf16[16,256,128]{2,1,0:T(8,128)(2,1)}, bf16[16,128,256]{2,1,0:T(8,128)(2,1)}) custom-call(s32[2]{0:T(128)} %pad_add_fusion.1.first_ref, s32[1024]{0:T(1024)} %degree_ref.1, s32[128]{0:T(128)} %band_ref.1, f32[128]{0:T(128)} %add_multiply_fusion.log_ref), custom_call_target="tpu_custom_call" | custom-call | flops 40000000 | bytes 30000000 | tf_op jit(solution)/shard_map/legendre/pallas_call | solution.py:174
  24.4 0.0 all-to-all-done.refs_0_
  24.4 0.0 collective-permute-done
  24.4 4.2 %all-to-all-start.1 = ((bf16[8,16,16,128]{3,2,1,0:T(8,128)(2,1)}), bf16[8,16,16,128]{3,2,1,0:T(8,128)(2,1)S(1)}, u32[]{:S(2)}, u32[]{:S(2)}) async-start(bf16[8,16,16,128]{3,2,1,0:T(8,128)(2,1)} %collective-permute-done), calls=%async_computation.1 | async-start | bytes 1048576 | tf_op jit(solution)/shard_map/all_to_all | solution.py:444
  28.6 2.7 %collective-permute-start.1 = (bf16[4,16,16,128]{3,2,1,0:T(8,128)(2,1)S(1)}, bf16[4,16,16,128]{3,2,1,0:T(8,128)(2,1)S(1)}, u32[]{:S(2)}, u32[]{:S(2)}) collective-permute-start(bf16[4,16,16,128]{3,2,1,0:T(8,128)(2,1)S(1)} %get-tuple-element.64), channel_id=1, source_target_pairs={{0,16},{8,24},{16,0},{24,8},{1,17},{9,25},{17,1},{25,9},{2,18},{10... | collective-permute-start | bytes 786440 | tf_op jit(solution)/shard_map/ppermute | solution.py:441
  31.3 0.6 pad_add_fusion.low_ref
  31.9 0.0 copy-done.4
  32.0 3.2 %harmonic.3 = bf16[8,32,16,128]{3,2,1,0:T(8,128)(2,1)} custom-call(s32[2]{0:T(128)} %pad_add_fusion.low_ref, bf16[16,256,128]{2,1,0:T(8,128)(2,1)} %get-tuple-element.46.lat_ref, bf16[8,16,16,128]{3,2,1,0:T(8,128)(2,1)} %copy-done.4), custom_call_target="tpu_custom_call" | custom-call | flops 2000000000 | bytes 12000000 | tf_op jit(solution)/shard_map/harmonic/pallas_call | solution.py:235
  35.1 3.2 %all-to-all-done.1.refs_0_ = bf16[8,16,16,128]{3,2,1,0:T(8,128)(2,1)S(1)} async-done(((bf16[8,16,16,128]{3,2,1,0:T(8,128)(2,1)}), bf16[8,16,16,128]{3,2,1,0:T(8,128)(2,1)S(1)}, u32[]{:S(2)}, u32[]{:S(2)}) %all-to-all-start.1) | async-done | bytes 524320 | tf_op jit(solution)/shard_map/all_to_all | solution.py:444
  38.4 5.5 %collective-permute-done.1.refs_0_ = bf16[4,16,16,128]{3,2,1,0:T(8,128)(2,1)S(1)} collective-permute-done((bf16[4,16,16,128]{3,2,1,0:T(8,128)(2,1)S(1)}, bf16[4,16,16,128]{3,2,1,0:T(8,128)(2,1)S(1)}, u32[]{:S(2)}, u32[]{:S(2)}) %collective-permute-start.1) | collective-permute-done | bytes 262176 | tf_op jit(solution)/shard_map/ppermute | solution.py:441
  43.8 3.8 %all-to-all-start.2 = ((bf16[8,32,16,128]{3,2,1,0:T(8,128)(2,1)}), bf16[8,32,16,128]{3,2,1,0:T(8,128)(2,1)S(1)}, u32[]{:S(2)}, u32[]{:S(2)}) async-start(bf16[8,32,16,128]{3,2,1,0:T(8,128)(2,1)} %harmonic.3), calls=%async_computation.2 | async-start | bytes 2097152 | tf_op jit(solution)/shard_map/all_to_all | solution.py:444
  47.7 0.0 collective-permute-start.2
  47.7 3.1 %collective-permute-start.3 = (bf16[4,16,16,128]{3,2,1,0:T(8,128)(2,1)S(1)}, bf16[4,16,16,128]{3,2,1,0:T(8,128)(2,1)S(1)}, u32[]{:S(2)}, u32[]{:S(2)}) collective-permute-start(bf16[4,16,16,128]{3,2,1,0:T(8,128)(2,1)S(1)} %collective-permute-done.1.refs_0_), channel_id=1, source_target_pairs={{0,8},{8,0},{16,24},{24,16},{1,9},{9,1},{17,25},{25,17},{2,10},{10... | collective-permute-start | bytes 786440 | tf_op jit(solution)/shard_map/ppermute | solution.py:441
  50.8 0.0 copy-done.8
  50.8 3.2 %harmonic.4 = bf16[8,32,16,128]{3,2,1,0:T(8,128)(2,1)} custom-call(s32[2]{0:T(128)} %pad_add_fusion.low_ref, bf16[16,256,128]{2,1,0:T(8,128)(2,1)} %get-tuple-element.46.lat_ref, bf16[8,16,16,128]{3,2,1,0:T(8,128)(2,1)} %copy-done.8), custom_call_target="tpu_custom_call" | custom-call | flops 2000000000 | bytes 12000000 | tf_op jit(solution)/shard_map/harmonic/pallas_call | solution.py:235
  54.0 0.0 copy-done.11
  54.0 9.1 %all-to-all-done.2.refs_0_ = bf16[8,32,16,128]{3,2,1,0:T(8,128)(2,1)S(1)} async-done(((bf16[8,32,16,128]{3,2,1,0:T(8,128)(2,1)}), bf16[8,32,16,128]{3,2,1,0:T(8,128)(2,1)S(1)}, u32[]{:S(2)}, u32[]{:S(2)}) %all-to-all-start.2) | async-done | bytes 1048608 | tf_op jit(solution)/shard_map/all_to_all | solution.py:444
  63.1 0.0 collective-permute-done.2.refs_1_
  63.1 0.0 collective-permute-done.3.refs_2_
  63.1 3.8 %all-to-all-start.3 = ((bf16[8,32,16,128]{3,2,1,0:T(8,128)(2,1)}), bf16[8,32,16,128]{3,2,1,0:T(8,128)(2,1)S(1)}, u32[]{:S(2)}, u32[]{:S(2)}) async-start(bf16[8,32,16,128]{3,2,1,0:T(8,128)(2,1)} %harmonic.4), calls=%async_computation.3 | async-start | bytes 2097152 | tf_op jit(solution)/shard_map/all_to_all | solution.py:444
  67.0 0.0 collective-permute-start.4
  67.0 8.7 %collective-permute-done.4.refs_3_ = bf16[4,16,16,128]{3,2,1,0:T(8,128)(2,1)S(1)} collective-permute-done((bf16[4,16,16,128]{3,2,1,0:T(8,128)(2,1)S(1)}, bf16[4,16,16,128]{3,2,1,0:T(8,128)(2,1)S(1)}, u32[]{:S(2)}, u32[]{:S(2)}) %collective-permute-start.4) | collective-permute-done | bytes 262176 | tf_op jit(solution)/shard_map/ppermute | solution.py:441
  75.7 0.0 copy-done.12
  75.7 0.0 copy-done.13
  75.7 0.7 copy-done.14
  76.4 4.6 %harmonic.5 = bf16[8,32,16,256]{3,2,1,0:T(8,128)(2,1)} custom-call(s32[2]{0:T(128)} %pad_add_fusion.low_ref, bf16[16,256,128]{2,1,0:T(8,128)(2,1)} %get-tuple-element.46.lat_ref, bf16[4,16,16,128]{3,2,1,0:T(8,128)(2,1)} %copy-done.11, bf16[4,16,16,128]{3,2,1,0:T(8,128)(2,1)} %copy-done.12, bf16[4,16,16,128]{3,2,1,0:T(8,128)(2,1)} %copy-done.13, ...), custom_call_target="tpu_custom_call" | custom-call | flops 2000000000 | bytes 12000000 | tf_op jit(solution)/shard_map/harmonic/pallas_call | solution.py:235
  81.0 0.0 copy-done
  81.0 1.4 all-to-all-done.3.refs_1_
  82.4 30.9 %all_to_all.45.refs_2_ = bf16[8,32,16,256]{3,2,1,0:T(8,128)(2,1)} all-to-all(bf16[8,32,16,256]{3,2,1,0:T(8,128)(2,1)} %harmonic.5), channel_id=1, replica_groups=mesh['chan'=4,'blk'=8] {'blk'}, dimensions={0} | all-to-all | bytes 4194304 | tf_op jit(solution)/shard_map/all_to_all | solution.py:444
  113.3 0.0 copy-done.1
  113.3 5.7 %filters.2 = bf16[8,16,32,256]{3,2,1,0:T(8,128)(2,1)} custom-call(s32[2]{0:T(128)} %pad_add_fusion.low_ref, bf16[32,256,256]{2,1,0:T(8,128)(2,1)} %filters_ref.3, bf16[8,32,16,128]{3,2,1,0:T(8,128)(2,1)} %copy-done, bf16[8,32,16,128]{3,2,1,0:T(8,128)(2,1)} %copy-done.1, bf16[8,32,16,256]{3,2,1,0:T(8,128)(2,1)} %all_to_all.45.refs_2_), custom_call_target="tpu_custom_call" | custom-call | flops 2000000000 | bytes 12000000 | tf_op jit(solution)/shard_map/filters/pallas_call | solution.py:300
  119.0 3.6 %all-to-all-start.6 = ((bf16[8,16,32,256]{3,2,1,0:T(8,128)(2,1)}), bf16[8,16,32,256]{3,2,1,0:T(8,128)(2,1)S(1)}, u32[]{:S(2)}, u32[]{:S(2)}) async-start(bf16[8,16,32,256]{3,2,1,0:T(8,128)(2,1)} %filters.2), calls=%async_computation.6 | async-start | bytes 4194304 | tf_op jit(solution)/shard_map/all_to_all | solution.py:444
  122.6 7.2 %filters.3 = (bf16[8,16,32,128]{3,2,1,0:T(8,128)(2,1)}, bf16[8,16,32,128]{3,2,1,0:T(8,128)(2,1)}) custom-call(s32[2]{0:T(128)} %pad_add_fusion.low_ref, bf16[32,256,256]{2,1,0:T(8,128)(2,1)} %filters_ref.3, bf16[8,32,16,128]{3,2,1,0:T(8,128)(2,1)} %copy-done, bf16[8,32,16,128]{3,2,1,0:T(8,128)(2,1)} %copy-done.1, bf16[8,32,16,256]{3,2,1,0:T(8,128)(2,1)} %all_to_all.45.refs_2_), custom_call_target="tpu_custom_call" | custom-call | flops 2000000000 | bytes 12000000 | tf_op jit(solution)/shard_map/filters/pallas_call | solution.py:300
  129.8 19.4 %all-to-all-done.6.filtered_ref = bf16[8,16,32,256]{3,2,1,0:T(8,128)(2,1)S(1)} async-done(((bf16[8,16,32,256]{3,2,1,0:T(8,128)(2,1)}), bf16[8,16,32,256]{3,2,1,0:T(8,128)(2,1)S(1)}, u32[]{:S(2)}, u32[]{:S(2)}) %all-to-all-start.6) | async-done | bytes 2097184 | tf_op jit(solution)/shard_map/all_to_all | solution.py:444
  149.2 3.6 %all-to-all-start.7 = ((bf16[8,16,32,128]{3,2,1,0:T(8,128)(2,1)}), bf16[8,16,32,128]{3,2,1,0:T(8,128)(2,1)S(1)}, u32[]{:S(2)}, u32[]{:S(2)}) async-start(bf16[8,16,32,128]{3,2,1,0:T(8,128)(2,1)} %get-tuple-element.62), calls=%async_computation.7 | async-start | bytes 2097152 | tf_op jit(solution)/shard_map/all_to_all | solution.py:444
  152.8 0.0 copy-done.3
  152.8 3.6 %cycles.4 = (bf16[8,16,16,128]{3,2,1,0:T(8,128)(2,1)}, bf16[8,16,16,128]{3,2,1,0:T(8,128)(2,1)}) custom-call(s32[2]{0:T(128)} %pad_add_fusion.low_ref, bf16[16,128,256]{2,1,0:T(8,128)(2,1)} %get-tuple-element.57.turned_ref, bf16[8,16,32,256]{3,2,1,0:T(8,128)(2,1)} %copy-done.3), custom_call_target="tpu_custom_call" | custom-call | flops 2000000000 | bytes 12000000 | tf_op jit(solution)/shard_map/cycles/pallas_call | solution.py:347
  156.4 0.0 collective-permute-start.5
  156.4 11.7 %all-to-all-done.7.filtered_ref = bf16[8,16,32,128]{3,2,1,0:T(8,128)(2,1)S(1)} async-done(((bf16[8,16,32,128]{3,2,1,0:T(8,128)(2,1)}), bf16[8,16,32,128]{3,2,1,0:T(8,128)(2,1)S(1)}, u32[]{:S(2)}, u32[]{:S(2)}) %all-to-all-start.7) | async-done | bytes 1048608 | tf_op jit(solution)/shard_map/all_to_all | solution.py:444
  168.1 3.7 %all-to-all-start.5 = ((bf16[8,16,32,128]{3,2,1,0:T(8,128)(2,1)}), bf16[8,16,32,128]{3,2,1,0:T(8,128)(2,1)S(1)}, u32[]{:S(2)}, u32[]{:S(2)}) async-start(bf16[8,16,32,128]{3,2,1,0:T(8,128)(2,1)} %get-tuple-element.58), calls=%async_computation.5 | async-start | bytes 2097152 | tf_op jit(solution)/shard_map/all_to_all | solution.py:444
  171.9 2.8 %cycles.5 = bf16[8,16,16,128]{3,2,1,0:T(8,128)(2,1)} custom-call(s32[2]{0:T(128)} %pad_add_fusion.low_ref, bf16[16,128,256]{2,1,0:T(8,128)(2,1)} %get-tuple-element.57.turned_ref, bf16[8,16,32,128]{3,2,1,0:T(8,128)(2,1)} %copy-done.6), custom_call_target="tpu_custom_call" | custom-call | flops 2000000000 | bytes 12000000 | tf_op jit(solution)/shard_map/cycles/pallas_call | solution.py:347
  174.7 0.0 collective-permute-start.7
  174.7 0.0 collective-permute-done.5
  174.7 0.1 add_convert_fusion.1
  174.9 2.9 %collective-permute-start.6 = (bf16[8,16,16,128]{3,2,1,0:T(8,128)(2,1)S(1)}, bf16[8,16,16,128]{3,2,1,0:T(8,128)(2,1)S(1)}, u32[]{:S(2)}, u32[]{:S(2)}) collective-permute-start(bf16[8,16,16,128]{3,2,1,0:T(8,128)(2,1)S(1)} %add_convert_fusion.1), channel_id=1, source_target_pairs={{0,16},{8,24},{16,0},{24,8},{1,17},{9,25},{17,1},{25,9},{2,18},{10... | collective-permute-start | bytes 1572872 | tf_op jit(solution)/shard_map/ppermute | solution.py:441
  177.7 9.3 %all-to-all-done.5.filtered_ref = bf16[8,16,32,128]{3,2,1,0:T(8,128)(2,1)S(1)} async-done(((bf16[8,16,32,128]{3,2,1,0:T(8,128)(2,1)}), bf16[8,16,32,128]{3,2,1,0:T(8,128)(2,1)S(1)}, u32[]{:S(2)}, u32[]{:S(2)}) %all-to-all-start.5) | async-done | bytes 1048608 | tf_op jit(solution)/shard_map/all_to_all | solution.py:444
  187.0 1.0 copy-done.5
  188.0 2.8 %cycles.3 = bf16[8,16,16,128]{3,2,1,0:T(8,128)(2,1)} custom-call(s32[2]{0:T(128)} %pad_add_fusion.low_ref, bf16[16,128,256]{2,1,0:T(8,128)(2,1)} %get-tuple-element.57.turned_ref, bf16[8,16,32,128]{3,2,1,0:T(8,128)(2,1)} %copy-done.5), custom_call_target="tpu_custom_call" | custom-call | flops 2000000000 | bytes 12000000 | tf_op jit(solution)/shard_map/cycles/pallas_call | solution.py:347
  190.8 9.1 %collective-permute-done.7 = bf16[8,16,16,128]{3,2,1,0:T(8,128)(2,1)S(1)} collective-permute-done((bf16[8,16,16,128]{3,2,1,0:T(8,128)(2,1)}, bf16[8,16,16,128]{3,2,1,0:T(8,128)(2,1)S(1)}, u32[]{:S(2)}, u32[]{:S(2)}) %collective-permute-start.7) | collective-permute-done | bytes 524320 | tf_op jit(solution)/shard_map/ppermute | solution.py:441
  199.8 1.3 collective-permute-done.6
  201.1 2.0 add_convert_fusion
  203.2 3.9 %all-to-all-start.8 = ((bf16[8,16,16,128]{3,2,1,0:T(8,128)(2,1)}), bf16[8,16,16,128]{3,2,1,0:T(8,128)(2,1)S(1)}, u32[]{:S(2)}, u32[]{:S(2)}) async-start(bf16[8,16,16,128]{3,2,1,0:T(8,128)(2,1)} %add_convert_fusion), calls=%async_computation.8 | async-start | bytes 1048576 | tf_op jit(solution)/shard_map/all_to_all | solution.py:503
  207.1 0.7 copy.5.modes_ref
  207.8 9.0 %all-to-all-done.8 = bf16[8,16,16,128]{3,2,1,0:T(8,128)(2,1)S(1)} async-done(((bf16[8,16,16,128]{3,2,1,0:T(8,128)(2,1)}), bf16[8,16,16,128]{3,2,1,0:T(8,128)(2,1)S(1)}, u32[]{:S(2)}, u32[]{:S(2)}) %all-to-all-start.8) | async-done | bytes 524320 | tf_op jit(solution)/shard_map/all_to_all | solution.py:503
  216.8 0.8 copy-done.2
  217.6 5.6 %synthesis.1 = bf16[64,16,2048]{2,1,0:T(8,128)(2,1)} custom-call(s32[128,1]{1,0:T(8,128)} %copy.5.modes_ref, bf16[128,16,128]{2,1,0:T(8,128)(2,1)} %bitcast.10), custom_call_target="tpu_custom_call" | custom-call | tf_op jit(solution)/shard_map/synthesis/pallas_call | solution.py:405
  (19 shorter events, 0.1 us)
Async XLA Ops:
  0.7 13.2 %copy-start.9 = (s32[128]{0:T(128)S(1)}, s32[128]{0:T(128)}, u32[]{:S(2)}) copy-start(s32[128]{0:T(128)} %band_ref.1) | copy-start | bytes 1540
  6.5 17.9 %collective-permute-start = (bf16[8,16,16,128]{3,2,1,0:T(8,128)(2,1)}, bf16[8,16,16,128]{3,2,1,0:T(8,128)(2,1)}, u32[]{:S(2)}, u32[]{:S(2)}) collective-permute-start(bf16[8,16,16,128]{3,2,1,0:T(8,128)(2,1)} %bitcast.8), channel_id=1, source_target_pairs={{0,8},{8,0},{16,24},{24,16},{1,9},{9,1},{17,25},{25,17},{2,10},{10... | collective-permute-start | bytes 1572872 | tf_op jit(solution)/shard_map/ppermute | solution.py:441
  9.5 14.9 %all-to-all-start = ((bf16[8,16,16,128]{3,2,1,0:T(8,128)(2,1)}), bf16[8,16,16,128]{3,2,1,0:T(8,128)(2,1)S(1)}, u32[]{:S(2)}, u32[]{:S(2)}) async-start(bf16[8,16,16,128]{3,2,1,0:T(8,128)(2,1)} %bitcast.9), calls=%async_computation | async-start | bytes 1048576 | tf_op jit(solution)/shard_map/all_to_all | solution.py:444
  24.4 7.6 %copy-start.4 = (bf16[8,16,16,128]{3,2,1,0:T(8,128)(2,1)}, bf16[8,16,16,128]{3,2,1,0:T(8,128)(2,1)S(1)}, u32[]{:S(2)}) copy-start(bf16[8,16,16,128]{3,2,1,0:T(8,128)(2,1)S(1)} %all-to-all-done.refs_0_) | copy-start | bytes 1572868
  24.4 14.0 %all-to-all-start.1 = ((bf16[8,16,16,128]{3,2,1,0:T(8,128)(2,1)}), bf16[8,16,16,128]{3,2,1,0:T(8,128)(2,1)S(1)}, u32[]{:S(2)}, u32[]{:S(2)}) async-start(bf16[8,16,16,128]{3,2,1,0:T(8,128)(2,1)} %collective-permute-done), calls=%async_computation.1 | async-start | bytes 1048576 | tf_op jit(solution)/shard_map/all_to_all | solution.py:444
  28.6 15.2 %collective-permute-start.1 = (bf16[4,16,16,128]{3,2,1,0:T(8,128)(2,1)S(1)}, bf16[4,16,16,128]{3,2,1,0:T(8,128)(2,1)S(1)}, u32[]{:S(2)}, u32[]{:S(2)}) collective-permute-start(bf16[4,16,16,128]{3,2,1,0:T(8,128)(2,1)S(1)} %get-tuple-element.64), channel_id=1, source_target_pairs={{0,16},{8,24},{16,0},{24,8},{1,17},{9,25},{17,1},{25,9},{2,18},{10... | collective-permute-start | bytes 786440 | tf_op jit(solution)/shard_map/ppermute | solution.py:441
  38.4 12.5 %copy-start.8 = (bf16[8,16,16,128]{3,2,1,0:T(8,128)(2,1)}, bf16[8,16,16,128]{3,2,1,0:T(8,128)(2,1)S(1)}, u32[]{:S(2)}) copy-start(bf16[8,16,16,128]{3,2,1,0:T(8,128)(2,1)S(1)} %all-to-all-done.1.refs_0_) | copy-start | bytes 1572868
  43.8 10.2 %copy-start.11 = (bf16[4,16,16,128]{3,2,1,0:T(8,128)(2,1)}, bf16[4,16,16,128]{3,2,1,0:T(8,128)(2,1)S(1)}, u32[]{:S(2)}) copy-start(bf16[4,16,16,128]{3,2,1,0:T(8,128)(2,1)S(1)} %collective-permute-done.1.refs_0_) | copy-start | bytes 786436
  43.8 19.3 %all-to-all-start.2 = ((bf16[8,32,16,128]{3,2,1,0:T(8,128)(2,1)}), bf16[8,32,16,128]{3,2,1,0:T(8,128)(2,1)S(1)}, u32[]{:S(2)}, u32[]{:S(2)}) async-start(bf16[8,32,16,128]{3,2,1,0:T(8,128)(2,1)} %harmonic.3), calls=%async_computation.2 | async-start | bytes 2097152 | tf_op jit(solution)/shard_map/all_to_all | solution.py:444
  47.7 15.4 %collective-permute-start.2 = (bf16[4,16,16,128]{3,2,1,0:T(8,128)(2,1)S(1)}, bf16[4,16,16,128]{3,2,1,0:T(8,128)(2,1)S(1)}, u32[]{:S(2)}, u32[]{:S(2)}) collective-permute-start(bf16[4,16,16,128]{3,2,1,0:T(8,128)(2,1)S(1)} %get-tuple-element.63), channel_id=1, source_target_pairs={{0,16},{8,24},{16,0},{24,8},{1,17},{9,25},{17,1},{25,9},{2,18},{10... | collective-permute-start | bytes 786440 | tf_op jit(solution)/shard_map/ppermute | solution.py:441
  47.7 15.4 %collective-permute-start.3 = (bf16[4,16,16,128]{3,2,1,0:T(8,128)(2,1)S(1)}, bf16[4,16,16,128]{3,2,1,0:T(8,128)(2,1)S(1)}, u32[]{:S(2)}, u32[]{:S(2)}) collective-permute-start(bf16[4,16,16,128]{3,2,1,0:T(8,128)(2,1)S(1)} %collective-permute-done.1.refs_0_), channel_id=1, source_target_pairs={{0,8},{8,0},{16,24},{24,16},{1,9},{9,1},{17,25},{25,17},{2,10},{10... | collective-permute-start | bytes 786440 | tf_op jit(solution)/shard_map/ppermute | solution.py:441
  63.1 17.9 %copy-start = (bf16[8,32,16,128]{3,2,1,0:T(8,128)(2,1)}, bf16[8,32,16,128]{3,2,1,0:T(8,128)(2,1)S(1)}, u32[]{:S(2)}) copy-start(bf16[8,32,16,128]{3,2,1,0:T(8,128)(2,1)S(1)} %all-to-all-done.2.refs_0_) | copy-start | bytes 3145732
  63.1 12.6 %copy-start.12 = (bf16[4,16,16,128]{3,2,1,0:T(8,128)(2,1)}, bf16[4,16,16,128]{3,2,1,0:T(8,128)(2,1)S(1)}, u32[]{:S(2)}) copy-start(bf16[4,16,16,128]{3,2,1,0:T(8,128)(2,1)S(1)} %collective-permute-done.2.refs_1_) | copy-start | bytes 786436
  63.1 12.6 %copy-start.13 = (bf16[4,16,16,128]{3,2,1,0:T(8,128)(2,1)}, bf16[4,16,16,128]{3,2,1,0:T(8,128)(2,1)S(1)}, u32[]{:S(2)}) copy-start(bf16[4,16,16,128]{3,2,1,0:T(8,128)(2,1)S(1)} %collective-permute-done.3.refs_2_) | copy-start | bytes 786436
  63.1 19.3 %all-to-all-start.3 = ((bf16[8,32,16,128]{3,2,1,0:T(8,128)(2,1)}), bf16[8,32,16,128]{3,2,1,0:T(8,128)(2,1)S(1)}, u32[]{:S(2)}, u32[]{:S(2)}) async-start(bf16[8,32,16,128]{3,2,1,0:T(8,128)(2,1)} %harmonic.4), calls=%async_computation.3 | async-start | bytes 2097152 | tf_op jit(solution)/shard_map/all_to_all | solution.py:444
  67.0 8.7 %collective-permute-start.4 = (bf16[4,16,16,128]{3,2,1,0:T(8,128)(2,1)S(1)}, bf16[4,16,16,128]{3,2,1,0:T(8,128)(2,1)S(1)}, u32[]{:S(2)}, u32[]{:S(2)}) collective-permute-start(bf16[4,16,16,128]{3,2,1,0:T(8,128)(2,1)S(1)} %collective-permute-done.2.refs_1_), channel_id=1, source_target_pairs={{0,8},{8,0},{16,24},{24,16},{1,9},{9,1},{17,25},{25,17},{2,10},{10... | collective-permute-start | bytes 786440 | tf_op jit(solution)/shard_map/ppermute | solution.py:441
  75.7 0.7 copy-start.14
  82.4 30.9 %copy-start.1 = (bf16[8,32,16,128]{3,2,1,0:T(8,128)(2,1)}, bf16[8,32,16,128]{3,2,1,0:T(8,128)(2,1)S(1)}, u32[]{:S(2)}) copy-start(bf16[8,32,16,128]{3,2,1,0:T(8,128)(2,1)S(1)} %all-to-all-done.3.refs_1_) | copy-start | bytes 3145732
  119.0 30.2 %all-to-all-start.6 = ((bf16[8,16,32,256]{3,2,1,0:T(8,128)(2,1)}), bf16[8,16,32,256]{3,2,1,0:T(8,128)(2,1)S(1)}, u32[]{:S(2)}, u32[]{:S(2)}) async-start(bf16[8,16,32,256]{3,2,1,0:T(8,128)(2,1)} %filters.2), calls=%async_computation.6 | async-start | bytes 4194304 | tf_op jit(solution)/shard_map/all_to_all | solution.py:444
  149.2 3.6 %copy-start.3 = (bf16[8,16,32,256]{3,2,1,0:T(8,128)(2,1)}, bf16[8,16,32,256]{3,2,1,0:T(8,128)(2,1)S(1)}, u32[]{:S(2)}) copy-start(bf16[8,16,32,256]{3,2,1,0:T(8,128)(2,1)S(1)} %all-to-all-done.6.filtered_ref) | copy-start | bytes 6291460
  149.2 18.9 %all-to-all-start.7 = ((bf16[8,16,32,128]{3,2,1,0:T(8,128)(2,1)}), bf16[8,16,32,128]{3,2,1,0:T(8,128)(2,1)S(1)}, u32[]{:S(2)}, u32[]{:S(2)}) async-start(bf16[8,16,32,128]{3,2,1,0:T(8,128)(2,1)} %get-tuple-element.62), calls=%async_computation.7 | async-start | bytes 2097152 | tf_op jit(solution)/shard_map/all_to_all | solution.py:444
  156.4 18.3 %collective-permute-start.5 = (bf16[8,16,16,128]{3,2,1,0:T(8,128)(2,1)}, bf16[8,16,16,128]{3,2,1,0:T(8,128)(2,1)S(1)}, u32[]{:S(2)}, u32[]{:S(2)}) collective-permute-start(bf16[8,16,16,128]{3,2,1,0:T(8,128)(2,1)} %get-tuple-element.61), channel_id=1, source_target_pairs={{0,8},{8,0},{16,24},{24,16},{1,9},{9,1},{17,25},{25,17},{2,10},{10... | collective-permute-start | bytes 1572872 | tf_op jit(solution)/shard_map/ppermute | solution.py:441
  168.1 3.7 %copy-start.6 = (bf16[8,16,32,128]{3,2,1,0:T(8,128)(2,1)}, bf16[8,16,32,128]{3,2,1,0:T(8,128)(2,1)S(1)}, u32[]{:S(2)}) copy-start(bf16[8,16,32,128]{3,2,1,0:T(8,128)(2,1)S(1)} %all-to-all-done.7.filtered_ref) | copy-start | bytes 3145732
  168.1 18.9 %all-to-all-start.5 = ((bf16[8,16,32,128]{3,2,1,0:T(8,128)(2,1)}), bf16[8,16,32,128]{3,2,1,0:T(8,128)(2,1)S(1)}, u32[]{:S(2)}, u32[]{:S(2)}) async-start(bf16[8,16,32,128]{3,2,1,0:T(8,128)(2,1)} %get-tuple-element.58), calls=%async_computation.5 | async-start | bytes 2097152 | tf_op jit(solution)/shard_map/all_to_all | solution.py:444
  171.9 2.8 %copy-start.7 = (bf16[8,16,16,128]{3,2,1,0:T(8,128)(2,1)S(1)}, bf16[8,16,16,128]{3,2,1,0:T(8,128)(2,1)}, u32[]{:S(2)}) copy-start(bf16[8,16,16,128]{3,2,1,0:T(8,128)(2,1)} %get-tuple-element.60) | copy-start | bytes 1572868
  174.7 25.2 %collective-permute-start.7 = (bf16[8,16,16,128]{3,2,1,0:T(8,128)(2,1)}, bf16[8,16,16,128]{3,2,1,0:T(8,128)(2,1)S(1)}, u32[]{:S(2)}, u32[]{:S(2)}) collective-permute-start(bf16[8,16,16,128]{3,2,1,0:T(8,128)(2,1)} %cycles.5), channel_id=1, source_target_pairs={{0,8},{8,0},{16,24},{24,16},{1,9},{9,1},{17,25},{25,17},{2,10},{10... | collective-permute-start | bytes 1572872 | tf_op jit(solution)/shard_map/ppermute | solution.py:441
  174.9 26.3 %collective-permute-start.6 = (bf16[8,16,16,128]{3,2,1,0:T(8,128)(2,1)S(1)}, bf16[8,16,16,128]{3,2,1,0:T(8,128)(2,1)S(1)}, u32[]{:S(2)}, u32[]{:S(2)}) collective-permute-start(bf16[8,16,16,128]{3,2,1,0:T(8,128)(2,1)S(1)} %add_convert_fusion.1), channel_id=1, source_target_pairs={{0,16},{8,24},{16,0},{24,8},{1,17},{9,25},{17,1},{25,9},{2,18},{10... | collective-permute-start | bytes 1572872 | tf_op jit(solution)/shard_map/ppermute | solution.py:441
  187.0 1.0 copy-start.5
  190.8 16.3 %copy-start.10 = (s32[128]{0:T(128)S(1)}, s32[128]{0:T(128)}, u32[]{:S(2)}) copy-start(s32[128]{0:T(128)} %band_ref.1) | copy-start | bytes 1540
  203.2 13.6 %all-to-all-start.8 = ((bf16[8,16,16,128]{3,2,1,0:T(8,128)(2,1)}), bf16[8,16,16,128]{3,2,1,0:T(8,128)(2,1)S(1)}, u32[]{:S(2)}, u32[]{:S(2)}) async-start(bf16[8,16,16,128]{3,2,1,0:T(8,128)(2,1)} %add_convert_fusion), calls=%async_computation.8 | async-start | bytes 1048576 | tf_op jit(solution)/shard_map/all_to_all | solution.py:503
  216.8 0.8 copy-start.2

commit v4 on v3

--- a/solution.py
+++ b/solution.py
@@ -355,12 +355,9 @@
     )(low, turned, filtered)
 
 
-def synthesis_kernel(modes_ref, parts_ref, out_ref, there_ref, phase_ref, wide_ref, turn_ref, left_ref, sent):
-    chans, cycles, pixels = there_ref.shape
-    steps = sent.shape[0]
-    modes, _, pair = parts_ref.shape
+def phases_kernel(modes_ref, phase_ref):
+    modes, pixels = modes_ref.shape[0], phase_ref.shape[1]
     low = 128
-    total = pair // 2
     ids = modes_ref[...]
     unit = 2.0 * math.pi / pixels
 
@@ -376,6 +373,27 @@
         columns = slice(h * low, (h + 1) * low)
         phase_ref[:modes, columns] = (ca * cos_low - sa * sin_low).astype(BF16)
         phase_ref[modes:, columns] = (-(sa * cos_low + ca * sin_low)).astype(BF16)
+
+
+def phases_of(modes, pixels):
+    count = modes.shape[0]
+    vmem = pl.BlockSpec(memory_space=pltpu.VMEM)
+    return pl.pallas_call(
+        phases_kernel,
+        in_specs=[vmem],
+        out_specs=vmem,
+        out_shape=jax.ShapeDtypeStruct((2 * count, pixels), BF16),
+        compiler_params=params(),
+        cost_estimate=COST,
+        name="phases",
+    )(modes.reshape(count, 1))
+
+
+def synthesis_kernel(phase_ref, parts_ref, out_ref, there_ref, wide_ref, turn_ref, left_ref, sent):
+    chans, cycles, pixels = there_ref.shape
+    steps = sent.shape[0]
+    modes, _, pair = parts_ref.shape
+    total = pair // 2
     put(wide_ref, slice(None), parts_ref[...].astype(F32).reshape(modes * cycles, pair))
     for r in range(cycles):
         part = get(wide_ref, pl.ds(r, modes, stride=cycles), pair)
@@ -397,8 +415,9 @@
         copy.wait()
 
 
-def synthesis(parts, modes, pixels):
+def synthesis(parts, phases):
     count, cycles, pair = parts.shape
+    pixels = phases.shape[1]
     chans = pair // 2
     steps = divisor(chans, 8)
     vmem = pl.BlockSpec(memory_space=pltpu.VMEM)
@@ -409,7 +428,6 @@
         out_shape=jax.ShapeDtypeStruct((chans, cycles, pixels), BF16),
         scratch_shapes=[
             pltpu.VMEM((chans, cycles, pixels), BF16),
-            pltpu.VMEM((2 * count, pixels), BF16),
             pltpu.VMEM((lane_blocks(pair), count * cycles, 128), F32),
             pltpu.VMEM((lane_blocks(2 * count), chans * cycles, 128), F32),
             pltpu.VMEM((chans * cycles, 2 * count), BF16),
@@ -417,7 +435,7 @@
         ],
         compiler_params=params(),
         name="synthesis",
-    )(modes.reshape(count, 1), parts)
+    )(phases, parts)
 
 
 def body(sky_maps, filters, band_order_values, slot_degree_values):
@@ -502,7 +520,7 @@
     cycle_part = total.astype(BF16)
     by_cycle = lax.all_to_all(cycle_part, "blk", split_axis=0, concat_axis=0, tiled=True)
     by_cycle = by_cycle.reshape(blk_groups * mode_dev, cycle_dev, 2 * chans)
-    return synthesis(by_cycle, band_order_values, pixels)
+    return synthesis(by_cycle, phases_of(band_order_values, pixels))
 
 
 def solution(mesh):

time: 224 us -> 224 us (level)
  waiting for transfers between devices: 87.7 us -> 84.7 us
    pallas_call x0 -> x1, Pallas kernels: none -> 2.95 us  [phases_of(): pl.pallas_call(phases_kernel, in_specs=[vmem], out_specs=vmem, out_shape=...]
    all_to_all x1, waiting for transfers between devices: 8.99 us -> 6.05 us  [body(): lax.all_to_all(cycle_part, 'blk', split_axis=0, concat_axis=0, tiled=True)]
  transfers between devices with their start and end apart: 16 -> 16, of which waited for: 11 -> 11; matrix products, arithmetic and copies ran while one was open for 1% -> 1% of each run, Pallas kernels for 17% -> 18%
where the time goes in v4:
time: 224 us; the launch traced here: 223 us
  waiting for transfers between devices  84.7 us (38%)
  Pallas kernels  56.4 us (25%)
  starting transfers between devices  42.1 us (19%)
  blocking collectives  30.9 us (14%)
  other arithmetic  4.18 us (2%)
  local copies, waits for them, and re-layouts  3.92 us (2%)
    all_to_all x7, waiting for transfers between devices, exchange(): return lax.all_to_all(value, 'blk', split_axis=0, concat_axis=0, tiled=True)  54.1 us
    all_to_all x1, blocking collectives, exchange(): return lax.all_to_all(value, 'blk', split_axis=0, concat_axis=0, tiled=True)  30.9 us
    all_to_all x7, starting transfers between devices, exchange(): return lax.all_to_all(value, 'blk', split_axis=0, concat_axis=0, tiled=True)  26.5 us
    ppermute x8, waiting for transfers between devices, swap(): return lax.ppermute(value, 'chan', [(i, i ^ t) for i in range(chan_groups)])  24.6 us
    pallas_call x2, Pallas kernels, apply_filters(): pl.pallas_call(functools.partial(filter_kernel, counts, wanted), grid=(sl...  12.9 us
    ppermute x8, starting transfers between devices, swap(): return lax.ppermute(value, 'chan', [(i, i ^ t) for i in range(chan_groups)])  11.7 us
    pallas_call x3, Pallas kernels, harmonic(): pl.pallas_call(functools.partial(harmonic_kernel, counts, family), grid=(...  10.9 us
    pallas_call x1, Pallas kernels, legendre(): pl.pallas_call(functools.partial(legendre_kernel, levels), in_specs=[pl.B...  9.83 us
  transfers between devices with their start and end apart: 16, of which 11 were waited for; matrix products, arithmetic and copies ran while one was open for 1% of the time, Pallas kernels for 18%

profile of v4, /device:TPU:0, one launch (start us, length us, event | category | flops | bytes accessed | tf_op | source)
XLA Modules:
  0.0 222.5 jit_solution(5746647310444009034)
XLA Ops:
  0.0 0.1 sine_multiply_fusion
  0.1 0.6 dynamic_slice.3.factor_ref
  0.7 5.8 %analysis.1 = bf16[128,16,128]{2,1,0:T(8,128)(2,1)} custom-call(f32[16]{0:T(128)} %dynamic_slice.3.factor_ref, s32[1,128]{1,0:T(1,128)} %bitcast.11, bf16[64,16,2048]{2,1,0:T(8,128)(2,1)} %sky_ref.1), custom_call_target="tpu_custom_call" | custom-call | tf_op jit(solution)/shard_map/analysis/pallas_call | solution.py:92
  6.5 3.0 %collective-permute-start = (bf16[8,16,16,128]{3,2,1,0:T(8,128)(2,1)}, bf16[8,16,16,128]{3,2,1,0:T(8,128)(2,1)}, u32[]{:S(2)}, u32[]{:S(2)}) collective-permute-start(bf16[8,16,16,128]{3,2,1,0:T(8,128)(2,1)} %bitcast.8), channel_id=1, source_target_pairs={{0,8},{8,0},{16,24},{24,16},{1,9},{9,1},{17,25},{25,17},{2,10},{10... | collective-permute-start | bytes 1572872 | tf_op jit(solution)/shard_map/ppermute | solution.py:459
  9.5 3.7 %all-to-all-start = ((bf16[8,16,16,128]{3,2,1,0:T(8,128)(2,1)}), bf16[8,16,16,128]{3,2,1,0:T(8,128)(2,1)S(1)}, u32[]{:S(2)}, u32[]{:S(2)}) async-start(bf16[8,16,16,128]{3,2,1,0:T(8,128)(2,1)} %bitcast.9), calls=%async_computation | async-start | bytes 1048576 | tf_op jit(solution)/shard_map/all_to_all | solution.py:462
  13.3 0.6 pad_add_fusion.1.first_ref
  13.9 0.0 copy-done.9
  13.9 0.7 add_multiply_fusion.log_ref
  14.6 9.8 %legendre.1 = (bf16[16,256,128]{2,1,0:T(8,128)(2,1)}, bf16[16,128,256]{2,1,0:T(8,128)(2,1)}) custom-call(s32[2]{0:T(128)} %pad_add_fusion.1.first_ref, s32[1024]{0:T(1024)} %degree_ref.1, s32[128]{0:T(128)} %band_ref.1, f32[128]{0:T(128)} %add_multiply_fusion.log_ref), custom_call_target="tpu_custom_call" | custom-call | flops 40000000 | bytes 30000000 | tf_op jit(solution)/shard_map/legendre/pallas_call | solution.py:174
  24.4 0.0 all-to-all-done.refs_0_
  24.4 0.0 collective-permute-done
  24.4 4.2 %all-to-all-start.1 = ((bf16[8,16,16,128]{3,2,1,0:T(8,128)(2,1)}), bf16[8,16,16,128]{3,2,1,0:T(8,128)(2,1)S(1)}, u32[]{:S(2)}, u32[]{:S(2)}) async-start(bf16[8,16,16,128]{3,2,1,0:T(8,128)(2,1)} %collective-permute-done), calls=%async_computation.1 | async-start | bytes 1048576 | tf_op jit(solution)/shard_map/all_to_all | solution.py:462
  28.6 2.7 %collective-permute-start.1 = (bf16[4,16,16,128]{3,2,1,0:T(8,128)(2,1)S(1)}, bf16[4,16,16,128]{3,2,1,0:T(8,128)(2,1)S(1)}, u32[]{:S(2)}, u32[]{:S(2)}) collective-permute-start(bf16[4,16,16,128]{3,2,1,0:T(8,128)(2,1)S(1)} %get-tuple-element.64), channel_id=1, source_target_pairs={{0,16},{8,24},{16,0},{24,8},{1,17},{9,25},{17,1},{25,9},{2,18},{10... | collective-permute-start | bytes 786440 | tf_op jit(solution)/shard_map/ppermute | solution.py:459
  31.3 0.6 pad_add_fusion.low_ref
  31.9 0.0 copy-done.3
  32.0 3.2 %harmonic.3 = bf16[8,32,16,128]{3,2,1,0:T(8,128)(2,1)} custom-call(s32[2]{0:T(128)} %pad_add_fusion.low_ref, bf16[16,256,128]{2,1,0:T(8,128)(2,1)} %get-tuple-element.46.lat_ref, bf16[8,16,16,128]{3,2,1,0:T(8,128)(2,1)} %copy-done.3), custom_call_target="tpu_custom_call" | custom-call | flops 2000000000 | bytes 12000000 | tf_op jit(solution)/shard_map/harmonic/pallas_call | solution.py:235
  35.1 3.2 %all-to-all-done.1.refs_0_ = bf16[8,16,16,128]{3,2,1,0:T(8,128)(2,1)S(1)} async-done(((bf16[8,16,16,128]{3,2,1,0:T(8,128)(2,1)}), bf16[8,16,16,128]{3,2,1,0:T(8,128)(2,1)S(1)}, u32[]{:S(2)}, u32[]{:S(2)}) %all-to-all-start.1) | async-done | bytes 524320 | tf_op jit(solution)/shard_map/all_to_all | solution.py:462
  38.4 5.5 %collective-permute-done.1.refs_0_ = bf16[4,16,16,128]{3,2,1,0:T(8,128)(2,1)S(1)} collective-permute-done((bf16[4,16,16,128]{3,2,1,0:T(8,128)(2,1)S(1)}, bf16[4,16,16,128]{3,2,1,0:T(8,128)(2,1)S(1)}, u32[]{:S(2)}, u32[]{:S(2)}) %collective-permute-start.1) | collective-permute-done | bytes 262176 | tf_op jit(solution)/shard_map/ppermute | solution.py:459
  43.8 3.8 %all-to-all-start.2 = ((bf16[8,32,16,128]{3,2,1,0:T(8,128)(2,1)}), bf16[8,32,16,128]{3,2,1,0:T(8,128)(2,1)S(1)}, u32[]{:S(2)}, u32[]{:S(2)}) async-start(bf16[8,32,16,128]{3,2,1,0:T(8,128)(2,1)} %harmonic.3), calls=%async_computation.2 | async-start | bytes 2097152 | tf_op jit(solution)/shard_map/all_to_all | solution.py:462
  47.7 0.0 collective-permute-start.2
  47.7 3.1 %collective-permute-start.3 = (bf16[4,16,16,128]{3,2,1,0:T(8,128)(2,1)S(1)}, bf16[4,16,16,128]{3,2,1,0:T(8,128)(2,1)S(1)}, u32[]{:S(2)}, u32[]{:S(2)}) collective-permute-start(bf16[4,16,16,128]{3,2,1,0:T(8,128)(2,1)S(1)} %collective-permute-done.1.refs_0_), channel_id=1, source_target_pairs={{0,8},{8,0},{16,24},{24,16},{1,9},{9,1},{17,25},{25,17},{2,10},{10... | collective-permute-start | bytes 786440 | tf_op jit(solution)/shard_map/ppermute | solution.py:459
  50.8 0.0 copy-done.8
  50.8 3.2 %harmonic.4 = bf16[8,32,16,128]{3,2,1,0:T(8,128)(2,1)} custom-call(s32[2]{0:T(128)} %pad_add_fusion.low_ref, bf16[16,256,128]{2,1,0:T(8,128)(2,1)} %get-tuple-element.46.lat_ref, bf16[8,16,16,128]{3,2,1,0:T(8,128)(2,1)} %copy-done.8), custom_call_target="tpu_custom_call" | custom-call | flops 2000000000 | bytes 12000000 | tf_op jit(solution)/shard_map/harmonic/pallas_call | solution.py:235
  54.0 0.0 copy-done.11
  54.0 9.1 %all-to-all-done.2.refs_0_ = bf16[8,32,16,128]{3,2,1,0:T(8,128)(2,1)S(1)} async-done(((bf16[8,32,16,128]{3,2,1,0:T(8,128)(2,1)}), bf16[8,32,16,128]{3,2,1,0:T(8,128)(2,1)S(1)}, u32[]{:S(2)}, u32[]{:S(2)}) %all-to-all-start.2) | async-done | bytes 1048608 | tf_op jit(solution)/shard_map/all_to_all | solution.py:462
  63.1 0.0 collective-permute-done.2.refs_1_
  63.1 0.0 collective-permute-done.3.refs_2_
  63.1 3.8 %all-to-all-start.3 = ((bf16[8,32,16,128]{3,2,1,0:T(8,128)(2,1)}), bf16[8,32,16,128]{3,2,1,0:T(8,128)(2,1)S(1)}, u32[]{:S(2)}, u32[]{:S(2)}) async-start(bf16[8,32,16,128]{3,2,1,0:T(8,128)(2,1)} %harmonic.4), calls=%async_computation.3 | async-start | bytes 2097152 | tf_op jit(solution)/shard_map/all_to_all | solution.py:462
  67.0 0.0 collective-permute-start.4
  67.0 8.7 %collective-permute-done.4.refs_3_ = bf16[4,16,16,128]{3,2,1,0:T(8,128)(2,1)S(1)} collective-permute-done((bf16[4,16,16,128]{3,2,1,0:T(8,128)(2,1)S(1)}, bf16[4,16,16,128]{3,2,1,0:T(8,128)(2,1)S(1)}, u32[]{:S(2)}, u32[]{:S(2)}) %collective-permute-start.4) | collective-permute-done | bytes 262176 | tf_op jit(solution)/shard_map/ppermute | solution.py:459
  75.7 0.0 copy-done.12
  75.7 0.0 copy-done.13
  75.7 0.7 copy-done.14
  76.4 4.6 %harmonic.5 = bf16[8,32,16,256]{3,2,1,0:T(8,128)(2,1)} custom-call(s32[2]{0:T(128)} %pad_add_fusion.low_ref, bf16[16,256,128]{2,1,0:T(8,128)(2,1)} %get-tuple-element.46.lat_ref, bf16[4,16,16,128]{3,2,1,0:T(8,128)(2,1)} %copy-done.11, bf16[4,16,16,128]{3,2,1,0:T(8,128)(2,1)} %copy-done.12, bf16[4,16,16,128]{3,2,1,0:T(8,128)(2,1)} %copy-done.13, ...), custom_call_target="tpu_custom_call" | custom-call | flops 2000000000 | bytes 12000000 | tf_op jit(solution)/shard_map/harmonic/pallas_call | solution.py:235
  81.0 0.0 copy-done
  81.0 1.4 all-to-all-done.3.refs_1_
  82.4 30.9 %all_to_all.45.refs_2_ = bf16[8,32,16,256]{3,2,1,0:T(8,128)(2,1)} all-to-all(bf16[8,32,16,256]{3,2,1,0:T(8,128)(2,1)} %harmonic.5), channel_id=1, replica_groups=mesh['chan'=4,'blk'=8] {'blk'}, dimensions={0} | all-to-all | bytes 4194304 | tf_op jit(solution)/shard_map/all_to_all | solution.py:462
  113.3 5.7 %filters.2 = bf16[8,16,32,256]{3,2,1,0:T(8,128)(2,1)} custom-call(s32[2]{0:T(128)} %pad_add_fusion.low_ref, bf16[32,256,256]{2,1,0:T(8,128)(2,1)} %filters_ref.3, bf16[8,32,16,128]{3,2,1,0:T(8,128)(2,1)} %copy-done, bf16[8,32,16,128]{3,2,1,0:T(8,128)(2,1)} %copy-done.1, bf16[8,32,16,256]{3,2,1,0:T(8,128)(2,1)} %all_to_all.45.refs_2_), custom_call_target="tpu_custom_call" | custom-call | flops 2000000000 | bytes 12000000 | tf_op jit(solution)/shard_map/filters/pallas_call | solution.py:300
  119.0 3.6 %all-to-all-start.6 = ((bf16[8,16,32,256]{3,2,1,0:T(8,128)(2,1)}), bf16[8,16,32,256]{3,2,1,0:T(8,128)(2,1)S(1)}, u32[]{:S(2)}, u32[]{:S(2)}) async-start(bf16[8,16,32,256]{3,2,1,0:T(8,128)(2,1)} %filters.2), calls=%async_computation.6 | async-start | bytes 4194304 | tf_op jit(solution)/shard_map/all_to_all | solution.py:462
  122.6 7.2 %filters.3 = (bf16[8,16,32,128]{3,2,1,0:T(8,128)(2,1)}, bf16[8,16,32,128]{3,2,1,0:T(8,128)(2,1)}) custom-call(s32[2]{0:T(128)} %pad_add_fusion.low_ref, bf16[32,256,256]{2,1,0:T(8,128)(2,1)} %filters_ref.3, bf16[8,32,16,128]{3,2,1,0:T(8,128)(2,1)} %copy-done, bf16[8,32,16,128]{3,2,1,0:T(8,128)(2,1)} %copy-done.1, bf16[8,32,16,256]{3,2,1,0:T(8,128)(2,1)} %all_to_all.45.refs_2_), custom_call_target="tpu_custom_call" | custom-call | flops 2000000000 | bytes 12000000 | tf_op jit(solution)/shard_map/filters/pallas_call | solution.py:300
  129.8 19.4 %all-to-all-done.6.filtered_ref = bf16[8,16,32,256]{3,2,1,0:T(8,128)(2,1)S(1)} async-done(((bf16[8,16,32,256]{3,2,1,0:T(8,128)(2,1)}), bf16[8,16,32,256]{3,2,1,0:T(8,128)(2,1)S(1)}, u32[]{:S(2)}, u32[]{:S(2)}) %all-to-all-start.6) | async-done | bytes 2097184 | tf_op jit(solution)/shard_map/all_to_all | solution.py:462
  149.2 3.6 %all-to-all-start.7 = ((bf16[8,16,32,128]{3,2,1,0:T(8,128)(2,1)}), bf16[8,16,32,128]{3,2,1,0:T(8,128)(2,1)S(1)}, u32[]{:S(2)}, u32[]{:S(2)}) async-start(bf16[8,16,32,128]{3,2,1,0:T(8,128)(2,1)} %get-tuple-element.62), calls=%async_computation.7 | async-start | bytes 2097152 | tf_op jit(solution)/shard_map/all_to_all | solution.py:462
  152.8 3.6 %cycles.4 = (bf16[8,16,16,128]{3,2,1,0:T(8,128)(2,1)}, bf16[8,16,16,128]{3,2,1,0:T(8,128)(2,1)}) custom-call(s32[2]{0:T(128)} %pad_add_fusion.low_ref, bf16[16,128,256]{2,1,0:T(8,128)(2,1)} %get-tuple-element.57.turned_ref, bf16[8,16,32,256]{3,2,1,0:T(8,128)(2,1)} %copy-done.2), custom_call_target="tpu_custom_call" | custom-call | flops 2000000000 | bytes 12000000 | tf_op jit(solution)/shard_map/cycles/pallas_call | solution.py:347
  156.4 0.0 collective-permute-start.5
  156.4 11.7 %all-to-all-done.7.filtered_ref = bf16[8,16,32,128]{3,2,1,0:T(8,128)(2,1)S(1)} async-done(((bf16[8,16,32,128]{3,2,1,0:T(8,128)(2,1)}), bf16[8,16,32,128]{3,2,1,0:T(8,128)(2,1)S(1)}, u32[]{:S(2)}, u32[]{:S(2)}) %all-to-all-start.7) | async-done | bytes 1048608 | tf_op jit(solution)/shard_map/all_to_all | solution.py:462
  168.1 3.7 %all-to-all-start.5 = ((bf16[8,16,32,128]{3,2,1,0:T(8,128)(2,1)}), bf16[8,16,32,128]{3,2,1,0:T(8,128)(2,1)S(1)}, u32[]{:S(2)}, u32[]{:S(2)}) async-start(bf16[8,16,32,128]{3,2,1,0:T(8,128)(2,1)} %get-tuple-element.58), calls=%async_computation.5 | async-start | bytes 2097152 | tf_op jit(solution)/shard_map/all_to_all | solution.py:462
  171.9 2.8 %cycles.5 = bf16[8,16,16,128]{3,2,1,0:T(8,128)(2,1)} custom-call(s32[2]{0:T(128)} %pad_add_fusion.low_ref, bf16[16,128,256]{2,1,0:T(8,128)(2,1)} %get-tuple-element.57.turned_ref, bf16[8,16,32,128]{3,2,1,0:T(8,128)(2,1)} %copy-done.6), custom_call_target="tpu_custom_call" | custom-call | flops 2000000000 | bytes 12000000 | tf_op jit(solution)/shard_map/cycles/pallas_call | solution.py:347
  174.7 0.0 collective-permute-start.7
  174.7 0.0 collective-permute-done.5
  174.7 0.1 add_convert_fusion.1
  174.9 2.9 %collective-permute-start.6 = (bf16[8,16,16,128]{3,2,1,0:T(8,128)(2,1)S(1)}, bf16[8,16,16,128]{3,2,1,0:T(8,128)(2,1)S(1)}, u32[]{:S(2)}, u32[]{:S(2)}) collective-permute-start(bf16[8,16,16,128]{3,2,1,0:T(8,128)(2,1)S(1)} %add_convert_fusion.1), channel_id=1, source_target_pairs={{0,16},{8,24},{16,0},{24,8},{1,17},{9,25},{17,1},{25,9},{2,18},{10... | collective-permute-start | bytes 1572872 | tf_op jit(solution)/shard_map/ppermute | solution.py:459
  177.7 9.3 %all-to-all-done.5.filtered_ref = bf16[8,16,32,128]{3,2,1,0:T(8,128)(2,1)S(1)} async-done(((bf16[8,16,32,128]{3,2,1,0:T(8,128)(2,1)}), bf16[8,16,32,128]{3,2,1,0:T(8,128)(2,1)S(1)}, u32[]{:S(2)}, u32[]{:S(2)}) %all-to-all-start.5) | async-done | bytes 1048608 | tf_op jit(solution)/shard_map/all_to_all | solution.py:462
  187.0 1.0 copy-done.5
  188.0 2.8 %cycles.3 = bf16[8,16,16,128]{3,2,1,0:T(8,128)(2,1)} custom-call(s32[2]{0:T(128)} %pad_add_fusion.low_ref, bf16[16,128,256]{2,1,0:T(8,128)(2,1)} %get-tuple-element.57.turned_ref, bf16[8,16,32,128]{3,2,1,0:T(8,128)(2,1)} %copy-done.5), custom_call_target="tpu_custom_call" | custom-call | flops 2000000000 | bytes 12000000 | tf_op jit(solution)/shard_map/cycles/pallas_call | solution.py:347
  190.8 9.1 %collective-permute-done.7 = bf16[8,16,16,128]{3,2,1,0:T(8,128)(2,1)S(1)} collective-permute-done((bf16[8,16,16,128]{3,2,1,0:T(8,128)(2,1)}, bf16[8,16,16,128]{3,2,1,0:T(8,128)(2,1)S(1)}, u32[]{:S(2)}, u32[]{:S(2)}) %collective-permute-start.7) | collective-permute-done | bytes 524320 | tf_op jit(solution)/shard_map/ppermute | solution.py:459
  199.8 1.3 collective-permute-done.6
  201.1 2.0 add_convert_fusion
  203.2 3.9 %all-to-all-start.8 = ((bf16[8,16,16,128]{3,2,1,0:T(8,128)(2,1)}), bf16[8,16,16,128]{3,2,1,0:T(8,128)(2,1)S(1)}, u32[]{:S(2)}, u32[]{:S(2)}) async-start(bf16[8,16,16,128]{3,2,1,0:T(8,128)(2,1)} %add_convert_fusion), calls=%async_computation.8 | async-start | bytes 1048576 | tf_op jit(solution)/shard_map/all_to_all | solution.py:521
  207.1 0.0 copy-done.10
  207.1 0.7 copy.5.modes_ref
  207.8 3.0 %phases.1.phase_ref = bf16[256,2048]{1,0:T(8,128)(2,1)} custom-call(s32[128,1]{1,0:T(8,128)} %copy.5.modes_ref), custom_call_target="tpu_custom_call" | custom-call | flops 2000000000 | bytes 12000000 | tf_op jit(solution)/shard_map/phases/pallas_call | solution.py:381
  210.8 6.0 %all-to-all-done.8 = bf16[8,16,16,128]{3,2,1,0:T(8,128)(2,1)S(1)} async-done(((bf16[8,16,16,128]{3,2,1,0:T(8,128)(2,1)}), bf16[8,16,16,128]{3,2,1,0:T(8,128)(2,1)S(1)}, u32[]{:S(2)}, u32[]{:S(2)}) %all-to-all-start.8) | async-done | bytes 524320 | tf_op jit(solution)/shard_map/all_to_all | solution.py:521
  216.8 0.8 copy-done.4
  217.6 4.8 %synthesis.1 = bf16[64,16,2048]{2,1,0:T(8,128)(2,1)} custom-call(bf16[256,2048]{1,0:T(8,128)(2,1)} %phases.1.phase_ref, bf16[128,16,128]{2,1,0:T(8,128)(2,1)} %bitcast.10), custom_call_target="tpu_custom_call" | custom-call | tf_op jit(solution)/shard_map/synthesis/pallas_call | solution.py:424
  (20 shorter events, 0.1 us)
Async XLA Ops:
  0.7 13.2 %copy-start.9 = (s32[128]{0:T(128)S(1)}, s32[128]{0:T(128)}, u32[]{:S(2)}) copy-start(s32[128]{0:T(128)} %band_ref.1) | copy-start | bytes 1540
  6.5 17.9 %collective-permute-start = (bf16[8,16,16,128]{3,2,1,0:T(8,128)(2,1)}, bf16[8,16,16,128]{3,2,1,0:T(8,128)(2,1)}, u32[]{:S(2)}, u32[]{:S(2)}) collective-permute-start(bf16[8,16,16,128]{3,2,1,0:T(8,128)(2,1)} %bitcast.8), channel_id=1, source_target_pairs={{0,8},{8,0},{16,24},{24,16},{1,9},{9,1},{17,25},{25,17},{2,10},{10... | collective-permute-start | bytes 1572872 | tf_op jit(solution)/shard_map/ppermute | solution.py:459
  9.5 14.9 %all-to-all-start = ((bf16[8,16,16,128]{3,2,1,0:T(8,128)(2,1)}), bf16[8,16,16,128]{3,2,1,0:T(8,128)(2,1)S(1)}, u32[]{:S(2)}, u32[]{:S(2)}) async-start(bf16[8,16,16,128]{3,2,1,0:T(8,128)(2,1)} %bitcast.9), calls=%async_computation | async-start | bytes 1048576 | tf_op jit(solution)/shard_map/all_to_all | solution.py:462
  24.4 7.6 %copy-start.3 = (bf16[8,16,16,128]{3,2,1,0:T(8,128)(2,1)}, bf16[8,16,16,128]{3,2,1,0:T(8,128)(2,1)S(1)}, u32[]{:S(2)}) copy-start(bf16[8,16,16,128]{3,2,1,0:T(8,128)(2,1)S(1)} %all-to-all-done.refs_0_) | copy-start | bytes 1572868
  24.4 14.0 %all-to-all-start.1 = ((bf16[8,16,16,128]{3,2,1,0:T(8,128)(2,1)}), bf16[8,16,16,128]{3,2,1,0:T(8,128)(2,1)S(1)}, u32[]{:S(2)}, u32[]{:S(2)}) async-start(bf16[8,16,16,128]{3,2,1,0:T(8,128)(2,1)} %collective-permute-done), calls=%async_computation.1 | async-start | bytes 1048576 | tf_op jit(solution)/shard_map/all_to_all | solution.py:462
  28.6 15.2 %collective-permute-start.1 = (bf16[4,16,16,128]{3,2,1,0:T(8,128)(2,1)S(1)}, bf16[4,16,16,128]{3,2,1,0:T(8,128)(2,1)S(1)}, u32[]{:S(2)}, u32[]{:S(2)}) collective-permute-start(bf16[4,16,16,128]{3,2,1,0:T(8,128)(2,1)S(1)} %get-tuple-element.64), channel_id=1, source_target_pairs={{0,16},{8,24},{16,0},{24,8},{1,17},{9,25},{17,1},{25,9},{2,18},{10... | collective-permute-start | bytes 786440 | tf_op jit(solution)/shard_map/ppermute | solution.py:459
  38.4 12.5 %copy-start.8 = (bf16[8,16,16,128]{3,2,1,0:T(8,128)(2,1)}, bf16[8,16,16,128]{3,2,1,0:T(8,128)(2,1)S(1)}, u32[]{:S(2)}) copy-start(bf16[8,16,16,128]{3,2,1,0:T(8,128)(2,1)S(1)} %all-to-all-done.1.refs_0_) | copy-start | bytes 1572868
  43.8 10.2 %copy-start.11 = (bf16[4,16,16,128]{3,2,1,0:T(8,128)(2,1)}, bf16[4,16,16,128]{3,2,1,0:T(8,128)(2,1)S(1)}, u32[]{:S(2)}) copy-start(bf16[4,16,16,128]{3,2,1,0:T(8,128)(2,1)S(1)} %collective-permute-done.1.refs_0_) | copy-start | bytes 786436
  43.8 19.3 %all-to-all-start.2 = ((bf16[8,32,16,128]{3,2,1,0:T(8,128)(2,1)}), bf16[8,32,16,128]{3,2,1,0:T(8,128)(2,1)S(1)}, u32[]{:S(2)}, u32[]{:S(2)}) async-start(bf16[8,32,16,128]{3,2,1,0:T(8,128)(2,1)} %harmonic.3), calls=%async_computation.2 | async-start | bytes 2097152 | tf_op jit(solution)/shard_map/all_to_all | solution.py:462
  47.7 15.4 %collective-permute-start.2 = (bf16[4,16,16,128]{3,2,1,0:T(8,128)(2,1)S(1)}, bf16[4,16,16,128]{3,2,1,0:T(8,128)(2,1)S(1)}, u32[]{:S(2)}, u32[]{:S(2)}) collective-permute-start(bf16[4,16,16,128]{3,2,1,0:T(8,128)(2,1)S(1)} %get-tuple-element.63), channel_id=1, source_target_pairs={{0,16},{8,24},{16,0},{24,8},{1,17},{9,25},{17,1},{25,9},{2,18},{10... | collective-permute-start | bytes 786440 | tf_op jit(solution)/shard_map/ppermute | solution.py:459
  47.7 15.4 %collective-permute-start.3 = (bf16[4,16,16,128]{3,2,1,0:T(8,128)(2,1)S(1)}, bf16[4,16,16,128]{3,2,1,0:T(8,128)(2,1)S(1)}, u32[]{:S(2)}, u32[]{:S(2)}) collective-permute-start(bf16[4,16,16,128]{3,2,1,0:T(8,128)(2,1)S(1)} %collective-permute-done.1.refs_0_), channel_id=1, source_target_pairs={{0,8},{8,0},{16,24},{24,16},{1,9},{9,1},{17,25},{25,17},{2,10},{10... | collective-permute-start | bytes 786440 | tf_op jit(solution)/shard_map/ppermute | solution.py:459
  63.1 17.9 %copy-start = (bf16[8,32,16,128]{3,2,1,0:T(8,128)(2,1)}, bf16[8,32,16,128]{3,2,1,0:T(8,128)(2,1)S(1)}, u32[]{:S(2)}) copy-start(bf16[8,32,16,128]{3,2,1,0:T(8,128)(2,1)S(1)} %all-to-all-done.2.refs_0_) | copy-start | bytes 3145732
  63.1 12.6 %copy-start.12 = (bf16[4,16,16,128]{3,2,1,0:T(8,128)(2,1)}, bf16[4,16,16,128]{3,2,1,0:T(8,128)(2,1)S(1)}, u32[]{:S(2)}) copy-start(bf16[4,16,16,128]{3,2,1,0:T(8,128)(2,1)S(1)} %collective-permute-done.2.refs_1_) | copy-start | bytes 786436
  63.1 12.6 %copy-start.13 = (bf16[4,16,16,128]{3,2,1,0:T(8,128)(2,1)}, bf16[4,16,16,128]{3,2,1,0:T(8,128)(2,1)S(1)}, u32[]{:S(2)}) copy-start(bf16[4,16,16,128]{3,2,1,0:T(8,128)(2,1)S(1)} %collective-permute-done.3.refs_2_) | copy-start | bytes 786436
  63.1 19.3 %all-to-all-start.3 = ((bf16[8,32,16,128]{3,2,1,0:T(8,128)(2,1)}), bf16[8,32,16,128]{3,2,1,0:T(8,128)(2,1)S(1)}, u32[]{:S(2)}, u32[]{:S(2)}) async-start(bf16[8,32,16,128]{3,2,1,0:T(8,128)(2,1)} %harmonic.4), calls=%async_computation.3 | async-start | bytes 2097152 | tf_op jit(solution)/shard_map/all_to_all | solution.py:462
  67.0 8.7 %collective-permute-start.4 = (bf16[4,16,16,128]{3,2,1,0:T(8,128)(2,1)S(1)}, bf16[4,16,16,128]{3,2,1,0:T(8,128)(2,1)S(1)}, u32[]{:S(2)}, u32[]{:S(2)}) collective-permute-start(bf16[4,16,16,128]{3,2,1,0:T(8,128)(2,1)S(1)} %collective-permute-done.2.refs_1_), channel_id=1, source_target_pairs={{0,8},{8,0},{16,24},{24,16},{1,9},{9,1},{17,25},{25,17},{2,10},{10... | collective-permute-start | bytes 786440 | tf_op jit(solution)/shard_map/ppermute | solution.py:459
  75.7 0.7 copy-start.14
  82.4 30.9 %copy-start.1 = (bf16[8,32,16,128]{3,2,1,0:T(8,128)(2,1)}, bf16[8,32,16,128]{3,2,1,0:T(8,128)(2,1)S(1)}, u32[]{:S(2)}) copy-start(bf16[8,32,16,128]{3,2,1,0:T(8,128)(2,1)S(1)} %all-to-all-done.3.refs_1_) | copy-start | bytes 3145732
  119.0 30.2 %all-to-all-start.6 = ((bf16[8,16,32,256]{3,2,1,0:T(8,128)(2,1)}), bf16[8,16,32,256]{3,2,1,0:T(8,128)(2,1)S(1)}, u32[]{:S(2)}, u32[]{:S(2)}) async-start(bf16[8,16,32,256]{3,2,1,0:T(8,128)(2,1)} %filters.2), calls=%async_computation.6 | async-start | bytes 4194304 | tf_op jit(solution)/shard_map/all_to_all | solution.py:462
  149.2 3.6 %copy-start.2 = (bf16[8,16,32,256]{3,2,1,0:T(8,128)(2,1)}, bf16[8,16,32,256]{3,2,1,0:T(8,128)(2,1)S(1)}, u32[]{:S(2)}) copy-start(bf16[8,16,32,256]{3,2,1,0:T(8,128)(2,1)S(1)} %all-to-all-done.6.filtered_ref) | copy-start | bytes 6291460
  149.2 18.9 %all-to-all-start.7 = ((bf16[8,16,32,128]{3,2,1,0:T(8,128)(2,1)}), bf16[8,16,32,128]{3,2,1,0:T(8,128)(2,1)S(1)}, u32[]{:S(2)}, u32[]{:S(2)}) async-start(bf16[8,16,32,128]{3,2,1,0:T(8,128)(2,1)} %get-tuple-element.62), calls=%async_computation.7 | async-start | bytes 2097152 | tf_op jit(solution)/shard_map/all_to_all | solution.py:462
  156.4 18.3 %collective-permute-start.5 = (bf16[8,16,16,128]{3,2,1,0:T(8,128)(2,1)}, bf16[8,16,16,128]{3,2,1,0:T(8,128)(2,1)S(1)}, u32[]{:S(2)}, u32[]{:S(2)}) collective-permute-start(bf16[8,16,16,128]{3,2,1,0:T(8,128)(2,1)} %get-tuple-element.61), channel_id=1, source_target_pairs={{0,8},{8,0},{16,24},{24,16},{1,9},{9,1},{17,25},{25,17},{2,10},{10... | collective-permute-start | bytes 1572872 | tf_op jit(solution)/shard_map/ppermute | solution.py:459
  168.1 3.7 %copy-start.6 = (bf16[8,16,32,128]{3,2,1,0:T(8,128)(2,1)}, bf16[8,16,32,128]{3,2,1,0:T(8,128)(2,1)S(1)}, u32[]{:S(2)}) copy-start(bf16[8,16,32,128]{3,2,1,0:T(8,128)(2,1)S(1)} %all-to-all-done.7.filtered_ref) | copy-start | bytes 3145732
  168.1 18.9 %all-to-all-start.5 = ((bf16[8,16,32,128]{3,2,1,0:T(8,128)(2,1)}), bf16[8,16,32,128]{3,2,1,0:T(8,128)(2,1)S(1)}, u32[]{:S(2)}, u32[]{:S(2)}) async-start(bf16[8,16,32,128]{3,2,1,0:T(8,128)(2,1)} %get-tuple-element.58), calls=%async_computation.5 | async-start | bytes 2097152 | tf_op jit(solution)/shard_map/all_to_all | solution.py:462
  171.9 2.8 %copy-start.7 = (bf16[8,16,16,128]{3,2,1,0:T(8,128)(2,1)S(1)}, bf16[8,16,16,128]{3,2,1,0:T(8,128)(2,1)}, u32[]{:S(2)}) copy-start(bf16[8,16,16,128]{3,2,1,0:T(8,128)(2,1)} %get-tuple-element.60) | copy-start | bytes 1572868
  174.7 25.2 %collective-permute-start.7 = (bf16[8,16,16,128]{3,2,1,0:T(8,128)(2,1)}, bf16[8,16,16,128]{3,2,1,0:T(8,128)(2,1)S(1)}, u32[]{:S(2)}, u32[]{:S(2)}) collective-permute-start(bf16[8,16,16,128]{3,2,1,0:T(8,128)(2,1)} %cycles.5), channel_id=1, source_target_pairs={{0,8},{8,0},{16,24},{24,16},{1,9},{9,1},{17,25},{25,17},{2,10},{10... | collective-permute-start | bytes 1572872 | tf_op jit(solution)/shard_map/ppermute | solution.py:459
  174.9 26.3 %collective-permute-start.6 = (bf16[8,16,16,128]{3,2,1,0:T(8,128)(2,1)S(1)}, bf16[8,16,16,128]{3,2,1,0:T(8,128)(2,1)S(1)}, u32[]{:S(2)}, u32[]{:S(2)}) collective-permute-start(bf16[8,16,16,128]{3,2,1,0:T(8,128)(2,1)S(1)} %add_convert_fusion.1), channel_id=1, source_target_pairs={{0,16},{8,24},{16,0},{24,8},{1,17},{9,25},{17,1},{25,9},{2,18},{10... | collective-permute-start | bytes 1572872 | tf_op jit(solution)/shard_map/ppermute | solution.py:459
  187.0 1.0 copy-start.5
  190.8 16.3 %copy-start.10 = (s32[128]{0:T(128)S(1)}, s32[128]{0:T(128)}, u32[]{:S(2)}) copy-start(s32[128]{0:T(128)} %band_ref.1) | copy-start | bytes 1540
  203.2 13.6 %all-to-all-start.8 = ((bf16[8,16,16,128]{3,2,1,0:T(8,128)(2,1)}), bf16[8,16,16,128]{3,2,1,0:T(8,128)(2,1)S(1)}, u32[]{:S(2)}, u32[]{:S(2)}) async-start(bf16[8,16,16,128]{3,2,1,0:T(8,128)(2,1)} %add_convert_fusion), calls=%async_computation.8 | async-start | bytes 1048576 | tf_op jit(solution)/shard_map/all_to_all | solution.py:521
  216.8 0.8 copy-start.4

commit v5 on v4

--- a/solution.py
+++ b/solution.py
@@ -9,7 +9,7 @@
 from jax.sharding import PartitionSpec as P
 
 BAND = 0.38
-VMEM_LIMIT = 56 * 1024 * 1024
+VMEM_LIMIT = 52 * 1024 * 1024
 F32 = jnp.float32
 BF16 = jnp.bfloat16
 COST = pl.CostEstimate(flops=2_000_000_000, bytes_accessed=12_000_000, transcendentals=0)

time: 224 us -> 222 us (level)
  Pallas kernels: 56.4 us -> 48.7 us
  waiting for transfers between devices: 84.7 us -> 92.1 us
    pallas_call x3, Pallas kernels: 9.18 us -> 5.95 us  [to_cycles(): pl.pallas_call(functools.partial(cycles_kernel, scale), in_specs=[pl.Bloc...]
    all_to_all x7, waiting for transfers between devices: 54.1 us -> 56.9 us  [exchange(): return lax.all_to_all(value, 'blk', split_axis=0, concat_axis=0, tiled=True)]
    all_to_all x1, waiting for transfers between devices: 6.05 us -> 8.51 us  [body(): lax.all_to_all(cycle_part, 'blk', split_axis=0, concat_axis=0, tiled=True)]
  transfers between devices with their start and end apart: 16 -> 16, of which waited for: 11 -> 11; matrix products, arithmetic and copies ran while one was open for 1% -> 1% of each run, Pallas kernels for 18% -> 15%
where the time goes in v5:
time: 222 us; the launch traced here: 221 us
  waiting for transfers between devices  92.1 us (41%)
  Pallas kernels  48.7 us (22%)
  starting transfers between devices  42.9 us (19%)
  blocking collectives  30.9 us (14%)
  other arithmetic  3.5 us (2%)
  local copies, waits for them, and re-layouts  2.84 us (1%)
    all_to_all x7, waiting for transfers between devices, exchange(): return lax.all_to_all(value, 'blk', split_axis=0, concat_axis=0, tiled=True)  56.9 us
    all_to_all x1, blocking collectives, exchange(): return lax.all_to_all(value, 'blk', split_axis=0, concat_axis=0, tiled=True)  30.9 us
    all_to_all x7, starting transfers between devices, exchange(): return lax.all_to_all(value, 'blk', split_axis=0, concat_axis=0, tiled=True)  27.2 us
    ppermute x8, waiting for transfers between devices, swap(): return lax.ppermute(value, 'chan', [(i, i ^ t) for i in range(chan_groups)])  26.6 us
    pallas_call x2, Pallas kernels, apply_filters(): pl.pallas_call(functools.partial(filter_kernel, counts, wanted), grid=(sl...  12.8 us
    ppermute x8, starting transfers between devices, swap(): return lax.ppermute(value, 'chan', [(i, i ^ t) for i in range(chan_groups)])  11.8 us
    pallas_call x3, Pallas kernels, harmonic(): pl.pallas_call(functools.partial(harmonic_kernel, counts, family), grid=(...  10.3 us
    pallas_call x1, Pallas kernels, legendre(): pl.pallas_call(functools.partial(legendre_kernel, levels), in_specs=[pl.B...  9.42 us
  transfers between devices with their start and end apart: 16, of which 11 were waited for; matrix products, arithmetic and copies ran while one was open for 1% of the time, Pallas kernels for 15%

profile of v5, /device:TPU:0, one launch (start us, length us, event | category | flops | bytes accessed | tf_op | source)
XLA Modules:
  0.0 221.2 jit_solution(17483931872630800205)
XLA Ops:
  0.0 0.1 sine_multiply_fusion
  0.1 0.1 dynamic_slice.3.factor_ref
  0.1 0.0 copy-start.1
  0.1 0.7 copy-done.1
  0.8 5.6 %analysis.1 = bf16[128,16,128]{2,1,0:T(8,128)(2,1)} custom-call(f32[16]{0:T(128)S(1)} %dynamic_slice.3.factor_ref, s32[1,128]{1,0:T(1,128)S(1)} %bitcast.9, bf16[64,16,2048]{2,1,0:T(8,128)(2,1)} %sky_ref.1), custom_call_target="tpu_custom_call" | custom-call | tf_op jit(solution)/shard_map/analysis/pallas_call | solution.py:92
  6.4 3.0 %collective-permute-start = (bf16[8,16,16,128]{3,2,1,0:T(8,128)(2,1)}, bf16[8,16,16,128]{3,2,1,0:T(8,128)(2,1)}, u32[]{:S(2)}, u32[]{:S(2)}) collective-permute-start(bf16[8,16,16,128]{3,2,1,0:T(8,128)(2,1)} %bitcast.4), channel_id=1, source_target_pairs={{0,8},{8,0},{16,24},{24,16},{1,9},{9,1},{17,25},{25,17},{2,10},{10... | collective-permute-start | bytes 1572872 | tf_op jit(solution)/shard_map/ppermute | solution.py:459
  9.5 3.7 %all-to-all-start = ((bf16[8,16,16,128]{3,2,1,0:T(8,128)(2,1)}), bf16[8,16,16,128]{3,2,1,0:T(8,128)(2,1)S(1)}, u32[]{:S(2)}, u32[]{:S(2)}) async-start(bf16[8,16,16,128]{3,2,1,0:T(8,128)(2,1)} %bitcast.4), calls=%async_computation | async-start | bytes 1048576 | tf_op jit(solution)/shard_map/all_to_all | solution.py:462
  13.2 0.1 pad_add_fusion.1.first_ref
  13.3 0.0 copy-done.2
  13.3 0.1 add_multiply_fusion.log_ref
  13.3 0.0 copy-done.3
  13.4 9.4 %legendre.1 = (bf16[16,256,128]{2,1,0:T(8,128)(2,1)S(1)}, bf16[16,128,256]{2,1,0:T(8,128)(2,1)}) custom-call(s32[2]{0:T(128)S(1)} %pad_add_fusion.1.first_ref, s32[1024]{0:T(1024)S(1)} %copy-done.3, s32[128]{0:T(128)S(1)} %copy-done.2, f32[128]{0:T(128)S(1)} %add_multiply_fusion.log_ref), custom_call_target="tpu_custom_call" | custom-call | flops 40000000 | bytes 30000000 | tf_op jit(solution)/shard_map/legendre/pallas_call | solution.py:174
  22.8 1.0 copy-done.5
  23.7 0.0 all-to-all-done.refs_0_
  23.8 0.0 collective-permute-done
  23.8 4.2 %all-to-all-start.1 = ((bf16[8,16,16,128]{3,2,1,0:T(8,128)(2,1)}), bf16[8,16,16,128]{3,2,1,0:T(8,128)(2,1)S(1)}, u32[]{:S(2)}, u32[]{:S(2)}) async-start(bf16[8,16,16,128]{3,2,1,0:T(8,128)(2,1)} %collective-permute-done), calls=%async_computation.1 | async-start | bytes 1048576 | tf_op jit(solution)/shard_map/all_to_all | solution.py:462
  28.0 2.7 %collective-permute-start.1 = (bf16[4,16,16,128]{3,2,1,0:T(8,128)(2,1)S(1)}, bf16[4,16,16,128]{3,2,1,0:T(8,128)(2,1)S(1)}, u32[]{:S(2)}, u32[]{:S(2)}) collective-permute-start(bf16[4,16,16,128]{3,2,1,0:T(8,128)(2,1)S(1)} %get-tuple-element.64), channel_id=1, source_target_pairs={{0,16},{8,24},{16,0},{24,8},{1,17},{9,25},{17,1},{25,9},{2,18},{10... | collective-permute-start | bytes 786440 | tf_op jit(solution)/shard_map/ppermute | solution.py:459
  30.7 0.1 pad_add_fusion.low_ref
  30.7 3.0 %harmonic.3 = bf16[8,32,16,128]{3,2,1,0:T(8,128)(2,1)} custom-call(s32[2]{0:T(128)S(1)} %pad_add_fusion.low_ref, bf16[16,256,128]{2,1,0:T(8,128)(2,1)} %copy-done.5, bf16[8,16,16,128]{3,2,1,0:T(8,128)(2,1)S(1)} %all-to-all-done.refs_0_), custom_call_target="tpu_custom_call" | custom-call | flops 2000000000 | bytes 12000000 | tf_op jit(solution)/shard_map/harmonic/pallas_call | solution.py:235
  33.8 3.9 %all-to-all-done.1.refs_0_ = bf16[8,16,16,128]{3,2,1,0:T(8,128)(2,1)S(1)} async-done(((bf16[8,16,16,128]{3,2,1,0:T(8,128)(2,1)}), bf16[8,16,16,128]{3,2,1,0:T(8,128)(2,1)S(1)}, u32[]{:S(2)}, u32[]{:S(2)}) %all-to-all-start.1) | async-done | bytes 524320 | tf_op jit(solution)/shard_map/all_to_all | solution.py:462
  37.7 5.5 %collective-permute-done.1.refs_0_ = bf16[4,16,16,128]{3,2,1,0:T(8,128)(2,1)S(1)} collective-permute-done((bf16[4,16,16,128]{3,2,1,0:T(8,128)(2,1)S(1)}, bf16[4,16,16,128]{3,2,1,0:T(8,128)(2,1)S(1)}, u32[]{:S(2)}, u32[]{:S(2)}) %collective-permute-start.1) | collective-permute-done | bytes 262176 | tf_op jit(solution)/shard_map/ppermute | solution.py:459
  43.2 3.8 %all-to-all-start.2 = ((bf16[8,32,16,128]{3,2,1,0:T(8,128)(2,1)}), bf16[8,32,16,128]{3,2,1,0:T(8,128)(2,1)S(1)}, u32[]{:S(2)}, u32[]{:S(2)}) async-start(bf16[8,32,16,128]{3,2,1,0:T(8,128)(2,1)} %harmonic.3), calls=%async_computation.2 | async-start | bytes 2097152 | tf_op jit(solution)/shard_map/all_to_all | solution.py:462
  47.0 0.0 collective-permute-start.2
  47.0 3.1 %collective-permute-start.3 = (bf16[4,16,16,128]{3,2,1,0:T(8,128)(2,1)S(1)}, bf16[4,16,16,128]{3,2,1,0:T(8,128)(2,1)S(1)}, u32[]{:S(2)}, u32[]{:S(2)}) collective-permute-start(bf16[4,16,16,128]{3,2,1,0:T(8,128)(2,1)S(1)} %collective-permute-done.1.refs_0_), channel_id=1, source_target_pairs={{0,8},{8,0},{16,24},{24,16},{1,9},{9,1},{17,25},{25,17},{2,10},{10... | collective-permute-start | bytes 786440 | tf_op jit(solution)/shard_map/ppermute | solution.py:459
  50.2 3.1 %harmonic.4 = bf16[8,32,16,128]{3,2,1,0:T(8,128)(2,1)} custom-call(s32[2]{0:T(128)S(1)} %pad_add_fusion.low_ref, bf16[16,256,128]{2,1,0:T(8,128)(2,1)} %copy-done.5, bf16[8,16,16,128]{3,2,1,0:T(8,128)(2,1)S(1)} %all-to-all-done.1.refs_0_), custom_call_target="tpu_custom_call" | custom-call | flops 2000000000 | bytes 12000000 | tf_op jit(solution)/shard_map/harmonic/pallas_call | solution.py:235
  53.2 9.2 %all-to-all-done.2.refs_0_ = bf16[8,32,16,128]{3,2,1,0:T(8,128)(2,1)S(1)} async-done(((bf16[8,32,16,128]{3,2,1,0:T(8,128)(2,1)}), bf16[8,32,16,128]{3,2,1,0:T(8,128)(2,1)S(1)}, u32[]{:S(2)}, u32[]{:S(2)}) %all-to-all-start.2) | async-done | bytes 1048608 | tf_op jit(solution)/shard_map/all_to_all | solution.py:462
  62.4 0.0 collective-permute-done.2.refs_1_
  62.4 0.0 collective-permute-done.3.refs_2_
  62.5 3.8 %all-to-all-start.3 = ((bf16[8,32,16,128]{3,2,1,0:T(8,128)(2,1)}), bf16[8,32,16,128]{3,2,1,0:T(8,128)(2,1)S(1)}, u32[]{:S(2)}, u32[]{:S(2)}) async-start(bf16[8,32,16,128]{3,2,1,0:T(8,128)(2,1)} %harmonic.4), calls=%async_computation.3 | async-start | bytes 2097152 | tf_op jit(solution)/shard_map/all_to_all | solution.py:462
  66.3 0.0 collective-permute-start.4
  66.3 8.7 %collective-permute-done.4.refs_3_ = bf16[4,16,16,128]{3,2,1,0:T(8,128)(2,1)S(1)} collective-permute-done((bf16[4,16,16,128]{3,2,1,0:T(8,128)(2,1)S(1)}, bf16[4,16,16,128]{3,2,1,0:T(8,128)(2,1)S(1)}, u32[]{:S(2)}, u32[]{:S(2)}) %collective-permute-start.4) | collective-permute-done | bytes 262176 | tf_op jit(solution)/shard_map/ppermute | solution.py:459
  75.0 4.3 %harmonic.5 = bf16[8,32,16,256]{3,2,1,0:T(8,128)(2,1)} custom-call(s32[2]{0:T(128)S(1)} %pad_add_fusion.low_ref, bf16[16,256,128]{2,1,0:T(8,128)(2,1)} %copy-done.5, bf16[4,16,16,128]{3,2,1,0:T(8,128)(2,1)S(1)} %collective-permute-done.1.refs_0_, bf16[4,16,16,128]{3,2,1,0:T(8,128)(2,1)S(1)} %collective-permute-done.2.refs_1_, ...), custom_call_target="tpu_custom_call" | custom-call | flops 2000000000 | bytes 12000000 | tf_op jit(solution)/shard_map/harmonic/pallas_call | solution.py:235
  79.3 2.4 %all-to-all-done.3.refs_1_ = bf16[8,32,16,128]{3,2,1,0:T(8,128)(2,1)S(1)} async-done(((bf16[8,32,16,128]{3,2,1,0:T(8,128)(2,1)}), bf16[8,32,16,128]{3,2,1,0:T(8,128)(2,1)S(1)}, u32[]{:S(2)}, u32[]{:S(2)}) %all-to-all-start.3) | async-done | bytes 1048608 | tf_op jit(solution)/shard_map/all_to_all | solution.py:462
  81.7 30.9 %all_to_all.45.refs_2_ = bf16[8,32,16,256]{3,2,1,0:T(8,128)(2,1)} all-to-all(bf16[8,32,16,256]{3,2,1,0:T(8,128)(2,1)} %harmonic.5), channel_id=1, replica_groups=mesh['chan'=4,'blk'=8] {'blk'}, dimensions={0} | all-to-all | bytes 4194304 | tf_op jit(solution)/shard_map/all_to_all | solution.py:462
  112.6 0.0 copy-done
  112.6 0.0 copy-done.6
  112.6 5.5 %filters.2 = bf16[8,16,32,256]{3,2,1,0:T(8,128)(2,1)} custom-call(s32[2]{0:T(128)S(1)} %pad_add_fusion.low_ref, bf16[32,256,256]{2,1,0:T(8,128)(2,1)} %filters_ref.3, bf16[8,32,16,128]{3,2,1,0:T(8,128)(2,1)S(1)} %all-to-all-done.2.refs_0_, bf16[8,32,16,128]{3,2,1,0:T(8,128)(2,1)} %copy-done.6, bf16[8,32,16,256]{3,2,1,0:T(8,128)(2,1)} %all_to_all.45.refs_2_), custom_call_target="tpu_custom_call" | custom-call | flops 2000000000 | bytes 12000000 | tf_op jit(solution)/shard_map/filters/pallas_call | solution.py:300
  118.1 3.6 %all-to-all-start.6 = ((bf16[8,16,32,256]{3,2,1,0:T(8,128)(2,1)}), bf16[8,16,32,256]{3,2,1,0:T(8,128)(2,1)S(1)}, u32[]{:S(2)}, u32[]{:S(2)}) async-start(bf16[8,16,32,256]{3,2,1,0:T(8,128)(2,1)} %filters.2), calls=%async_computation.6 | async-start | bytes 4194304 | tf_op jit(solution)/shard_map/all_to_all | solution.py:462
  121.7 7.3 %filters.3 = (bf16[8,16,32,128]{3,2,1,0:T(8,128)(2,1)}, bf16[8,16,32,128]{3,2,1,0:T(8,128)(2,1)}) custom-call(s32[2]{0:T(128)S(1)} %pad_add_fusion.low_ref, bf16[32,256,256]{2,1,0:T(8,128)(2,1)} %filters_ref.3, bf16[8,32,16,128]{3,2,1,0:T(8,128)(2,1)} %copy-done, bf16[8,32,16,128]{3,2,1,0:T(8,128)(2,1)} %copy-done.6, bf16[8,32,16,256]{3,2,1,0:T(8,128)(2,1)} %all_to_all.45.refs_2_), custom_call_target="tpu_custom_call" | custom-call | flops 2000000000 | bytes 12000000 | tf_op jit(solution)/shard_map/filters/pallas_call | solution.py:300
  129.0 19.3 %all-to-all-done.6.filtered_ref = bf16[8,16,32,256]{3,2,1,0:T(8,128)(2,1)S(1)} async-done(((bf16[8,16,32,256]{3,2,1,0:T(8,128)(2,1)}), bf16[8,16,32,256]{3,2,1,0:T(8,128)(2,1)S(1)}, u32[]{:S(2)}, u32[]{:S(2)}) %all-to-all-start.6) | async-done | bytes 2097184 | tf_op jit(solution)/shard_map/all_to_all | solution.py:462
  148.3 3.6 %all-to-all-start.7 = ((bf16[8,16,32,128]{3,2,1,0:T(8,128)(2,1)}), bf16[8,16,32,128]{3,2,1,0:T(8,128)(2,1)S(1)}, u32[]{:S(2)}, u32[]{:S(2)}) async-start(bf16[8,16,32,128]{3,2,1,0:T(8,128)(2,1)} %get-tuple-element.62), calls=%async_computation.7 | async-start | bytes 2097152 | tf_op jit(solution)/shard_map/all_to_all | solution.py:462
  151.9 0.0 copy-done.7
  151.9 2.6 %cycles.4 = (bf16[8,16,16,128]{3,2,1,0:T(8,128)(2,1)S(1)}, bf16[8,16,16,128]{3,2,1,0:T(8,128)(2,1)S(1)}) custom-call(s32[2]{0:T(128)S(1)} %pad_add_fusion.low_ref, bf16[16,128,256]{2,1,0:T(8,128)(2,1)} %get-tuple-element.57.turned_ref, bf16[8,16,32,256]{3,2,1,0:T(8,128)(2,1)} %copy-done.7), custom_call_target="tpu_custom_call" | custom-call | flops 2000000000 | bytes 12000000 | tf_op jit(solution)/shard_map/cycles/pallas_call | solution.py:347
  154.5 0.0 copy-start.4
  154.5 0.1 collective-permute-start.5
  154.6 12.6 %all-to-all-done.7.filtered_ref = bf16[8,16,32,128]{3,2,1,0:T(8,128)(2,1)S(1)} async-done(((bf16[8,16,32,128]{3,2,1,0:T(8,128)(2,1)}), bf16[8,16,32,128]{3,2,1,0:T(8,128)(2,1)S(1)}, u32[]{:S(2)}, u32[]{:S(2)}) %all-to-all-start.7) | async-done | bytes 1048608 | tf_op jit(solution)/shard_map/all_to_all | solution.py:462
  167.2 1.0 copy-done.8
  168.2 4.4 %all-to-all-start.5 = ((bf16[8,16,32,128]{3,2,1,0:T(8,128)(2,1)}), bf16[8,16,32,128]{3,2,1,0:T(8,128)(2,1)}, u32[]{:S(2)}, u32[]{:S(2)}) async-start(bf16[8,16,32,128]{3,2,1,0:T(8,128)(2,1)} %get-tuple-element.58), calls=%async_computation.5 | async-start | bytes 2097152 | tf_op jit(solution)/shard_map/all_to_all | solution.py:462
  172.6 0.0 copy-done.4
  172.6 1.7 cycles.5
  174.3 0.1 collective-permute-start.7
  174.4 0.0 collective-permute-done.5
  174.4 1.2 add_convert_fusion.1
  175.6 2.8 %collective-permute-start.6 = (bf16[8,16,16,128]{3,2,1,0:T(8,128)(2,1)S(1)}, bf16[8,16,16,128]{3,2,1,0:T(8,128)(2,1)}, u32[]{:S(2)}, u32[]{:S(2)}) collective-permute-start(bf16[8,16,16,128]{3,2,1,0:T(8,128)(2,1)S(1)} %add_convert_fusion.1), channel_id=1, source_target_pairs={{0,16},{8,24},{16,0},{24,8},{1,17},{9,25},{17,1},{25,9},{2,18},{10... | collective-permute-start | bytes 1572872 | tf_op jit(solution)/shard_map/ppermute | solution.py:459
  178.4 9.4 %all-to-all-done.5.filtered_ref = bf16[8,16,32,128]{3,2,1,0:T(8,128)(2,1)} async-done(((bf16[8,16,32,128]{3,2,1,0:T(8,128)(2,1)}), bf16[8,16,32,128]{3,2,1,0:T(8,128)(2,1)}, u32[]{:S(2)}, u32[]{:S(2)}) %all-to-all-start.5) | async-done | bytes 1048608 | tf_op jit(solution)/shard_map/all_to_all | solution.py:462
  187.9 1.7 cycles.3
  189.5 8.5 %collective-permute-done.7 = bf16[8,16,16,128]{3,2,1,0:T(8,128)(2,1)S(1)} collective-permute-done((bf16[8,16,16,128]{3,2,1,0:T(8,128)(2,1)S(1)}, bf16[8,16,16,128]{3,2,1,0:T(8,128)(2,1)S(1)}, u32[]{:S(2)}, u32[]{:S(2)}) %collective-permute-start.7) | collective-permute-done | bytes 524320 | tf_op jit(solution)/shard_map/ppermute | solution.py:459
  198.0 3.9 %collective-permute-done.6 = bf16[8,16,16,128]{3,2,1,0:T(8,128)(2,1)} collective-permute-done((bf16[8,16,16,128]{3,2,1,0:T(8,128)(2,1)S(1)}, bf16[8,16,16,128]{3,2,1,0:T(8,128)(2,1)}, u32[]{:S(2)}, u32[]{:S(2)}) %collective-permute-start.6) | collective-permute-done | bytes 524320 | tf_op jit(solution)/shard_map/ppermute | solution.py:459
  202.0 2.0 add_convert_fusion
  204.0 3.9 %all-to-all-start.8 = ((bf16[8,16,16,128]{3,2,1,0:T(8,128)(2,1)}), bf16[8,16,16,128]{3,2,1,0:T(8,128)(2,1)S(1)}, u32[]{:S(2)}, u32[]{:S(2)}) async-start(bf16[8,16,16,128]{3,2,1,0:T(8,128)(2,1)} %add_convert_fusion), calls=%async_computation.8 | async-start | bytes 1048576 | tf_op jit(solution)/shard_map/all_to_all | solution.py:521
  207.9 0.1 copy.5.modes_ref
  208.0 1.1 phases.1.phase_ref
  209.1 8.5 %all-to-all-done.8 = bf16[8,16,16,128]{3,2,1,0:T(8,128)(2,1)S(1)} async-done(((bf16[8,16,16,128]{3,2,1,0:T(8,128)(2,1)}), bf16[8,16,16,128]{3,2,1,0:T(8,128)(2,1)S(1)}, u32[]{:S(2)}, u32[]{:S(2)}) %all-to-all-start.8) | async-done | bytes 524320 | tf_op jit(solution)/shard_map/all_to_all | solution.py:521
  217.6 3.4 %synthesis.1 = bf16[64,16,2048]{2,1,0:T(8,128)(2,1)} custom-call(bf16[256,2048]{1,0:T(8,128)(2,1)S(1)} %phases.1.phase_ref, bf16[128,16,128]{2,1,0:T(8,128)(2,1)S(1)} %bitcast.8), custom_call_target="tpu_custom_call" | custom-call | tf_op jit(solution)/shard_map/synthesis/pallas_call | solution.py:424
  (8 shorter events, 0.0 us)
Async XLA Ops:
  0.1 0.7 copy-start.1
  0.8 12.5 %copy-start.2 = (s32[128]{0:T(128)S(1)}, s32[128]{0:T(128)}, u32[]{:S(2)}) copy-start(s32[128]{0:T(128)} %band_ref.1) | copy-start | bytes 1540
  0.8 12.6 %copy-start.3 = (s32[1024]{0:T(1024)S(1)}, s32[1024]{0:T(1024)}, u32[]{:S(2)}) copy-start(s32[1024]{0:T(1024)} %degree_ref.1) | copy-start | bytes 12292
  6.4 17.3 %collective-permute-start = (bf16[8,16,16,128]{3,2,1,0:T(8,128)(2,1)}, bf16[8,16,16,128]{3,2,1,0:T(8,128)(2,1)}, u32[]{:S(2)}, u32[]{:S(2)}) collective-permute-start(bf16[8,16,16,128]{3,2,1,0:T(8,128)(2,1)} %bitcast.4), channel_id=1, source_target_pairs={{0,8},{8,0},{16,24},{24,16},{1,9},{9,1},{17,25},{25,17},{2,10},{10... | collective-permute-start | bytes 1572872 | tf_op jit(solution)/shard_map/ppermute | solution.py:459
  9.5 14.3 %all-to-all-start = ((bf16[8,16,16,128]{3,2,1,0:T(8,128)(2,1)}), bf16[8,16,16,128]{3,2,1,0:T(8,128)(2,1)S(1)}, u32[]{:S(2)}, u32[]{:S(2)}) async-start(bf16[8,16,16,128]{3,2,1,0:T(8,128)(2,1)} %bitcast.4), calls=%async_computation | async-start | bytes 1048576 | tf_op jit(solution)/shard_map/all_to_all | solution.py:462
  22.8 1.0 copy-start.5
  23.8 13.9 %all-to-all-start.1 = ((bf16[8,16,16,128]{3,2,1,0:T(8,128)(2,1)}), bf16[8,16,16,128]{3,2,1,0:T(8,128)(2,1)S(1)}, u32[]{:S(2)}, u32[]{:S(2)}) async-start(bf16[8,16,16,128]{3,2,1,0:T(8,128)(2,1)} %collective-permute-done), calls=%async_computation.1 | async-start | bytes 1048576 | tf_op jit(solution)/shard_map/all_to_all | solution.py:462
  28.0 15.2 %collective-permute-start.1 = (bf16[4,16,16,128]{3,2,1,0:T(8,128)(2,1)S(1)}, bf16[4,16,16,128]{3,2,1,0:T(8,128)(2,1)S(1)}, u32[]{:S(2)}, u32[]{:S(2)}) collective-permute-start(bf16[4,16,16,128]{3,2,1,0:T(8,128)(2,1)S(1)} %get-tuple-element.64), channel_id=1, source_target_pairs={{0,16},{8,24},{16,0},{24,8},{1,17},{9,25},{17,1},{25,9},{2,18},{10... | collective-permute-start | bytes 786440 | tf_op jit(solution)/shard_map/ppermute | solution.py:459
  43.2 19.3 %all-to-all-start.2 = ((bf16[8,32,16,128]{3,2,1,0:T(8,128)(2,1)}), bf16[8,32,16,128]{3,2,1,0:T(8,128)(2,1)S(1)}, u32[]{:S(2)}, u32[]{:S(2)}) async-start(bf16[8,32,16,128]{3,2,1,0:T(8,128)(2,1)} %harmonic.3), calls=%async_computation.2 | async-start | bytes 2097152 | tf_op jit(solution)/shard_map/all_to_all | solution.py:462
  47.0 15.4 %collective-permute-start.2 = (bf16[4,16,16,128]{3,2,1,0:T(8,128)(2,1)S(1)}, bf16[4,16,16,128]{3,2,1,0:T(8,128)(2,1)S(1)}, u32[]{:S(2)}, u32[]{:S(2)}) collective-permute-start(bf16[4,16,16,128]{3,2,1,0:T(8,128)(2,1)S(1)} %get-tuple-element.63), channel_id=1, source_target_pairs={{0,16},{8,24},{16,0},{24,8},{1,17},{9,25},{17,1},{25,9},{2,18},{10... | collective-permute-start | bytes 786440 | tf_op jit(solution)/shard_map/ppermute | solution.py:459
  47.0 15.4 %collective-permute-start.3 = (bf16[4,16,16,128]{3,2,1,0:T(8,128)(2,1)S(1)}, bf16[4,16,16,128]{3,2,1,0:T(8,128)(2,1)S(1)}, u32[]{:S(2)}, u32[]{:S(2)}) collective-permute-start(bf16[4,16,16,128]{3,2,1,0:T(8,128)(2,1)S(1)} %collective-permute-done.1.refs_0_), channel_id=1, source_target_pairs={{0,8},{8,0},{16,24},{24,16},{1,9},{9,1},{17,25},{25,17},{2,10},{10... | collective-permute-start | bytes 786440 | tf_op jit(solution)/shard_map/ppermute | solution.py:459
  62.4 50.2 %copy-start = (bf16[8,32,16,128]{3,2,1,0:T(8,128)(2,1)}, bf16[8,32,16,128]{3,2,1,0:T(8,128)(2,1)S(1)}, u32[]{:S(2)}) copy-start(bf16[8,32,16,128]{3,2,1,0:T(8,128)(2,1)S(1)} %all-to-all-done.2.refs_0_) | copy-start | bytes 3145732
  62.5 19.3 %all-to-all-start.3 = ((bf16[8,32,16,128]{3,2,1,0:T(8,128)(2,1)}), bf16[8,32,16,128]{3,2,1,0:T(8,128)(2,1)S(1)}, u32[]{:S(2)}, u32[]{:S(2)}) async-start(bf16[8,32,16,128]{3,2,1,0:T(8,128)(2,1)} %harmonic.4), calls=%async_computation.3 | async-start | bytes 2097152 | tf_op jit(solution)/shard_map/all_to_all | solution.py:462
  66.3 8.7 %collective-permute-start.4 = (bf16[4,16,16,128]{3,2,1,0:T(8,128)(2,1)S(1)}, bf16[4,16,16,128]{3,2,1,0:T(8,128)(2,1)S(1)}, u32[]{:S(2)}, u32[]{:S(2)}) collective-permute-start(bf16[4,16,16,128]{3,2,1,0:T(8,128)(2,1)S(1)} %collective-permute-done.2.refs_1_), channel_id=1, source_target_pairs={{0,8},{8,0},{16,24},{24,16},{1,9},{9,1},{17,25},{25,17},{2,10},{10... | collective-permute-start | bytes 786440 | tf_op jit(solution)/shard_map/ppermute | solution.py:459
  81.7 30.9 %copy-start.6 = (bf16[8,32,16,128]{3,2,1,0:T(8,128)(2,1)}, bf16[8,32,16,128]{3,2,1,0:T(8,128)(2,1)S(1)}, u32[]{:S(2)}) copy-start(bf16[8,32,16,128]{3,2,1,0:T(8,128)(2,1)S(1)} %all-to-all-done.3.refs_1_) | copy-start | bytes 3145732
  118.1 30.2 %all-to-all-start.6 = ((bf16[8,16,32,256]{3,2,1,0:T(8,128)(2,1)}), bf16[8,16,32,256]{3,2,1,0:T(8,128)(2,1)S(1)}, u32[]{:S(2)}, u32[]{:S(2)}) async-start(bf16[8,16,32,256]{3,2,1,0:T(8,128)(2,1)} %filters.2), calls=%async_computation.6 | async-start | bytes 4194304 | tf_op jit(solution)/shard_map/all_to_all | solution.py:462
  148.3 3.6 %copy-start.7 = (bf16[8,16,32,256]{3,2,1,0:T(8,128)(2,1)}, bf16[8,16,32,256]{3,2,1,0:T(8,128)(2,1)S(1)}, u32[]{:S(2)}) copy-start(bf16[8,16,32,256]{3,2,1,0:T(8,128)(2,1)S(1)} %all-to-all-done.6.filtered_ref) | copy-start | bytes 6291460
  148.3 18.9 %all-to-all-start.7 = ((bf16[8,16,32,128]{3,2,1,0:T(8,128)(2,1)}), bf16[8,16,32,128]{3,2,1,0:T(8,128)(2,1)S(1)}, u32[]{:S(2)}, u32[]{:S(2)}) async-start(bf16[8,16,32,128]{3,2,1,0:T(8,128)(2,1)} %get-tuple-element.62), calls=%async_computation.7 | async-start | bytes 2097152 | tf_op jit(solution)/shard_map/all_to_all | solution.py:462
  154.5 18.1 %copy-start.4 = (bf16[16,128,256]{2,1,0:T(8,128)(2,1)S(1)}, bf16[16,128,256]{2,1,0:T(8,128)(2,1)}, u32[]{:S(2)}) copy-start(bf16[16,128,256]{2,1,0:T(8,128)(2,1)} %get-tuple-element.57.turned_ref) | copy-start | bytes 3145732
  154.5 19.9 %collective-permute-start.5 = (bf16[8,16,16,128]{3,2,1,0:T(8,128)(2,1)S(1)}, bf16[8,16,16,128]{3,2,1,0:T(8,128)(2,1)}, u32[]{:S(2)}, u32[]{:S(2)}) collective-permute-start(bf16[8,16,16,128]{3,2,1,0:T(8,128)(2,1)S(1)} %get-tuple-element.61), channel_id=1, source_target_pairs={{0,8},{8,0},{16,24},{24,16},{1,9},{9,1},{17,25},{25,17},{2,10},{10... | collective-permute-start | bytes 1572872 | tf_op jit(solution)/shard_map/ppermute | solution.py:459
  167.2 1.0 copy-start.8
  168.2 19.7 %all-to-all-start.5 = ((bf16[8,16,32,128]{3,2,1,0:T(8,128)(2,1)}), bf16[8,16,32,128]{3,2,1,0:T(8,128)(2,1)}, u32[]{:S(2)}, u32[]{:S(2)}) async-start(bf16[8,16,32,128]{3,2,1,0:T(8,128)(2,1)} %get-tuple-element.58), calls=%async_computation.5 | async-start | bytes 2097152 | tf_op jit(solution)/shard_map/all_to_all | solution.py:462
  174.3 23.7 %collective-permute-start.7 = (bf16[8,16,16,128]{3,2,1,0:T(8,128)(2,1)S(1)}, bf16[8,16,16,128]{3,2,1,0:T(8,128)(2,1)S(1)}, u32[]{:S(2)}, u32[]{:S(2)}) collective-permute-start(bf16[8,16,16,128]{3,2,1,0:T(8,128)(2,1)S(1)} %cycles.5), channel_id=1, source_target_pairs={{0,8},{8,0},{16,24},{24,16},{1,9},{9,1},{17,25},{25,17},{2,10},{10... | collective-permute-start | bytes 1572872 | tf_op jit(solution)/shard_map/ppermute | solution.py:459
  175.6 26.4 %collective-permute-start.6 = (bf16[8,16,16,128]{3,2,1,0:T(8,128)(2,1)S(1)}, bf16[8,16,16,128]{3,2,1,0:T(8,128)(2,1)}, u32[]{:S(2)}, u32[]{:S(2)}) collective-permute-start(bf16[8,16,16,128]{3,2,1,0:T(8,128)(2,1)S(1)} %add_convert_fusion.1), channel_id=1, source_target_pairs={{0,16},{8,24},{16,0},{24,8},{1,17},{9,25},{17,1},{25,9},{2,18},{10... | collective-permute-start | bytes 1572872 | tf_op jit(solution)/shard_map/ppermute | solution.py:459
  204.0 13.6 %all-to-all-start.8 = ((bf16[8,16,16,128]{3,2,1,0:T(8,128)(2,1)}), bf16[8,16,16,128]{3,2,1,0:T(8,128)(2,1)S(1)}, u32[]{:S(2)}, u32[]{:S(2)}) async-start(bf16[8,16,16,128]{3,2,1,0:T(8,128)(2,1)} %add_convert_fusion), calls=%async_computation.8 | async-start | bytes 1048576 | tf_op jit(solution)/shard_map/all_to_all | solution.py:521

commit v6 on v5

--- a/solution.py
+++ b/solution.py
@@ -342,12 +342,18 @@
 def to_cycles(low, turned, filtered, scale, blocks, parts):
     modes, cycle_total, slots = turned.shape
     width = filtered.shape[3]
-    vmem = pl.BlockSpec(memory_space=pltpu.VMEM)
+    groups, slot_dev = filtered.shape[0], filtered.shape[2]
+    steps = divisor(modes, 2)
     shape = (blocks, modes, cycle_total // blocks, width // parts)
     return pl.pallas_call(
         functools.partial(cycles_kernel, scale),
-        in_specs=[pl.BlockSpec(memory_space=pltpu.SMEM), vmem, vmem],
-        out_specs=[vmem] * parts,
+        grid=(steps,),
+        in_specs=[
+            pl.BlockSpec(memory_space=pltpu.SMEM),
+            pl.BlockSpec((modes // steps, cycle_total, slots), lambda i: (i, 0, 0)),
+            pl.BlockSpec((groups, modes // steps, slot_dev, width), lambda i: (0, i, 0, 0)),
+        ],
+        out_specs=[pl.BlockSpec((blocks, modes // steps) + shape[2:], lambda i: (0, i, 0, 0))] * parts,
         out_shape=[jax.ShapeDtypeStruct(shape, BF16)] * parts,
         compiler_params=params(),
         cost_estimate=COST,

time: 222 us -> 222 us (level)
  no operation moved by 1% of the time
where the time goes in v6:
time: 222 us; the launch traced here: 221 us
  waiting for transfers between devices  92.2 us (42%)
  Pallas kernels  48.6 us (22%)
  starting transfers between devices  42.9 us (19%)
  blocking collectives  30.9 us (14%)
  other arithmetic  3.5 us (2%)
  local copies, waits for them, and re-layouts  2.84 us (1%)
    all_to_all x7, waiting for transfers between devices, exchange(): return lax.all_to_all(value, 'blk', split_axis=0, concat_axis=0, tiled=True)  57.1 us
    all_to_all x1, blocking collectives, exchange(): return lax.all_to_all(value, 'blk', split_axis=0, concat_axis=0, tiled=True)  30.9 us
    all_to_all x7, starting transfers between devices, exchange(): return lax.all_to_all(value, 'blk', split_axis=0, concat_axis=0, tiled=True)  27.2 us
    ppermute x8, waiting for transfers between devices, swap(): return lax.ppermute(value, 'chan', [(i, i ^ t) for i in range(chan_groups)])  26.6 us
    pallas_call x2, Pallas kernels, apply_filters(): pl.pallas_call(functools.partial(filter_kernel, counts, wanted), grid=(sl...  12.8 us
    ppermute x8, starting transfers between devices, swap(): return lax.ppermute(value, 'chan', [(i, i ^ t) for i in range(chan_groups)])  11.8 us
    pallas_call x3, Pallas kernels, harmonic(): pl.pallas_call(functools.partial(harmonic_kernel, counts, family), grid=(...  10.3 us
    pallas_call x1, Pallas kernels, legendre(): pl.pallas_call(functools.partial(legendre_kernel, levels), in_specs=[pl.B...  9.42 us
  transfers between devices with their start and end apart: 16, of which 11 were waited for; matrix products, arithmetic and copies ran while one was open for 1% of the time, Pallas kernels for 15%

profile of v6, /device:TPU:0, one launch (start us, length us, event | category | flops | bytes accessed | tf_op | source)
XLA Modules:
  0.0 221.3 jit_solution(16837798460565280084)
XLA Ops:
  0.0 0.1 sine_multiply_fusion
  0.1 0.1 dynamic_slice.3.factor_ref
  0.1 0.0 copy-start.1
  0.1 0.7 copy-done.1
  0.8 5.6 %analysis.1 = bf16[128,16,128]{2,1,0:T(8,128)(2,1)} custom-call(f32[16]{0:T(128)S(1)} %dynamic_slice.3.factor_ref, s32[1,128]{1,0:T(1,128)S(1)} %bitcast.9, bf16[64,16,2048]{2,1,0:T(8,128)(2,1)} %sky_ref.1), custom_call_target="tpu_custom_call" | custom-call | tf_op jit(solution)/shard_map/analysis/pallas_call | solution.py:92
  6.4 3.0 %collective-permute-start = (bf16[8,16,16,128]{3,2,1,0:T(8,128)(2,1)}, bf16[8,16,16,128]{3,2,1,0:T(8,128)(2,1)}, u32[]{:S(2)}, u32[]{:S(2)}) collective-permute-start(bf16[8,16,16,128]{3,2,1,0:T(8,128)(2,1)} %bitcast.4), channel_id=1, source_target_pairs={{0,8},{8,0},{16,24},{24,16},{1,9},{9,1},{17,25},{25,17},{2,10},{10... | collective-permute-start | bytes 1572872 | tf_op jit(solution)/shard_map/ppermute | solution.py:465
  9.5 3.7 %all-to-all-start = ((bf16[8,16,16,128]{3,2,1,0:T(8,128)(2,1)}), bf16[8,16,16,128]{3,2,1,0:T(8,128)(2,1)S(1)}, u32[]{:S(2)}, u32[]{:S(2)}) async-start(bf16[8,16,16,128]{3,2,1,0:T(8,128)(2,1)} %bitcast.4), calls=%async_computation | async-start | bytes 1048576 | tf_op jit(solution)/shard_map/all_to_all | solution.py:468
  13.2 0.1 pad_add_fusion.1.first_ref
  13.3 0.0 copy-done.2
  13.3 0.1 add_multiply_fusion.log_ref
  13.3 0.0 copy-done.3
  13.4 9.4 %legendre.1 = (bf16[16,256,128]{2,1,0:T(8,128)(2,1)S(1)}, bf16[16,128,256]{2,1,0:T(8,128)(2,1)}) custom-call(s32[2]{0:T(128)S(1)} %pad_add_fusion.1.first_ref, s32[1024]{0:T(1024)S(1)} %copy-done.3, s32[128]{0:T(128)S(1)} %copy-done.2, f32[128]{0:T(128)S(1)} %add_multiply_fusion.log_ref), custom_call_target="tpu_custom_call" | custom-call | flops 40000000 | bytes 30000000 | tf_op jit(solution)/shard_map/legendre/pallas_call | solution.py:174
  22.8 1.0 copy-done.5
  23.7 0.0 all-to-all-done.refs_0_
  23.8 0.0 collective-permute-done
  23.8 4.2 %all-to-all-start.1 = ((bf16[8,16,16,128]{3,2,1,0:T(8,128)(2,1)}), bf16[8,16,16,128]{3,2,1,0:T(8,128)(2,1)S(1)}, u32[]{:S(2)}, u32[]{:S(2)}) async-start(bf16[8,16,16,128]{3,2,1,0:T(8,128)(2,1)} %collective-permute-done), calls=%async_computation.1 | async-start | bytes 1048576 | tf_op jit(solution)/shard_map/all_to_all | solution.py:468
  28.0 2.7 %collective-permute-start.1 = (bf16[4,16,16,128]{3,2,1,0:T(8,128)(2,1)S(1)}, bf16[4,16,16,128]{3,2,1,0:T(8,128)(2,1)S(1)}, u32[]{:S(2)}, u32[]{:S(2)}) collective-permute-start(bf16[4,16,16,128]{3,2,1,0:T(8,128)(2,1)S(1)} %get-tuple-element.64), channel_id=1, source_target_pairs={{0,16},{8,24},{16,0},{24,8},{1,17},{9,25},{17,1},{25,9},{2,18},{10... | collective-permute-start | bytes 786440 | tf_op jit(solution)/shard_map/ppermute | solution.py:465
  30.7 0.1 pad_add_fusion.low_ref
  30.7 3.0 %harmonic.3 = bf16[8,32,16,128]{3,2,1,0:T(8,128)(2,1)} custom-call(s32[2]{0:T(128)S(1)} %pad_add_fusion.low_ref, bf16[16,256,128]{2,1,0:T(8,128)(2,1)} %copy-done.5, bf16[8,16,16,128]{3,2,1,0:T(8,128)(2,1)S(1)} %all-to-all-done.refs_0_), custom_call_target="tpu_custom_call" | custom-call | flops 2000000000 | bytes 12000000 | tf_op jit(solution)/shard_map/harmonic/pallas_call | solution.py:235
  33.8 3.9 %all-to-all-done.1.refs_0_ = bf16[8,16,16,128]{3,2,1,0:T(8,128)(2,1)S(1)} async-done(((bf16[8,16,16,128]{3,2,1,0:T(8,128)(2,1)}), bf16[8,16,16,128]{3,2,1,0:T(8,128)(2,1)S(1)}, u32[]{:S(2)}, u32[]{:S(2)}) %all-to-all-start.1) | async-done | bytes 524320 | tf_op jit(solution)/shard_map/all_to_all | solution.py:468
  37.7 5.5 %collective-permute-done.1.refs_0_ = bf16[4,16,16,128]{3,2,1,0:T(8,128)(2,1)S(1)} collective-permute-done((bf16[4,16,16,128]{3,2,1,0:T(8,128)(2,1)S(1)}, bf16[4,16,16,128]{3,2,1,0:T(8,128)(2,1)S(1)}, u32[]{:S(2)}, u32[]{:S(2)}) %collective-permute-start.1) | collective-permute-done | bytes 262176 | tf_op jit(solution)/shard_map/ppermute | solution.py:465
  43.2 3.8 %all-to-all-start.2 = ((bf16[8,32,16,128]{3,2,1,0:T(8,128)(2,1)}), bf16[8,32,16,128]{3,2,1,0:T(8,128)(2,1)S(1)}, u32[]{:S(2)}, u32[]{:S(2)}) async-start(bf16[8,32,16,128]{3,2,1,0:T(8,128)(2,1)} %harmonic.3), calls=%async_computation.2 | async-start | bytes 2097152 | tf_op jit(solution)/shard_map/all_to_all | solution.py:468
  47.0 0.0 collective-permute-start.2
  47.0 3.1 %collective-permute-start.3 = (bf16[4,16,16,128]{3,2,1,0:T(8,128)(2,1)S(1)}, bf16[4,16,16,128]{3,2,1,0:T(8,128)(2,1)S(1)}, u32[]{:S(2)}, u32[]{:S(2)}) collective-permute-start(bf16[4,16,16,128]{3,2,1,0:T(8,128)(2,1)S(1)} %collective-permute-done.1.refs_0_), channel_id=1, source_target_pairs={{0,8},{8,0},{16,24},{24,16},{1,9},{9,1},{17,25},{25,17},{2,10},{10... | collective-permute-start | bytes 786440 | tf_op jit(solution)/shard_map/ppermute | solution.py:465
  50.2 3.1 %harmonic.4 = bf16[8,32,16,128]{3,2,1,0:T(8,128)(2,1)} custom-call(s32[2]{0:T(128)S(1)} %pad_add_fusion.low_ref, bf16[16,256,128]{2,1,0:T(8,128)(2,1)} %copy-done.5, bf16[8,16,16,128]{3,2,1,0:T(8,128)(2,1)S(1)} %all-to-all-done.1.refs_0_), custom_call_target="tpu_custom_call" | custom-call | flops 2000000000 | bytes 12000000 | tf_op jit(solution)/shard_map/harmonic/pallas_call | solution.py:235
  53.2 9.2 %all-to-all-done.2.refs_0_ = bf16[8,32,16,128]{3,2,1,0:T(8,128)(2,1)S(1)} async-done(((bf16[8,32,16,128]{3,2,1,0:T(8,128)(2,1)}), bf16[8,32,16,128]{3,2,1,0:T(8,128)(2,1)S(1)}, u32[]{:S(2)}, u32[]{:S(2)}) %all-to-all-start.2) | async-done | bytes 1048608 | tf_op jit(solution)/shard_map/all_to_all | solution.py:468
  62.4 0.0 collective-permute-done.2.refs_1_
  62.4 0.0 collective-permute-done.3.refs_2_
  62.5 3.8 %all-to-all-start.3 = ((bf16[8,32,16,128]{3,2,1,0:T(8,128)(2,1)}), bf16[8,32,16,128]{3,2,1,0:T(8,128)(2,1)S(1)}, u32[]{:S(2)}, u32[]{:S(2)}) async-start(bf16[8,32,16,128]{3,2,1,0:T(8,128)(2,1)} %harmonic.4), calls=%async_computation.3 | async-start | bytes 2097152 | tf_op jit(solution)/shard_map/all_to_all | solution.py:468
  66.3 0.0 collective-permute-start.4
  66.3 8.7 %collective-permute-done.4.refs_3_ = bf16[4,16,16,128]{3,2,1,0:T(8,128)(2,1)S(1)} collective-permute-done((bf16[4,16,16,128]{3,2,1,0:T(8,128)(2,1)S(1)}, bf16[4,16,16,128]{3,2,1,0:T(8,128)(2,1)S(1)}, u32[]{:S(2)}, u32[]{:S(2)}) %collective-permute-start.4) | collective-permute-done | bytes 262176 | tf_op jit(solution)/shard_map/ppermute | solution.py:465
  75.0 4.3 %harmonic.5 = bf16[8,32,16,256]{3,2,1,0:T(8,128)(2,1)} custom-call(s32[2]{0:T(128)S(1)} %pad_add_fusion.low_ref, bf16[16,256,128]{2,1,0:T(8,128)(2,1)} %copy-done.5, bf16[4,16,16,128]{3,2,1,0:T(8,128)(2,1)S(1)} %collective-permute-done.1.refs_0_, bf16[4,16,16,128]{3,2,1,0:T(8,128)(2,1)S(1)} %collective-permute-done.2.refs_1_, ...), custom_call_target="tpu_custom_call" | custom-call | flops 2000000000 | bytes 12000000 | tf_op jit(solution)/shard_map/harmonic/pallas_call | solution.py:235
  79.3 2.4 %all-to-all-done.3.refs_1_ = bf16[8,32,16,128]{3,2,1,0:T(8,128)(2,1)S(1)} async-done(((bf16[8,32,16,128]{3,2,1,0:T(8,128)(2,1)}), bf16[8,32,16,128]{3,2,1,0:T(8,128)(2,1)S(1)}, u32[]{:S(2)}, u32[]{:S(2)}) %all-to-all-start.3) | async-done | bytes 1048608 | tf_op jit(solution)/shard_map/all_to_all | solution.py:468
  81.7 30.9 %all_to_all.45.refs_2_ = bf16[8,32,16,256]{3,2,1,0:T(8,128)(2,1)} all-to-all(bf16[8,32,16,256]{3,2,1,0:T(8,128)(2,1)} %harmonic.5), channel_id=1, replica_groups=mesh['chan'=4,'blk'=8] {'blk'}, dimensions={0} | all-to-all | bytes 4194304 | tf_op jit(solution)/shard_map/all_to_all | solution.py:468
  112.6 0.0 copy-done
  112.6 0.0 copy-done.6
  112.6 5.5 %filters.2 = bf16[8,16,32,256]{3,2,1,0:T(8,128)(2,1)} custom-call(s32[2]{0:T(128)S(1)} %pad_add_fusion.low_ref, bf16[32,256,256]{2,1,0:T(8,128)(2,1)} %filters_ref.3, bf16[8,32,16,128]{3,2,1,0:T(8,128)(2,1)S(1)} %all-to-all-done.2.refs_0_, bf16[8,32,16,128]{3,2,1,0:T(8,128)(2,1)} %copy-done.6, bf16[8,32,16,256]{3,2,1,0:T(8,128)(2,1)} %all_to_all.45.refs_2_), custom_call_target="tpu_custom_call" | custom-call | flops 2000000000 | bytes 12000000 | tf_op jit(solution)/shard_map/filters/pallas_call | solution.py:300
  118.1 3.6 %all-to-all-start.6 = ((bf16[8,16,32,256]{3,2,1,0:T(8,128)(2,1)}), bf16[8,16,32,256]{3,2,1,0:T(8,128)(2,1)S(1)}, u32[]{:S(2)}, u32[]{:S(2)}) async-start(bf16[8,16,32,256]{3,2,1,0:T(8,128)(2,1)} %filters.2), calls=%async_computation.6 | async-start | bytes 4194304 | tf_op jit(solution)/shard_map/all_to_all | solution.py:468
  121.7 7.3 %filters.3 = (bf16[8,16,32,128]{3,2,1,0:T(8,128)(2,1)}, bf16[8,16,32,128]{3,2,1,0:T(8,128)(2,1)}) custom-call(s32[2]{0:T(128)S(1)} %pad_add_fusion.low_ref, bf16[32,256,256]{2,1,0:T(8,128)(2,1)} %filters_ref.3, bf16[8,32,16,128]{3,2,1,0:T(8,128)(2,1)} %copy-done, bf16[8,32,16,128]{3,2,1,0:T(8,128)(2,1)} %copy-done.6, bf16[8,32,16,256]{3,2,1,0:T(8,128)(2,1)} %all_to_all.45.refs_2_), custom_call_target="tpu_custom_call" | custom-call | flops 2000000000 | bytes 12000000 | tf_op jit(solution)/shard_map/filters/pallas_call | solution.py:300
  129.0 19.3 %all-to-all-done.6.filtered_ref = bf16[8,16,32,256]{3,2,1,0:T(8,128)(2,1)S(1)} async-done(((bf16[8,16,32,256]{3,2,1,0:T(8,128)(2,1)}), bf16[8,16,32,256]{3,2,1,0:T(8,128)(2,1)S(1)}, u32[]{:S(2)}, u32[]{:S(2)}) %all-to-all-start.6) | async-done | bytes 2097184 | tf_op jit(solution)/shard_map/all_to_all | solution.py:468
  148.3 3.6 %all-to-all-start.7 = ((bf16[8,16,32,128]{3,2,1,0:T(8,128)(2,1)}), bf16[8,16,32,128]{3,2,1,0:T(8,128)(2,1)S(1)}, u32[]{:S(2)}, u32[]{:S(2)}) async-start(bf16[8,16,32,128]{3,2,1,0:T(8,128)(2,1)} %get-tuple-element.62), calls=%async_computation.7 | async-start | bytes 2097152 | tf_op jit(solution)/shard_map/all_to_all | solution.py:468
  151.9 0.0 copy-done.7
  151.9 2.4 %cycles.4 = (bf16[8,16,16,128]{3,2,1,0:T(8,128)(2,1)S(1)}, bf16[8,16,16,128]{3,2,1,0:T(8,128)(2,1)S(1)}) custom-call(s32[2]{0:T(128)S(1)} %pad_add_fusion.low_ref, bf16[16,128,256]{2,1,0:T(8,128)(2,1)} %get-tuple-element.57.turned_ref, bf16[8,16,32,256]{3,2,1,0:T(8,128)(2,1)} %copy-done.7), custom_call_target="tpu_custom_call" | custom-call | flops 2000000000 | bytes 12000000 | tf_op jit(solution)/shard_map/cycles/pallas_call | solution.py:348
  154.3 0.0 copy-start.4
  154.3 0.1 collective-permute-start.5
  154.4 12.8 %all-to-all-done.7.filtered_ref = bf16[8,16,32,128]{3,2,1,0:T(8,128)(2,1)S(1)} async-done(((bf16[8,16,32,128]{3,2,1,0:T(8,128)(2,1)}), bf16[8,16,32,128]{3,2,1,0:T(8,128)(2,1)S(1)}, u32[]{:S(2)}, u32[]{:S(2)}) %all-to-all-start.7) | async-done | bytes 1048608 | tf_op jit(solution)/shard_map/all_to_all | solution.py:468
  167.2 1.0 copy-done.8
  168.2 4.4 %all-to-all-start.5 = ((bf16[8,16,32,128]{3,2,1,0:T(8,128)(2,1)}), bf16[8,16,32,128]{3,2,1,0:T(8,128)(2,1)}, u32[]{:S(2)}, u32[]{:S(2)}) async-start(bf16[8,16,32,128]{3,2,1,0:T(8,128)(2,1)} %get-tuple-element.58), calls=%async_computation.5 | async-start | bytes 2097152 | tf_op jit(solution)/shard_map/all_to_all | solution.py:468
  172.6 0.0 copy-done.4
  172.6 1.7 cycles.5
  174.4 0.1 collective-permute-start.7
  174.4 0.0 collective-permute-done.5
  174.5 1.2 add_convert_fusion.1
  175.6 2.8 %collective-permute-start.6 = (bf16[8,16,16,128]{3,2,1,0:T(8,128)(2,1)S(1)}, bf16[8,16,16,128]{3,2,1,0:T(8,128)(2,1)}, u32[]{:S(2)}, u32[]{:S(2)}) collective-permute-start(bf16[8,16,16,128]{3,2,1,0:T(8,128)(2,1)S(1)} %add_convert_fusion.1), channel_id=1, source_target_pairs={{0,16},{8,24},{16,0},{24,8},{1,17},{9,25},{17,1},{25,9},{2,18},{10... | collective-permute-start | bytes 1572872 | tf_op jit(solution)/shard_map/ppermute | solution.py:465
  178.5 9.4 %all-to-all-done.5.filtered_ref = bf16[8,16,32,128]{3,2,1,0:T(8,128)(2,1)} async-done(((bf16[8,16,32,128]{3,2,1,0:T(8,128)(2,1)}), bf16[8,16,32,128]{3,2,1,0:T(8,128)(2,1)}, u32[]{:S(2)}, u32[]{:S(2)}) %all-to-all-start.5) | async-done | bytes 1048608 | tf_op jit(solution)/shard_map/all_to_all | solution.py:468
  187.9 1.7 cycles.3
  189.6 8.5 %collective-permute-done.7 = bf16[8,16,16,128]{3,2,1,0:T(8,128)(2,1)S(1)} collective-permute-done((bf16[8,16,16,128]{3,2,1,0:T(8,128)(2,1)S(1)}, bf16[8,16,16,128]{3,2,1,0:T(8,128)(2,1)S(1)}, u32[]{:S(2)}, u32[]{:S(2)}) %collective-permute-start.7) | collective-permute-done | bytes 524320 | tf_op jit(solution)/shard_map/ppermute | solution.py:465
  198.1 3.9 %collective-permute-done.6 = bf16[8,16,16,128]{3,2,1,0:T(8,128)(2,1)} collective-permute-done((bf16[8,16,16,128]{3,2,1,0:T(8,128)(2,1)S(1)}, bf16[8,16,16,128]{3,2,1,0:T(8,128)(2,1)}, u32[]{:S(2)}, u32[]{:S(2)}) %collective-permute-start.6) | collective-permute-done | bytes 524320 | tf_op jit(solution)/shard_map/ppermute | solution.py:465
  202.0 2.0 add_convert_fusion
  204.0 3.9 %all-to-all-start.8 = ((bf16[8,16,16,128]{3,2,1,0:T(8,128)(2,1)}), bf16[8,16,16,128]{3,2,1,0:T(8,128)(2,1)S(1)}, u32[]{:S(2)}, u32[]{:S(2)}) async-start(bf16[8,16,16,128]{3,2,1,0:T(8,128)(2,1)} %add_convert_fusion), calls=%async_computation.8 | async-start | bytes 1048576 | tf_op jit(solution)/shard_map/all_to_all | solution.py:527
  207.9 0.1 copy.5.modes_ref
  208.0 1.1 phases.1.phase_ref
  209.2 8.5 %all-to-all-done.8 = bf16[8,16,16,128]{3,2,1,0:T(8,128)(2,1)S(1)} async-done(((bf16[8,16,16,128]{3,2,1,0:T(8,128)(2,1)}), bf16[8,16,16,128]{3,2,1,0:T(8,128)(2,1)S(1)}, u32[]{:S(2)}, u32[]{:S(2)}) %all-to-all-start.8) | async-done | bytes 524320 | tf_op jit(solution)/shard_map/all_to_all | solution.py:527
  217.7 3.4 %synthesis.1 = bf16[64,16,2048]{2,1,0:T(8,128)(2,1)} custom-call(bf16[256,2048]{1,0:T(8,128)(2,1)S(1)} %phases.1.phase_ref, bf16[128,16,128]{2,1,0:T(8,128)(2,1)S(1)} %bitcast.8), custom_call_target="tpu_custom_call" | custom-call | tf_op jit(solution)/shard_map/synthesis/pallas_call | solution.py:430
  (8 shorter events, 0.0 us)
Async XLA Ops:
  0.1 0.7 copy-start.1
  0.8 12.5 %copy-start.2 = (s32[128]{0:T(128)S(1)}, s32[128]{0:T(128)}, u32[]{:S(2)}) copy-start(s32[128]{0:T(128)} %band_ref.1) | copy-start | bytes 1540
  0.8 12.6 %copy-start.3 = (s32[1024]{0:T(1024)S(1)}, s32[1024]{0:T(1024)}, u32[]{:S(2)}) copy-start(s32[1024]{0:T(1024)} %degree_ref.1) | copy-start | bytes 12292
  6.4 17.3 %collective-permute-start = (bf16[8,16,16,128]{3,2,1,0:T(8,128)(2,1)}, bf16[8,16,16,128]{3,2,1,0:T(8,128)(2,1)}, u32[]{:S(2)}, u32[]{:S(2)}) collective-permute-start(bf16[8,16,16,128]{3,2,1,0:T(8,128)(2,1)} %bitcast.4), channel_id=1, source_target_pairs={{0,8},{8,0},{16,24},{24,16},{1,9},{9,1},{17,25},{25,17},{2,10},{10... | collective-permute-start | bytes 1572872 | tf_op jit(solution)/shard_map/ppermute | solution.py:465
  9.5 14.3 %all-to-all-start = ((bf16[8,16,16,128]{3,2,1,0:T(8,128)(2,1)}), bf16[8,16,16,128]{3,2,1,0:T(8,128)(2,1)S(1)}, u32[]{:S(2)}, u32[]{:S(2)}) async-start(bf16[8,16,16,128]{3,2,1,0:T(8,128)(2,1)} %bitcast.4), calls=%async_computation | async-start | bytes 1048576 | tf_op jit(solution)/shard_map/all_to_all | solution.py:468
  22.8 1.0 copy-start.5
  23.8 13.9 %all-to-all-start.1 = ((bf16[8,16,16,128]{3,2,1,0:T(8,128)(2,1)}), bf16[8,16,16,128]{3,2,1,0:T(8,128)(2,1)S(1)}, u32[]{:S(2)}, u32[]{:S(2)}) async-start(bf16[8,16,16,128]{3,2,1,0:T(8,128)(2,1)} %collective-permute-done), calls=%async_computation.1 | async-start | bytes 1048576 | tf_op jit(solution)/shard_map/all_to_all | solution.py:468
  28.0 15.2 %collective-permute-start.1 = (bf16[4,16,16,128]{3,2,1,0:T(8,128)(2,1)S(1)}, bf16[4,16,16,128]{3,2,1,0:T(8,128)(2,1)S(1)}, u32[]{:S(2)}, u32[]{:S(2)}) collective-permute-start(bf16[4,16,16,128]{3,2,1,0:T(8,128)(2,1)S(1)} %get-tuple-element.64), channel_id=1, source_target_pairs={{0,16},{8,24},{16,0},{24,8},{1,17},{9,25},{17,1},{25,9},{2,18},{10... | collective-permute-start | bytes 786440 | tf_op jit(solution)/shard_map/ppermute | solution.py:465
  43.2 19.3 %all-to-all-start.2 = ((bf16[8,32,16,128]{3,2,1,0:T(8,128)(2,1)}), bf16[8,32,16,128]{3,2,1,0:T(8,128)(2,1)S(1)}, u32[]{:S(2)}, u32[]{:S(2)}) async-start(bf16[8,32,16,128]{3,2,1,0:T(8,128)(2,1)} %harmonic.3), calls=%async_computation.2 | async-start | bytes 2097152 | tf_op jit(solution)/shard_map/all_to_all | solution.py:468
  47.0 15.4 %collective-permute-start.2 = (bf16[4,16,16,128]{3,2,1,0:T(8,128)(2,1)S(1)}, bf16[4,16,16,128]{3,2,1,0:T(8,128)(2,1)S(1)}, u32[]{:S(2)}, u32[]{:S(2)}) collective-permute-start(bf16[4,16,16,128]{3,2,1,0:T(8,128)(2,1)S(1)} %get-tuple-element.63), channel_id=1, source_target_pairs={{0,16},{8,24},{16,0},{24,8},{1,17},{9,25},{17,1},{25,9},{2,18},{10... | collective-permute-start | bytes 786440 | tf_op jit(solution)/shard_map/ppermute | solution.py:465
  47.0 15.4 %collective-permute-start.3 = (bf16[4,16,16,128]{3,2,1,0:T(8,128)(2,1)S(1)}, bf16[4,16,16,128]{3,2,1,0:T(8,128)(2,1)S(1)}, u32[]{:S(2)}, u32[]{:S(2)}) collective-permute-start(bf16[4,16,16,128]{3,2,1,0:T(8,128)(2,1)S(1)} %collective-permute-done.1.refs_0_), channel_id=1, source_target_pairs={{0,8},{8,0},{16,24},{24,16},{1,9},{9,1},{17,25},{25,17},{2,10},{10... | collective-permute-start | bytes 786440 | tf_op jit(solution)/shard_map/ppermute | solution.py:465
  62.4 50.2 %copy-start = (bf16[8,32,16,128]{3,2,1,0:T(8,128)(2,1)}, bf16[8,32,16,128]{3,2,1,0:T(8,128)(2,1)S(1)}, u32[]{:S(2)}) copy-start(bf16[8,32,16,128]{3,2,1,0:T(8,128)(2,1)S(1)} %all-to-all-done.2.refs_0_) | copy-start | bytes 3145732
  62.5 19.3 %all-to-all-start.3 = ((bf16[8,32,16,128]{3,2,1,0:T(8,128)(2,1)}), bf16[8,32,16,128]{3,2,1,0:T(8,128)(2,1)S(1)}, u32[]{:S(2)}, u32[]{:S(2)}) async-start(bf16[8,32,16,128]{3,2,1,0:T(8,128)(2,1)} %harmonic.4), calls=%async_computation.3 | async-start | bytes 2097152 | tf_op jit(solution)/shard_map/all_to_all | solution.py:468
  66.3 8.7 %collective-permute-start.4 = (bf16[4,16,16,128]{3,2,1,0:T(8,128)(2,1)S(1)}, bf16[4,16,16,128]{3,2,1,0:T(8,128)(2,1)S(1)}, u32[]{:S(2)}, u32[]{:S(2)}) collective-permute-start(bf16[4,16,16,128]{3,2,1,0:T(8,128)(2,1)S(1)} %collective-permute-done.2.refs_1_), channel_id=1, source_target_pairs={{0,8},{8,0},{16,24},{24,16},{1,9},{9,1},{17,25},{25,17},{2,10},{10... | collective-permute-start | bytes 786440 | tf_op jit(solution)/shard_map/ppermute | solution.py:465
  81.7 30.9 %copy-start.6 = (bf16[8,32,16,128]{3,2,1,0:T(8,128)(2,1)}, bf16[8,32,16,128]{3,2,1,0:T(8,128)(2,1)S(1)}, u32[]{:S(2)}) copy-start(bf16[8,32,16,128]{3,2,1,0:T(8,128)(2,1)S(1)} %all-to-all-done.3.refs_1_) | copy-start | bytes 3145732
  118.1 30.2 %all-to-all-start.6 = ((bf16[8,16,32,256]{3,2,1,0:T(8,128)(2,1)}), bf16[8,16,32,256]{3,2,1,0:T(8,128)(2,1)S(1)}, u32[]{:S(2)}, u32[]{:S(2)}) async-start(bf16[8,16,32,256]{3,2,1,0:T(8,128)(2,1)} %filters.2), calls=%async_computation.6 | async-start | bytes 4194304 | tf_op jit(solution)/shard_map/all_to_all | solution.py:468
  148.3 3.6 %copy-start.7 = (bf16[8,16,32,256]{3,2,1,0:T(8,128)(2,1)}, bf16[8,16,32,256]{3,2,1,0:T(8,128)(2,1)S(1)}, u32[]{:S(2)}) copy-start(bf16[8,16,32,256]{3,2,1,0:T(8,128)(2,1)S(1)} %all-to-all-done.6.filtered_ref) | copy-start | bytes 6291460
  148.3 18.9 %all-to-all-start.7 = ((bf16[8,16,32,128]{3,2,1,0:T(8,128)(2,1)}), bf16[8,16,32,128]{3,2,1,0:T(8,128)(2,1)S(1)}, u32[]{:S(2)}, u32[]{:S(2)}) async-start(bf16[8,16,32,128]{3,2,1,0:T(8,128)(2,1)} %get-tuple-element.62), calls=%async_computation.7 | async-start | bytes 2097152 | tf_op jit(solution)/shard_map/all_to_all | solution.py:468
  154.3 18.3 %copy-start.4 = (bf16[16,128,256]{2,1,0:T(8,128)(2,1)S(1)}, bf16[16,128,256]{2,1,0:T(8,128)(2,1)}, u32[]{:S(2)}) copy-start(bf16[16,128,256]{2,1,0:T(8,128)(2,1)} %get-tuple-element.57.turned_ref) | copy-start | bytes 3145732
  154.3 20.1 %collective-permute-start.5 = (bf16[8,16,16,128]{3,2,1,0:T(8,128)(2,1)S(1)}, bf16[8,16,16,128]{3,2,1,0:T(8,128)(2,1)}, u32[]{:S(2)}, u32[]{:S(2)}) collective-permute-start(bf16[8,16,16,128]{3,2,1,0:T(8,128)(2,1)S(1)} %get-tuple-element.61), channel_id=1, source_target_pairs={{0,8},{8,0},{16,24},{24,16},{1,9},{9,1},{17,25},{25,17},{2,10},{10... | collective-permute-start | bytes 1572872 | tf_op jit(solution)/shard_map/ppermute | solution.py:465
  167.2 1.0 copy-start.8
  168.2 19.7 %all-to-all-start.5 = ((bf16[8,16,32,128]{3,2,1,0:T(8,128)(2,1)}), bf16[8,16,32,128]{3,2,1,0:T(8,128)(2,1)}, u32[]{:S(2)}, u32[]{:S(2)}) async-start(bf16[8,16,32,128]{3,2,1,0:T(8,128)(2,1)} %get-tuple-element.58), calls=%async_computation.5 | async-start | bytes 2097152 | tf_op jit(solution)/shard_map/all_to_all | solution.py:468
  174.4 23.7 %collective-permute-start.7 = (bf16[8,16,16,128]{3,2,1,0:T(8,128)(2,1)S(1)}, bf16[8,16,16,128]{3,2,1,0:T(8,128)(2,1)S(1)}, u32[]{:S(2)}, u32[]{:S(2)}) collective-permute-start(bf16[8,16,16,128]{3,2,1,0:T(8,128)(2,1)S(1)} %cycles.5), channel_id=1, source_target_pairs={{0,8},{8,0},{16,24},{24,16},{1,9},{9,1},{17,25},{25,17},{2,10},{10... | collective-permute-start | bytes 1572872 | tf_op jit(solution)/shard_map/ppermute | solution.py:465
  175.6 26.4 %collective-permute-start.6 = (bf16[8,16,16,128]{3,2,1,0:T(8,128)(2,1)S(1)}, bf16[8,16,16,128]{3,2,1,0:T(8,128)(2,1)}, u32[]{:S(2)}, u32[]{:S(2)}) collective-permute-start(bf16[8,16,16,128]{3,2,1,0:T(8,128)(2,1)S(1)} %add_convert_fusion.1), channel_id=1, source_target_pairs={{0,16},{8,24},{16,0},{24,8},{1,17},{9,25},{17,1},{25,9},{2,18},{10... | collective-permute-start | bytes 1572872 | tf_op jit(solution)/shard_map/ppermute | solution.py:465
  204.0 13.6 %all-to-all-start.8 = ((bf16[8,16,16,128]{3,2,1,0:T(8,128)(2,1)}), bf16[8,16,16,128]{3,2,1,0:T(8,128)(2,1)S(1)}, u32[]{:S(2)}, u32[]{:S(2)}) async-start(bf16[8,16,16,128]{3,2,1,0:T(8,128)(2,1)} %add_convert_fusion), calls=%async_computation.8 | async-start | bytes 1048576 | tf_op jit(solution)/shard_map/all_to_all | solution.py:527
